TPU v7x, 32 devices: a whole 2x2x4 slice. The times are simulated.
32 devices in a mesh: chain: 2 (over y), px: 8 (over z, x), py: 2 (over core).
Axes of the slice: x: 2, y: 2, z: 4, core: 2. Of those that a mesh axis runs over, the one named last changes fastest.
Arguments:
- adjoint: float32 [512, 256, 256], P(('chain', 'px'), 'py'), parts along dimension 0, may hold values from -6 to 6
- saved: float32 [512, 256, 256], P(('chain', 'px'), 'py'), parts along dimension 0, may hold values from -6 to 6
- spectra: bfloat16 [2, 256, 256, 256], P(None, None, 'px'), may hold values from -6 to 6, as said below
- freq_index: int32 [8], replicated, may hold values from 1 to 8
- picked: int32 [2], replicated, may hold values from 0 to 7
Outputs:
- force: float32 [512, 256, 256], P(('chain', 'px'), 'py'), parts along dimension 0
There are 2 independent parts, one for each index of `chain`. A program takes and returns all parts, laid end to end along the dimension named above; an argument that names none is the same for every part. Nothing has to cross between parts.
Inputs may be any that keep to these rules, and one draw needn't show every extreme that they name: Each kernel is even in every momentum coordinate separately: spectra[j][k1, k2, k3] is unchanged when k1 is replaced by (256 - k1) mod 256, and likewise k2 with 256 and k3 with 256.
All inputs are finite; a program needn't handle non-finite values.
Results may differ from a plain program's by a relative error of at most 0.0003.
Values sent between devices are 32-bit elements; how exact they have to be, the bound alone decides.
No kernel may reach another device: no remote copies, remote signals or barrier semaphores. Data moves between devices by JAX's collectives and lax.ppermute only.
A program may use at most 128 MiB of HBM per device.

v0:
```python
import math

import jax
import jax.numpy as jnp
from jax import lax
from jax.sharding import PartitionSpec as P

L1 = 256
L2 = 256
L3 = 256


def tables(length):
    counter = jnp.arange(length, dtype=jnp.int32)
    product = counter[:, None] * counter[None, :] % length
    angle = product.astype(jnp.float32) * (2.0 * math.pi / length)
    return (jnp.cos(angle), jnp.sin(angle))


def half_tables(length):
    cosine, sine = tables(length)
    half_width = length // 2
    counter = jnp.arange(length, dtype=jnp.int32)
    parity = (1 - 2 * (counter % 2)).astype(jnp.float32)
    first_column = jnp.arange(half_width, dtype=jnp.int32) == 0
    forward_real = cosine[:, :half_width]
    forward_imag = jnp.where(first_column[None, :], parity[:, None], -sine[:, :half_width])
    inverse_real = jnp.where(first_column[:, None], 1.0, 2.0 * cosine[:half_width, :])
    inverse_imag = jnp.where(first_column[:, None], parity[None, :], -2.0 * sine[:half_width, :])
    return (forward_real, forward_imag, inverse_real, inverse_imag)


def reflect(field, axis):
    return jnp.roll(jnp.flip(field, axis), 1, axis)


def along(field, table, axis):
    letters = "abcdef"[: field.ndim]
    result = letters[:axis] + "z" + letters[axis + 1 :]
    return jnp.einsum(
        letters + "," + letters[axis] + "z->" + result,
        field,
        table,
        precision=lax.Precision.HIGHEST,
    )


def rotate(pair, axis, cosine, sine, forward):
    with_cos = along(pair, cosine, axis)
    with_sin = along(pair, sine, axis)
    if forward:
        return jnp.stack([with_cos[0] + with_sin[1], with_cos[1] - with_sin[0]])
    return jnp.stack([with_cos[0] - with_sin[1], with_cos[1] + with_sin[0]])


def on_device(adjoint, saved, spectra, freq_index, picked):
    width_py = lax.axis_size("py")
    py_index = lax.axis_index("py")
    px_index = lax.axis_index("px")
    cos_one, sin_one = tables(L1)
    cos_two, sin_two = tables(L2)
    half_width = L3 // 2
    forward_real, forward_imag, inverse_real, inverse_imag = half_tables(L3)
    real_part = along(adjoint, forward_real, 2)
    imag_part = along(adjoint, forward_imag, 2)
    column_count = half_width // width_py
    columns = lax.all_to_all(
        jnp.stack([real_part, imag_part]), "py", split_axis=3, concat_axis=2, tiled=True
    )
    columns = rotate(columns, 2, cos_two, sin_two, True)
    leading_column = jnp.arange(column_count, dtype=jnp.int32) == 0
    first_slot = leading_column & (py_index == 0)
    slot_ids = jnp.arange(L2, dtype=jnp.int32)
    lower_half = (slot_ids > 0) & (slot_ids < L2 // 2)
    upper_half = slot_ids > L2 // 2
    special = columns[:, :, :, 0]
    mirror = reflect(special, 2)
    packed_real = jnp.where(
        lower_half,
        (special[0] + mirror[0]) * 0.5,
        jnp.where(upper_half, (special[1] + mirror[1]) * 0.5, special[0]),
    )
    packed_imag = jnp.where(
        lower_half,
        (special[1] - mirror[1]) * 0.5,
        jnp.where(upper_half, (mirror[0] - special[0]) * 0.5, special[1]),
    )
    columns = jnp.where(first_slot, jnp.stack([packed_real, packed_imag])[..., None], columns)
    spectral = rotate(
        lax.all_to_all(columns, "px", split_axis=2, concat_axis=1, tiled=True),
        1,
        cos_one,
        sin_one,
        True,
    )
    kernels_all = spectra.astype(jnp.float32)
    local_width = spectra.shape[2]
    global_slots = px_index * local_width + jnp.arange(local_width, dtype=jnp.int32)
    lower_local = (global_slots > 0) & (global_slots < L2 // 2)
    upper_local = global_slots > L2 // 2
    kernel = lax.dynamic_slice_in_dim(kernels_all, py_index * column_count, column_count, 3)
    nyquist = kernels_all[:, :, :, half_width]
    lowest = kernel[..., 0]
    alpha_column = jnp.where(
        lower_local, lowest, jnp.where(upper_local, nyquist, (lowest + nyquist) * 0.5)
    )
    beta_column = jnp.where(lower_local | upper_local, 0.0, (lowest - nyquist) * 0.5) * jnp.where(
        py_index == 0, 1.0, 0.0
    )
    kernel = jnp.where(first_slot, alpha_column[..., None], kernel)
    spectral_mirror = reflect(spectral[..., 0], 1)
    feature_ids = jnp.arange(freq_index.shape[0], dtype=jnp.int32)
    chosen = jnp.sum(
        jnp.where(feature_ids[None, :] == picked[:, None], freq_index[None, :], 0), axis=1
    )
    omegas = chosen.astype(jnp.float32) * (math.pi / 8.0)
    scale = 1.0 / (L1 * L2 * L3)
    slot_count = picked.shape[0]
    groups = [(index, index + 1) for index in range(slot_count)]
    total = jnp.zeros(saved.shape, jnp.float32)
    for start, stop in groups:
        product = spectral[:, None] * kernel[None, start:stop]
        correction = (
            beta_column[start:stop][None]
            * jnp.stack([spectral_mirror[0], -spectral_mirror[1]])[:, None]
        )
        product = product + jnp.where(leading_column, correction[..., None], 0.0)
        product = rotate(product, 2, cos_one, sin_one, False)
        back = lax.all_to_all(product, "px", split_axis=2, concat_axis=3, tiled=True)
        special = back[..., 0]
        mirror = reflect(special, 3)
        untangled_real = jnp.where(
            lower_half,
            special[0] + mirror[1],
            jnp.where(upper_half, mirror[0] - special[1], special[0]),
        )
        untangled_imag = jnp.where(
            lower_half,
            special[1] + mirror[0],
            jnp.where(upper_half, special[0] - mirror[1], special[1]),
        )
        back = jnp.where(first_slot, jnp.stack([untangled_real, untangled_imag])[..., None], back)
        back = rotate(back, 3, cos_two, sin_two, False)
        back = lax.all_to_all(back, "py", split_axis=3, concat_axis=4, tiled=True)
        fields = (along(back[0], inverse_real, 3) + along(back[1], inverse_imag, 3)) * scale
        omega_grid = omegas[start:stop][:, None, None, None]
        total = total + jnp.sum(omega_grid * jnp.cos(omega_grid * saved[None]) * fields, axis=0)
    return total


def solution(mesh):
    placed = (
        P(("chain", "px"), "py", None),
        P(("chain", "px"), "py", None),
        P(None, None, "px", None),
        P(),
        P(),
    )
    return jax.shard_map(
        on_device,
        mesh=mesh,
        in_specs=placed,
        out_specs=P(("chain", "px"), "py", None),
        check_vma=False,
    )
```

profile of v0, /device:TPU:21, one launch (start us, length us, event | category | flops | bytes accessed | tf_op | source)
XLA Modules:
  0.0 783.6 jit_solution(17898030757995129049)
XLA Ops:
  2.0 6.2 convolution_bitcast_fusion.2
  8.3 4.4 convolution_bitcast_fusion.1
  15.6 7.9 %all_to_all.108 = f32[2,32,128,128]{2,1,0,3:T(8,128)S(1)} all-to-all(f32[2,32,128,128]{2,1,0,3:T(8,128)S(1)} %copy.440), channel_id=1, replica_groups=mesh['chain'=2,'px'=8,'py'=2] {'py'}, dimensions={3} | all-to-all | bytes 8388608 | tf_op jit(solution)/shard_map/all_to_all | solution.py:67
  23.5 5.2 copy.561
  28.7 6.4 all_to_all.81
  35.1 8.5 %convolution_bitcast_fusion = f32[2,32,256,64]{2,3,1,0:T(8,128)S(1)} fusion(f32[2,32,256,64]{2,3,1,0:T(8,128)} %all_to_all.81), kind=kOutput, calls=%fused_computation.35 | convolution fusion | flops 3222142976 | bytes 8388608 | tf_op jit(solution)/shard_map/abcd,cz->abzd/dot_general | solution.py:40
  43.7 4.9 fusion.26
  52.0 4.4 slice_add_fusion.5
  63.2 6.6 fusion
  69.8 9.2 %copy.448 = f32[2,32,256,64]{3,1,0,2:T(8,128)} copy(f32[2,32,256,64]{2,0,1,3:T(2,128)} %fusion) | data formatting | bytes 8388608 | tf_op jit(solution)/shard_map/jit(_where)/select_n | solution.py:88
  79.0 9.8 %reshape.449 = f32[8,1,131072]{2,1,0:T(1,128)} reshape(f32[256,2,32,64]{3,2,1,0:T(8,128)} %bitcast.257) | data formatting | bytes 8388608
  88.8 5.9 all-to-all-start.1
  94.7 15.9 %copy.455 = bf16[2,256,32,256]{1,2,3,0:T(8,128)(2,1)} copy(bf16[2,256,32,256]{3,2,1,0:T(8,128)(2,1)} %param.7) | data formatting | bytes 16777216 | tf_op args[2]
  110.6 11.3 %convert_element_type.63 = f32[2,256,32,256]{1,2,3,0:T(8,128)} convert(bf16[2,256,32,256]{1,2,3,0:T(8,128)(2,1)} %copy.455) | non-fusion elementwise | flops 4194304 | bytes 25165824 | tf_op jit(solution)/shard_map/convert_element_type | solution.py:96
  132.1 52.2 %all-to-all-done.1 = f32[8,1,131072]{2,1,0:T(1,128)} async-done(((f32[8,1,131072]{2,1,0:T(1,128)}), f32[8,1,131072]{2,1,0:T(1,128)}, u32[]{:S(2)}, u32[]{:S(2)}) %all-to-all-start.1) | async-done | bytes 4194336 | tf_op jit(solution)/shard_map/all_to_all | solution.py:90
  184.7 14.1 %reduce.6 = f32[8,131072]{1,0:T(8,128)} reduce(f32[8,1,131072]{2,1,0:T(1,128)} %all-to-all-done.1, f32[]{:T(128)} %broadcast.356), dimensions={1}, to_apply=%all_to_all.82.reduce_sub_computation | reduce | bytes 8388612 | tf_op jit(solution)/shard_map/all_to_all | solution.py:90
  198.9 8.7 %reshape.450 = f32[256,2,32,64]{3,2,1,0:T(8,128)} reshape(f32[8,131072]{1,0:T(8,128)} %reduce.6) | data formatting | bytes 8388608
  207.6 13.1 %copy.450 = f32[2,8,32,32,64]{4,3,2,1,0:T(8,128)} copy(f32[2,8,32,32,64]{4,2,0,3,1:T(8,128)} %bitcast.264) | data formatting | bytes 8388608 | tf_op jit(solution)/shard_map/all_to_all | solution.py:90
  220.7 7.8 copy.452
  228.5 7.8 fusion.58
  236.3 4.6 fusion.48
  243.8 5.0 select_add_fusion.1
  248.8 4.7 fusion.56
  253.5 4.6 fusion.46
  261.7 9.2 %copy.459 = f32[2,1,256,32,64]{4,3,0,1,2:T(8,128)} copy(f32[2,1,256,32,64]{2,4,3,0,1:T(8,128)} %pad_maximum_fusion.3) | data formatting | bytes 8388608 | tf_op jit(solution)/shard_map/stack | solution.py:53
  270.9 10.2 %reshape.455 = f32[8,1,131072]{2,1,0:T(1,128)} reshape(f32[256,1,2,32,64]{4,3,2,1,0:T(8,128)} %bitcast.258) | data formatting | bytes 8388608
  281.1 7.6 all-to-all-start.2
  288.7 7.6 fusion.54
  296.3 4.6 fusion.50
  304.6 9.2 %copy.482 = f32[2,1,256,32,64]{4,3,0,1,2:T(8,128)} copy(f32[2,1,256,32,64]{2,4,3,0,1:T(8,128)} %pad_maximum_fusion.5) | data formatting | bytes 8388608 | tf_op jit(solution)/shard_map/stack | solution.py:53
  313.8 9.8 %reshape.451 = f32[8,1,131072]{2,1,0:T(1,128)} reshape(f32[256,1,2,32,64]{4,3,2,1,0:T(8,128)} %bitcast.259) | data formatting | bytes 8388608
  323.6 53.9 %all-to-all-done.2 = f32[8,1,131072]{2,1,0:T(1,128)} async-done(((f32[8,1,131072]{2,1,0:T(1,128)}), f32[8,1,131072]{2,1,0:T(1,128)}, u32[]{:S(2)}, u32[]{:S(2)}) %all-to-all-start.2) | async-done | bytes 4194336 | tf_op jit(solution)/shard_map/all_to_all | solution.py:129
  377.5 8.5 %all-to-all-start.4 = ((f32[8,1,131072]{2,1,0:T(1,128)}), f32[8,1,131072]{2,1,0:T(1,128)}, u32[]{:S(2)}, u32[]{:S(2)}) async-start(f32[8,1,131072]{2,1,0:T(1,128)} %reshape.451), calls=%async_computation.4 | async-start | bytes 8388608 | tf_op jit(solution)/shard_map/all_to_all | solution.py:129
  386.8 13.7 %reduce.7 = f32[8,131072]{1,0:T(8,128)} reduce(f32[8,1,131072]{2,1,0:T(1,128)} %all-to-all-done.2, f32[]{:T(128)} %broadcast.356), dimensions={1}, to_apply=%all_to_all.86.reduce_sub_computation | reduce | bytes 8388612 | tf_op jit(solution)/shard_map/all_to_all | solution.py:129
  400.5 8.7 %reshape.456 = f32[256,1,2,32,64]{4,3,2,1,0:T(8,128)} reshape(f32[8,131072]{1,0:T(8,128)} %reduce.7) | data formatting | bytes 8388608
  409.2 4.4 copy.460
  420.6 54.0 %all-to-all-done.4 = f32[8,1,131072]{2,1,0:T(1,128)} async-done(((f32[8,1,131072]{2,1,0:T(1,128)}), f32[8,1,131072]{2,1,0:T(1,128)}, u32[]{:S(2)}, u32[]{:S(2)}) %all-to-all-start.4) | async-done | bytes 4194336 | tf_op jit(solution)/shard_map/all_to_all | solution.py:129
  474.6 13.9 %reduce.8 = f32[8,131072]{1,0:T(8,128)} reduce(f32[8,1,131072]{2,1,0:T(1,128)} %all-to-all-done.4, f32[]{:T(128)} %broadcast.356), dimensions={1}, to_apply=%all_to_all.94.reduce_sub_computation | reduce | bytes 8388612 | tf_op jit(solution)/shard_map/all_to_all | solution.py:129
  488.5 8.7 %reshape.452 = f32[256,1,2,32,64]{4,3,2,1,0:T(8,128)} reshape(f32[8,131072]{1,0:T(8,128)} %reduce.8) | data formatting | bytes 8388608
  497.2 4.4 copy.483
  503.0 4.1 fusion.159
  508.7 5.2 copy.537
  514.0 8.6 %copy.466 = f32[2,32,256,64]{2,0,1,3:T(2,128)} copy(f32[2,32,256,64]{3,2,1,0:T(8,128)} %bitcast.247) | data formatting | bytes 8388608 | tf_op jit(solution)/shard_map/all_to_all | solution.py:129
  523.1 8.7 %copy.490 = f32[2,32,256,64]{2,0,1,3:T(2,128)} copy(f32[2,32,256,64]{3,2,1,0:T(8,128)} %bitcast.250) | data formatting | bytes 8388608 | tf_op jit(solution)/shard_map/all_to_all | solution.py:129
  538.3 11.5 %broadcast_select_fusion.1 = (f32[2,32,256,64]{2,0,1,3:T(2,128)S(1)}, f32[2,32,256,64]{2,0,1,3:T(2,128)}) fusion(f32[2,32,256,64]{2,0,1,3:T(2,128)} %copy.466, pred[64]{0:T(512)(128)(4,1)S(1)} %get-tuple-element.47, f32[2,32,256]{2,0,1:T(2,128)S(1)} %copy.464, f32[2,32,256,64]{2,0,1,3:T(2,128)} %copy.490, f32[2,32,256]{2,0,1:T(2,128)S(1)} %copy.488), kind=kLoop, calls=%fused_computation.22 | loop fusion | flops 2097152 | bytes 16908352 | tf_op jit(solution)/shard_map/jit(_where)/select_n | solution.py:142
  549.8 10.6 %fusion.18 = f32[2,1,32,256,64]{3,4,2,0,1:T(8,128)S(1)} fusion(f32[2,32,256,64]{2,0,1,3:T(2,128)} %get-tuple-element.44), kind=kOutput, calls=%fused_computation.34 | convolution fusion | flops 3222142976 | bytes 8388608 | tf_op jit(solution)/shard_map/abcde,dz->abcze/dot_general | solution.py:40
  560.4 6.4 fusion.15
  566.8 8.2 %fusion.12 = f32[2,1,32,256,64]{3,4,2,0,1:T(8,128)} fusion(f32[2,32,256,64]{2,0,1,3:T(2,128)S(1)} %get-tuple-element.43), kind=kOutput, calls=%fused_computation.32 | convolution fusion | flops 3222142976 | bytes 8388608 | tf_op jit(solution)/shard_map/abcde,dz->abcze/dot_general | solution.py:40
  575.0 8.4 %fusion.9 = f32[2,1,32,256,64]{3,4,2,0,1:T(8,128)} fusion(f32[2,32,256,64]{2,0,1,3:T(2,128)S(1)} %get-tuple-element.43), kind=kOutput, calls=%fused_computation.31 | convolution fusion | flops 3222142976 | bytes 8388608 | tf_op jit(solution)/shard_map/abcde,dz->abcze/dot_general | solution.py:40
  587.1 9.2 %copy.495 = f32[2,1,32,256,64]{4,2,0,1,3:T(8,128)} copy(f32[2,1,32,256,64]{3,4,2,0,1:T(8,128)} %pad_maximum_fusion.6) | data formatting | bytes 8388608 | tf_op jit(solution)/shard_map/stack | solution.py:53
  596.3 8.7 %reshape.453 = f32[2,1,524288]{2,1,0:T(1,128)} reshape(f32[256,1,2,32,64]{4,3,2,1,0:T(8,128)} %bitcast.260) | data formatting | bytes 8388608
  605.0 14.3 %all_to_all.109 = f32[2,1,524288]{2,1,0:T(1,128)} all-to-all(f32[2,1,524288]{2,1,0:T(1,128)} %reshape.453), channel_id=1, replica_groups=mesh['chain'=2,'px'=8,'py'=2] {'py'}, dimensions={0} | all-to-all | bytes 8388608 | tf_op jit(solution)/shard_map/all_to_all | solution.py:144
  619.3 16.5 %reduce.9 = f32[2,524288]{1,0:T(2,128)} reduce(f32[2,1,524288]{2,1,0:T(1,128)} %all_to_all.109, f32[]{:T(128)} %broadcast.356), dimensions={1}, to_apply=%all_to_all.99.reduce_sub_computation | reduce | bytes 8388612 | tf_op jit(solution)/shard_map/all_to_all | solution.py:144
  635.8 10.0 %reshape.454 = f32[256,1,2,32,64]{4,3,2,1,0:T(8,128)} reshape(f32[2,524288]{1,0:T(2,128)} %reduce.9) | data formatting | bytes 8388608
  645.8 12.2 %copy.496 = f32[2,1,32,256,64]{3,1,4,2,0:T(1,128)} copy(f32[2,1,32,256,64]{4,2,0,1,3:T(8,128)} %bitcast.261) | data formatting | bytes 8388608 | tf_op jit(solution)/shard_map/all_to_all | solution.py:144
  661.4 5.2 fusion.61
  670.2 9.2 %copy.471 = f32[2,1,32,256,64]{4,2,0,1,3:T(8,128)} copy(f32[2,1,32,256,64]{3,4,2,0,1:T(8,128)} %pad_maximum_fusion.4) | data formatting | bytes 8388608 | tf_op jit(solution)/shard_map/stack | solution.py:53
  679.4 8.7 %reshape.457 = f32[2,1,524288]{2,1,0:T(1,128)} reshape(f32[256,1,2,32,64]{4,3,2,1,0:T(8,128)} %bitcast.262) | data formatting | bytes 8388608
  688.1 11.8 %all_to_all.110 = f32[2,1,524288]{2,1,0:T(1,128)} all-to-all(f32[2,1,524288]{2,1,0:T(1,128)} %reshape.457), channel_id=1, replica_groups=mesh['chain'=2,'px'=8,'py'=2] {'py'}, dimensions={0} | all-to-all | bytes 8388608 | tf_op jit(solution)/shard_map/all_to_all | solution.py:144
  699.9 16.4 %reduce.10 = f32[2,524288]{1,0:T(2,128)} reduce(f32[2,1,524288]{2,1,0:T(1,128)} %all_to_all.110, f32[]{:T(128)} %broadcast.356), dimensions={1}, to_apply=%all_to_all.91.reduce_sub_computation | reduce | bytes 8388612 | tf_op jit(solution)/shard_map/all_to_all | solution.py:144
  716.4 10.0 %reshape.458 = f32[256,1,2,32,64]{4,3,2,1,0:T(8,128)} reshape(f32[2,524288]{1,0:T(2,128)} %reduce.10) | data formatting | bytes 8388608
  726.4 12.6 %copy.472 = f32[2,1,32,256,64]{3,1,4,2,0:T(1,128)} copy(f32[2,1,32,256,64]{4,2,0,1,3:T(8,128)} %bitcast.263) | data formatting | bytes 8388608 | tf_op jit(solution)/shard_map/all_to_all | solution.py:144
  741.8 3.6 fusion.63
  749.7 33.7 %multiply_add_fusion = f32[32,128,256]{2,1,0:T(8,128)} fusion(f32[32,128,256]{2,1,0:T(8,128)S(1)} %copy-done.11, f32[32,128,256]{2,1,0:T(8,128)S(1)} %copy-done.13, f32[32,128,256]{2,1,0:T(8,128)S(1)} %fusion.63, f32[32,128,256]{2,1,0:T(8,128)S(1)} %fusion.66, f32[32,128,128]{1,2,0:T(8,128)S(1)} %bitcast.284, f32[]{:T(128)} %bitcast.71, f32[]{:T(128)} %bitcast, ...), kind=kOutput, calls=%fused_computation.17 | convolution fusion | flops 1622212608 | bytes 23201288 | tf_op jit(solution)/shard_map/abcd,dz->abcz/dot_general | solution.py:40
  (124 shorter events, 70.8 us)
Async XLA Ops:
  0.0 8.3 %copy-start.8 = (f32[32,128,256]{2,1,0:T(8,128)S(1)}, f32[32,128,256]{2,1,0:T(8,128)}, u32[]{:S(2)}) copy-start(f32[32,128,256]{2,1,0:T(8,128)} %param.5) | copy-start | bytes 12582916
  1.0 7.3 copy-start.14
  1.0 7.2 copy-start.20
  1.0 7.2 copy-start.18
  2.0 6.3 copy-start.16
  35.1 8.5 %copy-start.2 = (f32[2,32,256,64]{2,3,1,0:T(8,128)S(1)}, f32[2,32,256,64]{2,3,1,0:T(8,128)}, u32[]{:S(2)}) copy-start(f32[2,32,256,64]{2,3,1,0:T(8,128)} %all_to_all.81) | copy-start | bytes 12582916
  57.6 3.6 copy-start.12
  59.8 1.3 copy-start.7
  88.8 95.5 %all-to-all-start.1 = ((f32[8,1,131072]{2,1,0:T(1,128)}), f32[8,1,131072]{2,1,0:T(1,128)}, u32[]{:S(2)}, u32[]{:S(2)}) async-start(f32[8,1,131072]{2,1,0:T(1,128)} %reshape.449), calls=%async_computation.1 | async-start | bytes 8388608 | tf_op jit(solution)/shard_map/all_to_all | solution.py:90
  228.5 7.8 copy-start.5
  241.9 1.3 copy-start.6
  281.1 96.4 %all-to-all-start.2 = ((f32[8,1,131072]{2,1,0:T(1,128)}), f32[8,1,131072]{2,1,0:T(1,128)}, u32[]{:S(2)}, u32[]{:S(2)}) async-start(f32[8,1,131072]{2,1,0:T(1,128)} %reshape.455), calls=%async_computation.2 | async-start | bytes 8388608 | tf_op jit(solution)/shard_map/all_to_all | solution.py:129
  288.7 7.6 copy-start.4
  323.6 62.4 %copy-start.22 = (s32[8]{0:T(128)S(1)}, s32[8]{0:T(128)}, u32[]{:S(2)}) copy-start(s32[8]{0:T(128)} %param.8) | copy-start | bytes 100
  323.6 62.4 %copy-start.23 = (s32[2]{0:T(128)S(1)}, s32[2]{0:T(128)}, u32[]{:S(2)}) copy-start(s32[2]{0:T(128)} %param.9) | copy-start | bytes 28
  377.5 97.2 %all-to-all-start.4 = ((f32[8,1,131072]{2,1,0:T(1,128)}), f32[8,1,131072]{2,1,0:T(1,128)}, u32[]{:S(2)}, u32[]{:S(2)}) async-start(f32[8,1,131072]{2,1,0:T(1,128)} %reshape.451), calls=%async_computation.4 | async-start | bytes 8388608 | tf_op jit(solution)/shard_map/all_to_all | solution.py:129
  415.1 3.3 copy-start
  503.0 5.7 copy-start.1
  549.7 10.6 %copy-start.3 = (f32[2,32,256,64]{2,0,1,3:T(2,128)S(1)}, f32[2,32,256,64]{2,0,1,3:T(2,128)}, u32[]{:S(2)}) copy-start(f32[2,32,256,64]{2,0,1,3:T(2,128)} %get-tuple-element.44) | copy-start | bytes 12582916
  660.4 1.0 copy-start.17
  660.5 0.9 copy-start.19
  660.5 6.1 copy-start.10
  660.8 5.9 copy-start.9
  741.8 4.0 copy-start.15
  741.8 4.0 copy-start.21
  745.8 3.9 copy-start.11
  745.8 3.9 copy-start.13
where the time goes:
time: 799 us; the launch traced here: 784 us
  local copies, waits for them, and re-layouts  290 us (36%)
  waiting for transfers between devices  160 us (20%)
  other arithmetic  139 us (17%)
  matrix products  138 us (17%)
  blocking collectives  34 us (4%)
  starting transfers between devices  22 us (3%)
    unnamed x71, local copies, waits for them, and re-layouts  128 us
    all_to_all x2, waiting for transfers between devices, on_device(): lax.all_to_all(product, 'px', split_axis=2, concat_axis=3, tiled=True)  108 us
    dot_general x12, matrix products, along(): jnp.einsum(letters + ',' + letters[axis] + 'z->' + result, field, table,...  104 us
    all_to_all x1, waiting for transfers between devices, on_device(): lax.all_to_all(columns, 'px', split_axis=2, concat_axis=1, tiled=True)  52.2 us
    another operation x4, local copies, waits for them, and re-layouts, rotate(): return jnp.stack([with_cos[0] - with_sin[1], with_cos[1] + with_sin[0]])  36.8 us
    unnamed x6, matrix products  34 us
    all_to_all x2, other arithmetic, on_device(): back = lax.all_to_all(back, 'py', split_axis=3, concat_axis=4, tiled=True)  32.9 us
    all_to_all x6, local copies, waits for them, and re-layouts, on_device(): lax.all_to_all(product, 'px', split_axis=2, concat_axis=3, tiled=True)  28.9 us
  transfers between devices with their start and end apart: 3, of which 3 were waited for; matrix products, arithmetic and copies ran while one was open for 14% of the time, Pallas kernels for 0%

commit v1 on v0

v1 whole, which is shorter than its diff:
```python
import math

import jax
import jax.numpy as jnp
import numpy as np
from jax import lax
from jax.experimental import pallas as pl
from jax.experimental.pallas import tpu as pltpu
from jax.sharding import PartitionSpec as P

VMEM_BYTES = 56 * 1024 * 1024
CHUNKS = 2


def hartley(length):
    counter = np.arange(length)
    angle = 2.0 * np.pi * ((counter[:, None] * counter[None, :]) % length) / length
    return np.cos(angle) + np.sin(angle)


def split_table(table):
    high = table.astype(np.float32).astype(jnp.bfloat16)
    low = (table - high.astype(np.float64)).astype(np.float32).astype(jnp.bfloat16)
    return high, low


def left_table(table):
    high, low = split_table(table)
    return np.concatenate([high, high, low], axis=1)


def right_table(table):
    high, low = split_table(table)
    return np.concatenate([high, high, low], axis=0)


def folded_order(length, base):
    half = length // 2
    first = (base + np.arange(half)) % length
    second = (base - np.arange(half)) % length
    second[0] = (base + half) % length
    return np.concatenate([first, second])


def paired_order(length):
    half = length // 2
    order = [0, half]
    for index in range(1, half):
        order += [index, length - index]
    return np.array(order)


def split_value(value):
    high = value.astype(jnp.bfloat16)
    low = (value - high.astype(jnp.float32)).astype(jnp.bfloat16)
    return high, low


def left_dot(table, value):
    high, low = split_value(value)
    stacked = jnp.concatenate([high, low, high], axis=0)
    return jnp.dot(table, stacked, preferred_element_type=jnp.float32)


def right_dot(value, table):
    high, low = split_value(value)
    stacked = jnp.concatenate([high, low, high], axis=1)
    return jnp.dot(stacked, table, preferred_element_type=jnp.float32)


def params():
    return pltpu.CompilerParams(vmem_limit_bytes=VMEM_BYTES)


def forward_last(adjoint, table):
    rows_one, rows_two, length = adjoint.shape
    count = table.shape[0]
    block = min(8, rows_one)

    def body(adjoint_ref, table_ref, out_ref):
        flat = out_ref.reshape(count * block, rows_two)
        for start in range(0, block, 2):
            value = adjoint_ref[start : start + 2].reshape(2 * rows_two, length)
            high, low = split_value(value)
            stacked = jnp.concatenate([high, low, high], axis=1)
            result = lax.dot_general(
                table_ref[...],
                stacked,
                (((1,), (1,)), ((), ())),
                preferred_element_type=jnp.float32,
            )
            for inner in range(2):
                flat[pl.ds(start + inner, count, stride=block), :] = result[
                    :, inner * rows_two : (inner + 1) * rows_two
                ]

    return pl.pallas_call(
        body,
        grid=(rows_one // block,),
        in_specs=[
            pl.BlockSpec((block, rows_two, length), lambda i: (i, 0, 0)),
            pl.BlockSpec(table.shape, lambda i: (0, 0)),
        ],
        out_specs=pl.BlockSpec((count, block, rows_two), lambda i: (0, i, 0)),
        out_shape=jax.ShapeDtypeStruct((count, rows_one, rows_two), jnp.float32),
        compiler_params=params(),
        cost_estimate=pl.CostEstimate(
            flops=6 * count * rows_one * rows_two * length,
            bytes_accessed=4 * rows_one * rows_two * (length + count),
            transcendentals=0,
        ),
        name="forward_last",
    )(adjoint, table)


def filter_planes(planes, kernels, tables):
    width_px, width_py, planes_count, rows_one, rows_two = planes.shape
    slots = kernels.shape[0]
    length_one = width_px * rows_one
    length_two = width_py * rows_two

    def body(planes_ref, kernels_ref, one_f, two_f, one_b, two_b, out_ref):
        value = jnp.concatenate(
            [
                planes_ref[:, part, 0].reshape(length_one, rows_two)
                for part in range(width_py)
            ],
            axis=1,
        )
        value = right_dot(value, two_f[...])
        value = left_dot(one_f[...], value)
        for slot in range(slots):
            product = value * kernels_ref[slot, 0]
            back = left_dot(one_b[...], product)
            back = right_dot(back, two_b[...])
            for part in range(width_py):
                out_ref[:, part, slot, 0] = back[
                    :, part * rows_two : (part + 1) * rows_two
                ].reshape(width_px, rows_one, rows_two)

    plane_size = length_one * length_two
    return pl.pallas_call(
        body,
        grid=(planes_count,),
        in_specs=[
            pl.BlockSpec(
                (width_px, width_py, 1, rows_one, rows_two), lambda i: (0, 0, i, 0, 0)
            ),
            pl.BlockSpec((slots, 1, length_one, length_two), lambda i: (0, i, 0, 0)),
        ]
        + [pl.BlockSpec(table.shape, lambda i: (0, 0)) for table in tables],
        out_specs=pl.BlockSpec(
            (width_px, width_py, slots, 1, rows_one, rows_two),
            lambda i: (0, 0, 0, i, 0, 0),
        ),
        out_shape=jax.ShapeDtypeStruct(
            (width_px, width_py, slots, planes_count, rows_one, rows_two), jnp.float32
        ),
        compiler_params=params(),
        cost_estimate=pl.CostEstimate(
            flops=6 * planes_count * plane_size * (1 + slots) * (length_one + length_two),
            bytes_accessed=planes_count * plane_size * (4 + 6 * slots),
            transcendentals=0,
        ),
        name="filter_planes",
    )(planes, kernels, *tables)


def backward_last(parts, factors, table, total):
    sources, slots, depth, rows_one, rows_two = parts.shape
    length = table.shape[1]
    block = min(8, rows_one)

    def body(*refs):
        if total is None:
            parts_ref, factors_ref, table_ref, out_ref = refs
        else:
            parts_ref, factors_ref, table_ref, total_ref, out_ref = refs
        flat = parts_ref.reshape(sources * slots * depth * block, rows_two)
        for start in range(0, block, 2):
            result = None
            for slot in range(slots):
                values = []
                for inner in range(2):
                    columns = jnp.concatenate(
                        [
                            flat[
                                pl.ds(
                                    (source * slots + slot) * depth * block
                                    + start
                                    + inner,
                                    depth,
                                    stride=block,
                                ),
                                :,
                            ]
                            for source in range(sources)
                        ],
                        axis=0,
                    )
                    values.append(columns.T)
                field = right_dot(jnp.concatenate(values, axis=0), table_ref[...])
                field = field.reshape(2, rows_two, length)
                term = field * factors_ref[slot, start : start + 2]
                result = term if result is None else result + term
            if total is not None:
                result = result + total_ref[start : start + 2]
            out_ref[start : start + 2] = result

    space = pl.BlockSpec((block, rows_two, length), lambda i: (i, 0, 0))
    operands = [parts, factors, table]
    in_specs = [
        pl.BlockSpec(
            (sources, slots, depth, block, rows_two), lambda i: (0, 0, 0, i, 0)
        ),
        pl.BlockSpec((slots, block, rows_two, length), lambda i: (0, i, 0, 0)),
        pl.BlockSpec(table.shape, lambda i: (0, 0)),
    ]
    if total is not None:
        operands.append(total)
        in_specs.append(space)
    size = rows_one * rows_two
    return pl.pallas_call(
        body,
        grid=(rows_one // block,),
        in_specs=in_specs,
        out_specs=space,
        out_shape=jax.ShapeDtypeStruct((rows_one, rows_two, length), jnp.float32),
        compiler_params=params(),
        cost_estimate=pl.CostEstimate(
            flops=6 * slots * size * sources * depth * length,
            bytes_accessed=4 * size * (slots * sources * depth + (2 + slots) * length),
            transcendentals=0,
        ),
        name="backward_last",
    )(*operands)


def cosine_turns():
    points = np.cos(np.pi * (np.arange(64) + 0.5) / 64) * 0.125 + 0.125
    fit = np.polynomial.Polynomial.fit(
        points, np.cos(2.0 * np.pi * np.sqrt(points)), 8, domain=[0.0, 0.25]
    )
    return [float(value) for value in fit.convert().coef]


def cosine_factors(saved, chosen, scale):
    rows_one, rows_two, length = saved.shape
    slots = chosen.shape[0]
    block = min(8, rows_one)
    coefficients = cosine_turns()

    def body(chosen_ref, saved_ref, out_ref):
        for slot in range(slots):
            feature = chosen_ref[slot]
            turns = saved_ref[...] * (feature * (1.0 / 16.0))
            turns = turns - jnp.round(turns)
            square = turns * turns
            result = jnp.full_like(square, coefficients[-1])
            for value in coefficients[-2::-1]:
                result = result * square + value
            out_ref[slot] = result * (feature * (math.pi / 8.0 * scale))

    size = rows_one * rows_two * length
    return pl.pallas_call(
        body,
        grid=(rows_one // block,),
        in_specs=[
            pl.BlockSpec(memory_space=pltpu.SMEM),
            pl.BlockSpec((block, rows_two, length), lambda i: (i, 0, 0)),
        ],
        out_specs=pl.BlockSpec((slots, block, rows_two, length), lambda i: (0, i, 0, 0)),
        out_shape=jax.ShapeDtypeStruct((slots, rows_one, rows_two, length), jnp.float32),
        compiler_params=params(),
        cost_estimate=pl.CostEstimate(
            flops=24 * slots * size, bytes_accessed=4 * size * (1 + slots), transcendentals=0
        ),
        name="cosine_factors",
    )(chosen, saved)


def kernel_planes(spectra, order, width_px, width_py):
    slots, length_one, local_two, length_three = spectra.shape
    half_one = length_one // 2
    half_px = width_px // 2
    devices = width_px * width_py
    own = length_three // devices
    px_index = lax.axis_index("px")
    py_index = lax.axis_index("py")
    folded = np.minimum(order, length_three - order).reshape(devices, own)
    distinct = [list(dict.fromkeys(row.tolist())) for row in folded]
    wanted = max(len(row) for row in distinct)
    padded = np.array([row + [row[-1]] * (wanted - len(row)) for row in distinct])
    place = np.array([[row.index(k) for k in ks] for row, ks in zip(distinct, folded)])
    padded = padded.reshape(2, half_px, width_py, wanted).transpose(0, 2, 1, 3)
    upper = px_index // half_px
    rows = jnp.asarray(padded.reshape(2 * width_py, half_px * wanted))[
        upper * width_py + py_index
    ]
    select = (rows[:, None] == jnp.arange(length_three)[None, :]).astype(jnp.bfloat16)
    pairs = [(0, half_px), (half_px, 0)]
    edge = lax.ppermute(spectra[:, : half_one + 1, 0].astype(jnp.float32), "px", pairs)
    chosen = jnp.einsum(
        "rk,jabk->rjba",
        select,
        spectra[:, : half_one + 1],
        preferred_element_type=jnp.float32,
    )
    chosen_edge = jnp.einsum(
        "rk,jak->rja",
        select.astype(jnp.float32),
        edge,
        precision=lax.Precision.HIGHEST,
        preferred_element_type=jnp.float32,
    )
    chosen = jnp.concatenate([chosen, chosen_edge[:, :, None]], axis=2)
    body = chosen[:, :, :, :half_one]
    last = chosen[:, :, None, :, half_one]
    last = jnp.pad(last, ((0, 0), (0, 0), (0, 0), (0, half_one - local_two - 1)))
    message = jnp.concatenate([body, last], axis=2)
    message = message.reshape(half_px, -1, half_one)
    groups = [list(range(half_px)), list(range(half_px, width_px))]
    message = lax.all_to_all(
        message, "px", 0, 0, axis_index_groups=groups, tiled=True
    )
    message = message.reshape(half_px, wanted, slots, local_two + 2, half_one)
    inner = message[:, :, :, :local_two].transpose(1, 2, 0, 3, 4)
    inner = inner.reshape(wanted, slots, half_px * local_two, half_one)
    edge_two = message[0, :, :, local_two]
    edge_one = message[:, :, :, local_two + 1, :local_two].transpose(1, 2, 0, 3)
    edge_one = edge_one.reshape(wanted, slots, half_px * local_two)
    corner = message[0, :, :, local_two + 1, local_two]
    inner = jnp.swapaxes(inner, 2, 3)
    lower = jnp.concatenate([edge_one[:, :, None], inner[:, :, 1:]], axis=2)
    left = jnp.concatenate([inner, lower], axis=2)
    column = jnp.concatenate([edge_two, corner[..., None], edge_two[..., 1:]], axis=2)
    right = jnp.concatenate([column[..., None], left[..., 1:]], axis=3)
    planes = jnp.concatenate([left, right], axis=3)
    places = jnp.asarray(place)[px_index * width_py + py_index]
    return jnp.take(planes, places, axis=0).transpose(1, 0, 2, 3)


def on_device(adjoint, saved, spectra, freq_index, picked):
    width_px = lax.axis_size("px")
    width_py = lax.axis_size("py")
    devices = width_px * width_py
    rows_one, rows_two, length_three = adjoint.shape
    length_one = rows_one * width_px
    length_two = rows_two * width_py
    slots = picked.shape[0]
    own = length_three // devices
    chunks = CHUNKS if own % (8 * CHUNKS) == 0 else 1
    depth = own // chunks
    order = paired_order(length_three)
    last = hartley(length_three)[order].reshape(devices, chunks, depth, length_three)
    order_one = folded_order(length_one, 0)
    one = hartley(length_one)[order_one]
    one_f = left_table(one)
    one_b = left_table(one.T)
    two = [hartley(length_two)[folded_order(length_two, b)] for b in (0, length_two // 2)]
    upper = lax.axis_index("px") >= width_px // 2
    two_f = jnp.where(upper, right_table(two[1].T), right_table(two[0].T))
    two_b = jnp.where(upper, right_table(two[1]), right_table(two[0]))
    tables = (jnp.asarray(one_f), two_f, jnp.asarray(one_b), two_b)

    feature_ids = jnp.arange(freq_index.shape[0], dtype=jnp.int32)
    chosen = jnp.sum(
        jnp.where(feature_ids[None, :] == picked[:, None], freq_index[None, :], 0), axis=1
    ).astype(jnp.float32)

    arrived = []
    for chunk in range(chunks):
        table = last[:, chunk].reshape(devices * depth, length_three)
        sent = forward_last(adjoint, jnp.asarray(left_table(table)))
        sent = sent.reshape(devices, depth, rows_one, rows_two)
        arrived.append(lax.all_to_all(sent, ("px", "py"), 0, 0, tiled=True))
    planes = kernel_planes(spectra, order, width_px, width_py)
    factors = cosine_factors(saved, chosen, 1.0 / (length_one * length_two * length_three))
    total = None
    returned = []
    for chunk in range(chunks):
        value = arrived[chunk].reshape(width_px, width_py, depth, rows_one, rows_two)
        value = filter_planes(
            value, planes[:, chunk * depth : (chunk + 1) * depth], tables
        )
        value = value.reshape(devices, slots, depth, rows_one, rows_two)
        returned.append(lax.all_to_all(value, ("px", "py"), 0, 0, tiled=True))
    for chunk in range(chunks):
        table = last[:, chunk].reshape(devices * depth, length_three)
        total = backward_last(
            returned[chunk], factors, jnp.asarray(right_table(table)), total
        )
    return total


def solution(mesh):
    placed = (
        P(("chain", "px"), "py", None),
        P(("chain", "px"), "py", None),
        P(None, None, "px", None),
        P(),
        P(),
    )
    return jax.shard_map(
        on_device,
        mesh=mesh,
        in_specs=placed,
        out_specs=P(("chain", "px"), "py", None),
        check_vma=False,
    )
```

time: 799 us -> 347 us (0.43); the launches traced: 784 us -> 346 us
  local copies, waits for them, and re-layouts: 290 us -> 23.3 us
  matrix products: 138 us -> 5.18 us
  other arithmetic: 139 us -> 13.6 us
  Pallas kernels: 0 us -> 66.1 us
  waiting for transfers between devices: 160 us -> 209 us
  blocking collectives: 34 us -> 0 us
    unnamed x71 -> x8, local copies, waits for them, and re-layouts: 128 us -> 0.01 us
    dot_general x12 -> x2, matrix products: 104 us -> 5.18 us  [the longest x1 4.9 us: kernel_planes(): jnp.einsum('rk,jabk->rjba', select, spectra[:, :half_one + 1], preferred_...]
    all_to_all x13 -> x1, local copies, waits for them, and re-layouts: 86.8 us -> 0.32 us  [kernel_planes(): lax.all_to_all(message, 'px', 0, 0, axis_index_groups=groups, tiled=True)]
    all_to_all x5 -> x0, other arithmetic: 74.6 us -> none  [the longest x2 32.9 us: on_device(): back = lax.all_to_all(back, 'py', split_axis=3, concat_axis=4, tiled=True)]
    pallas_call x0 -> x7, Pallas kernels: none -> 66.1 us  [the longest x2 28.7 us: filter_planes(): pl.pallas_call(body, grid=(planes_count,), in_specs=[pl.BlockSpec((width_...]
    all_to_all x3 -> x5, waiting for transfers between devices: 160 us -> 209 us  [the longest x2 152 us: on_device(): returned.append(lax.all_to_all(value, ('px', 'py'), 0, 0, tiled=True))]
    another operation x5 -> x3, local copies, waits for them, and re-layouts: 39.2 us -> 0.3 us  [the longest x1 0.11 us: kernel_planes(): last = chosen[:, :, None, :, half_one]]
    all_to_all x3 -> x0, blocking collectives: 34 us -> none  [the longest x2 26.2 us: on_device(): back = lax.all_to_all(back, 'py', split_axis=3, concat_axis=4, tiled=True)]
  transfers between devices with their start and end apart: 3 -> 6, of which waited for: 3 -> 5; matrix products, arithmetic and copies ran while one was open for 14% -> 11% of each run, Pallas kernels for 0% -> 16%
where the time goes in v1:
time: 347 us; the launch traced here: 346 us
  waiting for transfers between devices  209 us (60%)
  Pallas kernels  66.1 us (19%)
  starting transfers between devices  28.5 us (8%)
  local copies, waits for them, and re-layouts  23.3 us (7%)
  other arithmetic  13.6 us (4%)
  matrix products  5.18 us (1%)
    all_to_all x2, waiting for transfers between devices, on_device(): returned.append(lax.all_to_all(value, ('px', 'py'), 0, 0, tiled=True))  152 us
    all_to_all x2, waiting for transfers between devices, on_device(): arrived.append(lax.all_to_all(sent, ('px', 'py'), 0, 0, tiled=True))  47.2 us
    pallas_call x2, Pallas kernels, filter_planes(): pl.pallas_call(body, grid=(planes_count,), in_specs=[pl.BlockSpec((width_...  28.7 us
    pallas_call x2, Pallas kernels, backward_last(): pl.pallas_call(body, grid=(rows_one // block,), in_specs=in_specs, out_sp...  17.2 us
    all_to_all x2, starting transfers between devices, on_device(): arrived.append(lax.all_to_all(sent, ('px', 'py'), 0, 0, tiled=True))  12.5 us
    pallas_call x2, Pallas kernels, forward_last(): pl.pallas_call(body, grid=(rows_one // block,), in_specs=[pl.BlockSpec((b...  11.2 us
    all_to_all x2, starting transfers between devices, on_device(): returned.append(lax.all_to_all(value, ('px', 'py'), 0, 0, tiled=True))  10.5 us
    all_to_all x1, waiting for transfers between devices, kernel_planes(): lax.all_to_all(message, 'px', 0, 0, axis_index_groups=groups, tiled=True)  9.76 us
  transfers between devices with their start and end apart: 6, of which 5 were waited for; matrix products, arithmetic and copies ran while one was open for 11% of the time, Pallas kernels for 16%

profile of v1, /device:TPU:21, one launch (start us, length us, event | category | flops | bytes accessed | tf_op | source)
XLA Modules:
  0.0 346.0 jit_solution(62534805840288563)
XLA Ops:
  0.0 1.4 slice.40
  1.4 2.0 collective-permute-start
  3.4 4.6 %slice.39 = bf16[2,129,32,256]{3,2,1,0:T(8,128)(2,1)} slice(bf16[2,256,32,256]{3,2,1,0:T(8,128)(2,1)} %param.19), slice={[0:2], [0:129], [0:32], [0:256]} | slice | bytes 8454144 | tf_op jit(solution)/shard_map/slice | solution.py:306
  8.0 0.7 dynamic-slice_bitcast_fusion
  8.7 4.9 %fusion.4 = f32[36,2,32,129]{3,0,2,1:T(8,128)S(1)} fusion(bf16[2,129,32,256]{3,2,1,0:T(8,128)(2,1)} %slice.39, s32[36]{0:T(128)S(1)} %dynamic-slice_bitcast_fusion), kind=kOutput, calls=%fused_computation.11 | convolution fusion | flops 152183808 | bytes 5416080 | tf_op jit(solution)/shard_map/rk,jabk->rjba/dot_general | solution.py:303
  13.6 0.0 collective-permute-done
  13.6 0.3 convolution_bitcast_fusion
  13.9 0.1 pad_maximum_fusion
  14.0 0.1 fusion.7
  14.1 0.6 copy.47
  14.7 0.1 copy.48
  14.8 0.1 select_maximum_fusion.2
  14.9 0.3 copy.49
  15.2 1.2 reshape.68
  16.3 3.5 %all-to-all-start.1 = ((f32[4,612,128]{2,1,0:T(8,128)}), f32[4,612,128]{2,1,0:T(8,128)S(1)}, u32[]{:S(2)}, u32[]{:S(2)}) async-start(f32[4,612,128]{2,1,0:T(8,128)} %reshape.68), calls=%async_computation.1 | async-start | bytes 2523136 | tf_op jit(solution)/shard_map/all_to_all | solution.py:323
  19.9 5.6 %forward_last.3 = f32[128,32,128]{2,1,0:T(8,128)} custom-call(f32[32,128,256]{2,1,0:T(8,128)} %adjoint_ref.3, bf16[128,768]{1,0:T(8,128)(2,1)} %constant.76.clone.table_ref), custom_call_target="tpu_custom_call" | custom-call | flops 805306368 | bytes 6291456 | tf_op jit(solution)/shard_map/forward_last/pallas_call | solution.py:97
  25.5 9.8 %all-to-all-done.1 = f32[4,612,128]{2,1,0:T(8,128)S(1)} async-done(((f32[4,612,128]{2,1,0:T(8,128)}), f32[4,612,128]{2,1,0:T(8,128)S(1)}, u32[]{:S(2)}, u32[]{:S(2)}) %all-to-all-start.1) | async-done | bytes 1253408 | tf_op jit(solution)/shard_map/all_to_all | solution.py:323
  35.2 7.3 %all-to-all-start.3 = ((f32[16,8,32,128]{3,2,1,0:T(8,128)}), f32[16,8,32,128]{3,2,1,0:T(8,128)S(1)}, u32[]{:S(2)}, u32[]{:S(2)}) async-start(f32[16,8,32,128]{3,2,1,0:T(8,128)} %bitcast.51), calls=%async_computation.3 | async-start | bytes 4194304 | tf_op jit(solution)/shard_map/all_to_all | solution.py:376
  42.5 5.6 %forward_last.2 = f32[128,32,128]{2,1,0:T(8,128)} custom-call(f32[32,128,256]{2,1,0:T(8,128)} %adjoint_ref.3, bf16[128,768]{1,0:T(8,128)(2,1)} %constant.77.clone.table_ref), custom_call_target="tpu_custom_call" | custom-call | flops 805306368 | bytes 6291456 | tf_op jit(solution)/shard_map/forward_last/pallas_call | solution.py:97
  48.1 41.5 %all-to-all-done.3 = f32[16,8,32,128]{3,2,1,0:T(8,128)S(1)} async-done(((f32[16,8,32,128]{3,2,1,0:T(8,128)}), f32[16,8,32,128]{3,2,1,0:T(8,128)S(1)}, u32[]{:S(2)}, u32[]{:S(2)}) %all-to-all-start.3) | async-done | bytes 2097184 | tf_op jit(solution)/shard_map/all_to_all | solution.py:376
  89.6 0.0 copy-start
  89.6 5.2 %all-to-all-start = ((f32[16,8,32,128]{3,2,1,0:T(8,128)}), f32[16,8,32,128]{3,2,1,0:T(8,128)}, u32[]{:S(2)}, u32[]{:S(2)}) async-start(f32[16,8,32,128]{3,2,1,0:T(8,128)} %bitcast.50), calls=%async_computation | async-start | bytes 4194304 | tf_op jit(solution)/shard_map/all_to_all | solution.py:376
  94.8 0.7 fusion.16
  95.5 1.2 compare_and_fusion
  96.7 0.0 copy-done
  96.7 2.1 broadcast_select_fusion
  98.8 0.3 copy.50
  99.1 0.1 slice.60
  99.2 0.1 copy.53
  99.3 0.1 copy.54
  99.5 0.1 slice.61
  99.5 0.1 broadcast_in_dim_reshape.3
  99.6 0.1 slice_bitcast_fusion
  99.8 0.1 copy.51
  99.9 0.4 copy.52
  100.3 1.1 slice.58
  101.4 0.7 maximum_bitcast_fusion
  102.1 1.4 copy.55
  103.5 3.7 %fusion.1 = f32[9,2,256,256]{3,2,1,0:T(8,128)} fusion(f32[9,2,127,128]{3,2,1,0:T(8,128)} %slice.58, f32[9,2,1,128]{3,2,1,0:T(1,128)S(1)} %broadcast_in_dim_reshape.3, f32[9,2,128,128]{3,2,1,0:T(8,128)S(1)} %bitcast.49, f32[9,2,256,1]{3,2,1,0:T(8,128)S(1)} %copy.55), kind=kLoop, calls=%fused_computation.4 | loop fusion | flops 11796480 | bytes 7096320 | tf_op jit(solution)/shard_map/concatenate | solution.py:338
  107.2 0.0 copy-start.1
  107.2 6.6 %gather_fusion = f32[16,2,256,256]{3,2,1,0:T(8,128)} fusion(f32[9,2,256,256]{3,2,1,0:T(8,128)} %fusion.1, s32[1024]{0:T(1024)S(1)} %pad_clamp_fusion), kind=kCustom, calls=%fused_computation | custom fusion | bytes 16777280 | tf_op jit(solution)/shard_map/jit(_take)/gather | solution.py:340
  113.9 0.0 copy-done.1
  113.9 4.3 %fusion = f32[2,16,256,256]{3,2,1,0:T(8,128)S(1)} fusion(f32[16,2,256,256]{3,2,1,0:T(8,128)} %gather_fusion, pred[16]{0:T(512)(128)(4,1)S(1)} %copy-done.1), kind=kLoop, calls=%fused_computation.2 | loop fusion | flops 2097152 | bytes 16777232 | tf_op jit(solution)/shard_map/jit(_take)/select_n | solution.py:340
  118.1 3.9 %fusion.17 = (f32[2,8,256,256]{3,2,1,0:T(8,128)}, f32[2,8,256,256]{3,2,1,0:T(8,128)}) fusion(f32[2,16,256,256]{3,2,1,0:T(8,128)S(1)} %fusion), kind=kLoop, calls=%fused_computation.38 | loop fusion | bytes 16777216 | tf_op jit(solution)/shard_map/slice | solution.py:384
  122.0 14.3 %filter_planes.3 = f32[8,2,2,8,32,128]{5,4,3,2,1,0:T(8,128)} custom-call(f32[8,2,8,32,128]{4,3,2,1,0:T(8,128)} %bitcast.59, f32[2,8,256,256]{3,2,1,0:T(8,128)} %get-tuple-element.5.kernels_ref, bf16[256,768]{1,0:T(8,128)(2,1)} %constant.74.clone.one_f, bf16[768,256]{1,0:T(8,128)(2,1)} %get-tuple-element.8.two_f, bf16[256,768]{1,0:T(8,128)(2,1)} %constant.75.clone.one_b, ...), custom_call_target="tpu_custom_call" | custom-call | flops 4831838208 | bytes 8388608 | tf_op jit(solution)/shard_map/filter_planes/pallas_call | solution.py:142
  136.4 5.7 %all-to-all-done = f32[16,8,32,128]{3,2,1,0:T(8,128)} async-done(((f32[16,8,32,128]{3,2,1,0:T(8,128)}), f32[16,8,32,128]{3,2,1,0:T(8,128)}, u32[]{:S(2)}, u32[]{:S(2)}) %all-to-all-start) | async-done | bytes 2097184 | tf_op jit(solution)/shard_map/all_to_all | solution.py:376
  142.1 5.2 %all-to-all-start.4 = ((f32[16,2,8,32,128]{4,3,2,1,0:T(8,128)}), f32[16,2,8,32,128]{4,3,2,1,0:T(8,128)}, u32[]{:S(2)}, u32[]{:S(2)}) async-start(f32[16,2,8,32,128]{4,3,2,1,0:T(8,128)} %bitcast.58), calls=%async_computation.4 | async-start | bytes 8388608 | tf_op jit(solution)/shard_map/all_to_all | solution.py:387
  147.3 14.3 %filter_planes.2 = f32[8,2,2,8,32,128]{5,4,3,2,1,0:T(8,128)} custom-call(f32[8,2,8,32,128]{4,3,2,1,0:T(8,128)} %bitcast.1.planes_ref, f32[2,8,256,256]{3,2,1,0:T(8,128)} %get-tuple-element.6.kernels_ref, bf16[256,768]{1,0:T(8,128)(2,1)} %constant.74.clone.one_f, bf16[768,256]{1,0:T(8,128)(2,1)} %get-tuple-element.8.two_f, ...), custom_call_target="tpu_custom_call" | custom-call | flops 4831838208 | bytes 8388608 | tf_op jit(solution)/shard_map/filter_planes/pallas_call | solution.py:142
  161.6 77.8 %all-to-all-done.4.refs_0_ = f32[16,2,8,32,128]{4,3,2,1,0:T(8,128)} async-done(((f32[16,2,8,32,128]{4,3,2,1,0:T(8,128)}), f32[16,2,8,32,128]{4,3,2,1,0:T(8,128)}, u32[]{:S(2)}, u32[]{:S(2)}) %all-to-all-start.4) | async-done | bytes 4194336 | tf_op jit(solution)/shard_map/all_to_all | solution.py:387
  239.4 0.0 copy-start.2
  239.4 0.0 copy-start.3
  239.4 5.3 %all-to-all-start.2 = ((f32[16,2,8,32,128]{4,3,2,1,0:T(8,128)}), f32[16,2,8,32,128]{4,3,2,1,0:T(8,128)}, u32[]{:S(2)}, u32[]{:S(2)}) async-start(f32[16,2,8,32,128]{4,3,2,1,0:T(8,128)} %bitcast.57), calls=%async_computation.2 | async-start | bytes 8388608 | tf_op jit(solution)/shard_map/all_to_all | solution.py:387
  244.8 0.0 copy-done.2
  244.8 0.0 copy-done.3
  244.8 0.2 fusion.15
  245.0 0.5 convert_element_type.15.chosen_ref
  245.5 9.0 %cosine_factors.1.refs_1_ = f32[2,32,128,256]{3,2,1,0:T(8,128)} custom-call(f32[2]{0:T(128)} %convert_element_type.15.chosen_ref, f32[32,128,256]{2,1,0:T(8,128)} %saved_ref.1), custom_call_target="tpu_custom_call" | custom-call | flops 50331648 | bytes 12582912 | tf_op jit(solution)/shard_map/cosine_factors/pallas_call | solution.py:265
  254.5 8.2 %backward_last.2.refs_3_ = f32[32,128,256]{2,1,0:T(8,128)} custom-call(f32[16,2,8,32,128]{4,3,2,1,0:T(8,128)} %all-to-all-done.4.refs_0_, f32[2,32,128,256]{3,2,1,0:T(8,128)} %cosine_factors.1.refs_1_, bf16[384,256]{1,0:T(8,128)(2,1)} %constant.80.clone.refs_2_), custom_call_target="tpu_custom_call" | custom-call | flops 1610612736 | bytes 20971520 | tf_op jit(solution)/shard_map/backward_last/pallas_call | solution.py:223
  262.7 74.3 %all-to-all-done.2.refs_0_ = f32[16,2,8,32,128]{4,3,2,1,0:T(8,128)} async-done(((f32[16,2,8,32,128]{4,3,2,1,0:T(8,128)}), f32[16,2,8,32,128]{4,3,2,1,0:T(8,128)}, u32[]{:S(2)}, u32[]{:S(2)}) %all-to-all-start.2) | async-done | bytes 4194336 | tf_op jit(solution)/shard_map/all_to_all | solution.py:387
  337.0 9.0 %backward_last.3 = f32[32,128,256]{2,1,0:T(8,128)} custom-call(f32[16,2,8,32,128]{4,3,2,1,0:T(8,128)} %all-to-all-done.2.refs_0_, f32[2,32,128,256]{3,2,1,0:T(8,128)} %cosine_factors.1.refs_1_, bf16[384,256]{1,0:T(8,128)(2,1)} %constant.81.clone.refs_2_, f32[32,128,256]{2,1,0:T(8,128)} %backward_last.2.refs_3_), custom_call_target="tpu_custom_call" | custom-call | flops 1610612736 | bytes 20971520 | tf_op jit(solution)/shard_map/backward_last/pallas_call | solution.py:223
  (4 shorter events, 0.0 us)
Async XLA Ops:
  1.4 12.2 %collective-permute-start = (f32[2,129,256]{2,1,0:T(8,128)S(1)}, f32[2,129,256]{2,1,0:T(8,128)S(1)}, u32[]{:S(2)}, u32[]{:S(2)}) collective-permute-start(f32[2,129,256]{2,1,0:T(8,128)S(1)} %fusion.8), channel_id=1, source_target_pairs={{0,8},{8,0},{1,9},{9,1},{16,24},{24,16},{17,25},{25,17}} | collective-permute-start | bytes 792584 | tf_op jit(solution)/shard_map/ppermute | solution.py:302
  16.3 18.9 %all-to-all-start.1 = ((f32[4,612,128]{2,1,0:T(8,128)}), f32[4,612,128]{2,1,0:T(8,128)S(1)}, u32[]{:S(2)}, u32[]{:S(2)}) async-start(f32[4,612,128]{2,1,0:T(8,128)} %reshape.68), calls=%async_computation.1 | async-start | bytes 2523136 | tf_op jit(solution)/shard_map/all_to_all | solution.py:323
  35.2 54.4 %all-to-all-start.3 = ((f32[16,8,32,128]{3,2,1,0:T(8,128)}), f32[16,8,32,128]{3,2,1,0:T(8,128)S(1)}, u32[]{:S(2)}, u32[]{:S(2)}) async-start(f32[16,8,32,128]{3,2,1,0:T(8,128)} %bitcast.51), calls=%async_computation.3 | async-start | bytes 4194304 | tf_op jit(solution)/shard_map/all_to_all | solution.py:376
  89.6 7.1 %copy-start = (f32[16,8,32,128]{3,2,1,0:T(8,128)}, f32[16,8,32,128]{3,2,1,0:T(8,128)S(1)}, u32[]{:S(2)}) copy-start(f32[16,8,32,128]{3,2,1,0:T(8,128)S(1)} %all-to-all-done.3) | copy-start | bytes 6291460
  89.6 52.4 %all-to-all-start = ((f32[16,8,32,128]{3,2,1,0:T(8,128)}), f32[16,8,32,128]{3,2,1,0:T(8,128)}, u32[]{:S(2)}, u32[]{:S(2)}) async-start(f32[16,8,32,128]{3,2,1,0:T(8,128)} %bitcast.50), calls=%async_computation | async-start | bytes 4194304 | tf_op jit(solution)/shard_map/all_to_all | solution.py:376
  107.2 6.6 %copy-start.1 = (pred[16]{0:T(512)(128)(4,1)S(1)}, pred[16]{0:T(512)(128)(4,1)}, u32[]{:S(2)}) copy-start(pred[16]{0:T(512)(128)(4,1)} %compare_and_fusion) | copy-start | bytes 52
  142.1 97.4 %all-to-all-start.4 = ((f32[16,2,8,32,128]{4,3,2,1,0:T(8,128)}), f32[16,2,8,32,128]{4,3,2,1,0:T(8,128)}, u32[]{:S(2)}, u32[]{:S(2)}) async-start(f32[16,2,8,32,128]{4,3,2,1,0:T(8,128)} %bitcast.58), calls=%async_computation.4 | async-start | bytes 8388608 | tf_op jit(solution)/shard_map/all_to_all | solution.py:387
  239.4 5.3 %copy-start.2 = (s32[8]{0:T(128)S(1)}, s32[8]{0:T(128)}, u32[]{:S(2)}) copy-start(s32[8]{0:T(128)} %param.20) | copy-start | bytes 100
  239.4 5.3 %copy-start.3 = (s32[2]{0:T(128)S(1)}, s32[2]{0:T(128)}, u32[]{:S(2)}) copy-start(s32[2]{0:T(128)} %param.21) | copy-start | bytes 28
  239.4 97.5 %all-to-all-start.2 = ((f32[16,2,8,32,128]{4,3,2,1,0:T(8,128)}), f32[16,2,8,32,128]{4,3,2,1,0:T(8,128)}, u32[]{:S(2)}, u32[]{:S(2)}) async-start(f32[16,2,8,32,128]{4,3,2,1,0:T(8,128)} %bitcast.57), calls=%async_computation.2 | async-start | bytes 8388608 | tf_op jit(solution)/shard_map/all_to_all | solution.py:387

commit v2 on v1

v2 whole, which is shorter than its diff:
```python
import math

import jax
import jax.numpy as jnp
import numpy as np
from jax import lax
from jax.experimental import pallas as pl
from jax.experimental.pallas import tpu as pltpu
from jax.sharding import PartitionSpec as P

VMEM_BYTES = 56 * 1024 * 1024
SHARED = 2


def hartley(length):
    counter = np.arange(length)
    angle = 2.0 * np.pi * ((counter[:, None] * counter[None, :]) % length) / length
    return np.cos(angle) + np.sin(angle)


def split_table(table):
    high = table.astype(np.float32).astype(jnp.bfloat16)
    low = (table - high.astype(np.float64)).astype(np.float32).astype(jnp.bfloat16)
    return high, low


def left_table(table):
    high, low = split_table(table)
    return jnp.asarray(np.concatenate([high, high, low], axis=1))


def right_table(table):
    high, low = split_table(table)
    return jnp.asarray(np.concatenate([high, high, low], axis=0))


def traced_table(rows, columns, length, axis):
    product = rows[:, None] * columns[None, :] % length
    angle = product.astype(jnp.float32) * (2.0 * math.pi / length)
    value = jnp.cos(angle) + jnp.sin(angle)
    high = lax.reduce_precision(value, 8, 7)
    low = value - high
    return jnp.concatenate([high, high, low], axis=axis).astype(jnp.bfloat16)


def partners(first, length):
    base = first % (length // 2) == 0
    return jnp.where(base, (first + length // 2) % length, (length - first) % length)


def paired_order(length):
    half = length // 2
    order = [0, half]
    for index in range(1, half):
        order += [index, length - index]
    return np.array(order)


def split_value(value):
    high = value.astype(jnp.bfloat16)
    low = (value - high.astype(jnp.float32)).astype(jnp.bfloat16)
    return high, low


def left_dot(table, value):
    high, low = split_value(value)
    stacked = jnp.concatenate([high, low, high], axis=0)
    return jnp.dot(table, stacked, preferred_element_type=jnp.float32)


def right_dot(value, table):
    high, low = split_value(value)
    stacked = jnp.concatenate([high, low, high], axis=1)
    return jnp.dot(stacked, table, preferred_element_type=jnp.float32)


def params():
    return pltpu.CompilerParams(vmem_limit_bytes=VMEM_BYTES)


def forward_last(adjoint, table, copies):
    rows_one, rows_two, length = adjoint.shape
    count = table.shape[0]
    block = min(8, rows_one)

    def body(adjoint_ref, table_ref, out_ref):
        flat = out_ref.reshape(copies * count * block, rows_two)
        for start in range(0, block, 2):
            value = adjoint_ref[start : start + 2].reshape(2 * rows_two, length)
            high, low = split_value(value)
            stacked = jnp.concatenate([high, low, high], axis=1)
            result = lax.dot_general(
                table_ref[...],
                stacked,
                (((1,), (1,)), ((), ())),
                preferred_element_type=jnp.float32,
            )
            for inner in range(2):
                piece = result[:, inner * rows_two : (inner + 1) * rows_two]
                for copy in range(copies):
                    first = copy * count * block + start + inner
                    flat[pl.ds(first, count, stride=block), :] = piece

    return pl.pallas_call(
        body,
        grid=(rows_one // block,),
        in_specs=[
            pl.BlockSpec((block, rows_two, length), lambda i: (i, 0, 0)),
            pl.BlockSpec(table.shape, lambda i: (0, 0)),
        ],
        out_specs=pl.BlockSpec((copies, count, block, rows_two), lambda i: (0, 0, i, 0)),
        out_shape=jax.ShapeDtypeStruct((copies, count, rows_one, rows_two), jnp.float32),
        compiler_params=params(),
        cost_estimate=pl.CostEstimate(
            flops=6 * count * rows_one * rows_two * length,
            bytes_accessed=4 * rows_one * rows_two * (length + copies * count),
            transcendentals=0,
        ),
        name="forward_last",
    )(adjoint, table)


def whole_plane(message_refs, slot, slots, special, local_two):
    blocks = [ref[0] for ref in message_refs]
    body = [block[slot * local_two : (slot + 1) * local_two] for block in blocks]
    folded = jnp.concatenate(body, axis=0)
    first = slots * local_two + 3 * slot
    edges = blocks[0][first : first + 3]
    for block in blocks[1:]:
        edges = edges + block[first : first + 3]
    edge_two, edge_one, corner = edges[0:1], edges[1:2], edges[2:3]
    extent = folded.shape
    row = lax.broadcasted_iota(jnp.int32, extent, 0)
    column = lax.broadcasted_iota(jnp.int32, extent, 1)
    right = jnp.where(row == special, edge_two, folded).T
    left = folded.T
    top = row == 0
    lower_left = jnp.where(top, edge_one, left)
    lower_right = jnp.where(top, jnp.where(column == special, corner, edge_one), right)
    return jnp.concatenate(
        [
            jnp.concatenate([left, right], axis=1),
            jnp.concatenate([lower_left, lower_right], axis=1),
        ],
        axis=0,
    )


def filter_planes(planes, messages, places, special, tables, slots, split):
    width_px, width_py, planes_count, rows_one, rows_two = planes.shape
    length_one = width_px * rows_one
    length_two = width_py * rows_two
    out_px = tables[2].shape[0] // rows_one
    message_rows = messages[0].shape[1]
    local_two = length_two // 2 // len(messages)

    def body(places_ref, special_ref, planes_ref, *refs):
        message_refs = refs[: len(messages)]
        one_f, two_f, one_b, two_b = refs[len(messages) : len(messages) + 4]
        out_refs = refs[len(messages) + 4 :]
        value = jnp.concatenate(
            [
                planes_ref[:, part, 0].reshape(length_one, rows_two)
                for part in range(width_py)
            ],
            axis=1,
        )
        value = right_dot(value, two_f[...])
        value = left_dot(one_f[...], value)
        for slot in range(slots):
            plane = whole_plane(message_refs, slot, slots, special_ref[0], local_two)
            back = left_dot(one_b[...], value * plane)
            back = right_dot(back, two_b[...])
            for part in range(width_py):
                piece = back[:, part * rows_two : (part + 1) * rows_two]
                if split:
                    for index in range(out_px):
                        out_refs[index][part, slot, 0] = piece[
                            index * rows_one : (index + 1) * rows_one
                        ]
                else:
                    out_refs[0][:, part, slot, 0] = piece.reshape(
                        out_px, rows_one, rows_two
                    )

    plane_size = length_one * length_two
    if split:
        extent = (width_py, slots, planes_count, rows_one, rows_two)
        out_shape = [jax.ShapeDtypeStruct(extent, jnp.float32)] * out_px
        out_specs = [
            pl.BlockSpec(
                (width_py, slots, 1, rows_one, rows_two), lambda i, *_: (0, 0, i, 0, 0)
            )
        ] * out_px
    else:
        extent = (out_px, width_py, slots, planes_count, rows_one, rows_two)
        out_shape = [jax.ShapeDtypeStruct(extent, jnp.float32)]
        out_specs = [
            pl.BlockSpec(
                (out_px, width_py, slots, 1, rows_one, rows_two),
                lambda i, *_: (0, 0, 0, i, 0, 0),
            )
        ]
    out_rows = out_px * rows_one
    outs = pl.pallas_call(
        body,
        grid_spec=pltpu.PrefetchScalarGridSpec(
            num_scalar_prefetch=2,
            grid=(planes_count,),
            in_specs=[
                pl.BlockSpec(
                    (width_px, width_py, 1, rows_one, rows_two),
                    lambda i, *_: (0, 0, i, 0, 0),
                )
            ]
            + [
                pl.BlockSpec(
                    (1, message_rows, length_one // 2),
                    lambda i, places_ref, special_ref: (places_ref[i], 0, 0),
                )
            ]
            * len(messages)
            + [pl.BlockSpec(table.shape, lambda i, *_: (0, 0)) for table in tables],
            out_specs=out_specs,
        ),
        out_shape=out_shape,
        compiler_params=params(),
        cost_estimate=pl.CostEstimate(
            flops=6
            * planes_count
            * (
                plane_size * (length_one + length_two)
                + slots * out_rows * length_two * (length_one + length_two)
            ),
            bytes_accessed=4
            * planes_count
            * (plane_size + slots * (plane_size // 4 + out_rows * length_two)),
            transcendentals=0,
        ),
        name="filter_planes",
    )(places, special, planes, *messages, *tables)
    return outs if split else outs[0]


def backward_last(groups, factors, total):
    parts = [part for members, _ in groups for part in members]
    tables = [table for _, table in groups]
    slots = factors.shape[0]
    rows_one, rows_two = parts[0].shape[3:]
    length = tables[0].shape[1]
    block = min(8, rows_one)

    def body(*refs):
        factors_ref = refs[0]
        table_refs = refs[1 : 1 + len(groups)]
        part_refs = refs[1 + len(groups) : 1 + len(groups) + len(parts)]
        out_ref = refs[-1]
        flats = [
            ref.reshape(math.prod(part.shape[:3]) * block, rows_two)
            for ref, part in zip(part_refs, parts)
        ]

        def columns(slot, site, first, last):
            found = []
            for index in range(first, last):
                sources, _, depth = parts[index].shape[:3]
                for source in range(sources):
                    row = (source * slots + slot) * depth * block + site
                    found.append(flats[index][pl.ds(row, depth, stride=block), :])
            return jnp.concatenate(found, axis=0).T

        for start in range(0, block, 2):
            result = None
            for slot in range(slots):
                field = None
                first = 0
                for (members, _), table_ref in zip(groups, table_refs):
                    last = first + len(members)
                    value = jnp.concatenate(
                        [columns(slot, start + inner, first, last) for inner in range(2)],
                        axis=0,
                    )
                    value = right_dot(value, table_ref[...])
                    field = value if field is None else field + value
                    first = last
                field = field.reshape(2, rows_two, length)
                term = field * factors_ref[slot, start : start + 2]
                result = term if result is None else result + term
            if total is not None:
                result = result + refs[-2][start : start + 2]
            out_ref[start : start + 2] = result

    space = pl.BlockSpec((block, rows_two, length), lambda i: (i, 0, 0))
    operands = [factors] + tables + parts
    in_specs = (
        [pl.BlockSpec((slots, block, rows_two, length), lambda i: (0, i, 0, 0))]
        + [pl.BlockSpec(table.shape, lambda i: (0, 0)) for table in tables]
        + [
            pl.BlockSpec(part.shape[:3] + (block, rows_two), lambda i: (0, 0, 0, i, 0))
            for part in parts
        ]
    )
    if total is not None:
        operands.append(total)
        in_specs.append(space)
    size = rows_one * rows_two
    planes_count = sum(part.shape[0] * part.shape[2] for part in parts)
    return pl.pallas_call(
        body,
        grid=(rows_one // block,),
        in_specs=in_specs,
        out_specs=space,
        out_shape=jax.ShapeDtypeStruct((rows_one, rows_two, length), jnp.float32),
        compiler_params=params(),
        cost_estimate=pl.CostEstimate(
            flops=6 * slots * size * planes_count * length,
            bytes_accessed=4 * size * (slots * planes_count + (2 + slots) * length),
            transcendentals=0,
        ),
        name="backward_last",
    )(*operands)


def cosine_turns():
    points = np.cos(np.pi * (np.arange(64) + 0.5) / 64) * 0.125 + 0.125
    fit = np.polynomial.Polynomial.fit(
        points, np.cos(2.0 * np.pi * np.sqrt(points)), 8, domain=[0.0, 0.25]
    )
    return [float(value) for value in fit.convert().coef]


def cosine_factors(saved, chosen, scale):
    rows_one, rows_two, length = saved.shape
    slots = chosen.shape[0]
    block = min(8, rows_one)
    coefficients = cosine_turns()

    def body(chosen_ref, saved_ref, out_ref):
        for slot in range(slots):
            feature = chosen_ref[slot]
            turns = saved_ref[...] * (feature * (1.0 / 16.0))
            turns = turns - jnp.round(turns)
            square = turns * turns
            result = jnp.full_like(square, coefficients[-1])
            for value in coefficients[-2::-1]:
                result = result * square + value
            out_ref[slot] = result * (feature * (math.pi / 8.0 * scale))

    size = rows_one * rows_two * length
    return pl.pallas_call(
        body,
        grid=(rows_one // block,),
        in_specs=[
            pl.BlockSpec(memory_space=pltpu.SMEM),
            pl.BlockSpec((block, rows_two, length), lambda i: (i, 0, 0)),
        ],
        out_specs=pl.BlockSpec((slots, block, rows_two, length), lambda i: (0, i, 0, 0)),
        out_shape=jax.ShapeDtypeStruct((slots, rows_one, rows_two, length), jnp.float32),
        compiler_params=params(),
        cost_estimate=pl.CostEstimate(
            flops=24 * slots * size, bytes_accessed=4 * size * (1 + slots), transcendentals=0
        ),
        name="cosine_factors",
    )(chosen, saved)


def swap_pairs(width_px, half_px, delta):
    return [(px, px // half_px * half_px + (px % half_px ^ delta)) for px in range(width_px)]


def send_messages(message, width_px):
    half_px = width_px // 2
    if half_px <= 8:
        return [message[0]] + [
            lax.ppermute(message[delta], "px", swap_pairs(width_px, half_px, delta))
            for delta in range(1, half_px)
        ]
    groups = [list(range(half_px)), list(range(half_px, width_px))]
    index = lax.axis_index("px") % half_px ^ jnp.arange(half_px)
    message = jnp.take(jnp.stack(message), index, axis=0)
    message = lax.all_to_all(message, "px", 0, 0, axis_index_groups=groups, tiled=True)
    message = jnp.take(message, index, axis=0)
    return [message[delta] for delta in range(half_px)]


def message_rows(spectra, edge, select, count):
    slots, length_one, local_two, length_three = spectra.shape
    half_one = length_one // 2
    half_px = half_one // local_two
    padded = select.shape[0] // half_px
    used = slots * (local_two + 3)
    extent = used + -used % 8
    group = 4
    lanes = 128

    def body(spectra_ref, edge_ref, select_ref, *refs):
        flats = [ref.reshape(count * extent, half_one) for ref in refs[:half_px]]
        scratch = refs[half_px:]

        def chosen(value):
            return lax.dot_general(
                select_ref[...],
                value.astype(jnp.bfloat16),
                (((1,), (1,)), ((), ())),
                preferred_element_type=jnp.float32,
            )

        def store(value, row):
            for delta in range(half_px):
                flats[delta][pl.ds(row, count, stride=extent), :] = value[
                    delta * padded : delta * padded + count
                ]

        for slot in range(slots):
            for part, ref in enumerate(scratch):
                ref[...] = (
                    spectra_ref[slot, :half_one, :, part * lanes : (part + 1) * lanes]
                    .astype(jnp.float32)
                    .reshape(half_one * local_two, lanes)
                )
            for start in range(0, local_two, group):
                value = jnp.concatenate(
                    [
                        jnp.concatenate(
                            [
                                ref[pl.ds(start + inner, half_one, stride=local_two), :]
                                for ref in scratch
                            ],
                            axis=1,
                        )
                        for inner in range(group)
                    ],
                    axis=0,
                )
                value = chosen(value)
                for inner in range(group):
                    store(
                        value[:, inner * half_one : (inner + 1) * half_one],
                        slot * local_two + start + inner,
                    )
            first = slots * local_two + 3 * slot
            store(chosen(edge_ref[slot, :half_one]), first)
            tiled = jnp.concatenate([spectra_ref[slot, half_one]] * half_px, axis=0)
            value = chosen(tiled)
            row = lax.broadcasted_iota(jnp.int32, value.shape, 0) // padded
            lane = lax.broadcasted_iota(jnp.int32, value.shape, 1) // local_two
            store(jnp.where(row == lane, value, 0.0), first + 1)
            corner = edge_ref[slot, half_one : half_one + 1]
            store(chosen(jnp.broadcast_to(corner, (half_one, length_three))), first + 2)
        for flat in flats:
            for row in range(used, extent):
                flat[pl.ds(row, count, stride=extent), :] = jnp.zeros(
                    (count, half_one), jnp.float32
                )

    part = (slots, half_one + 1, local_two, length_three)
    return pl.pallas_call(
        body,
        grid=(1,),
        in_specs=[
            pl.BlockSpec(part, lambda i: (0, 0, 0, 0)),
            pl.BlockSpec(edge.shape, lambda i: (0, 0, 0)),
            pl.BlockSpec(select.shape, lambda i: (0, 0)),
        ],
        out_specs=[pl.BlockSpec((count, extent, half_one), lambda i: (0, 0, 0))] * half_px,
        out_shape=[jax.ShapeDtypeStruct((count, extent, half_one), jnp.float32)] * half_px,
        scratch_shapes=[pltpu.VMEM((half_one * local_two, lanes), jnp.float32)]
        * (length_three // lanes),
        compiler_params=params(),
        cost_estimate=pl.CostEstimate(
            flops=2 * slots * select.shape[0] * half_one * local_two * length_three,
            bytes_accessed=2 * math.prod(part) + 4 * half_px * count * extent * half_one,
            transcendentals=0,
        ),
        name="message_rows",
    )(spectra, edge, select)


def kernel_messages(spectra, edge, wanted, width_px, width_py):
    slots, length_one, local_two, length_three = spectra.shape
    half_one = length_one // 2
    half_px = width_px // 2
    count = wanted.shape[1]
    px_index = lax.axis_index("px")
    py_index = lax.axis_index("py")
    wanted = wanted.reshape(width_px, width_py, count)
    sources = np.arange(width_px)
    targets = np.stack(
        [sources // half_px * half_px + (sources % half_px ^ d) for d in range(half_px)],
        axis=1,
    )
    rows = jnp.asarray(wanted[targets].transpose(0, 2, 1, 3).reshape(-1, half_px * count))
    rows = rows[px_index * width_py + py_index]
    sublanes = 16
    if local_two % sublanes == 0:
        padded = count + -count % sublanes
        rows = rows.reshape(half_px, count)
        rows = jnp.pad(rows, ((0, 0), (0, padded - count)), constant_values=-1)
        rows = rows.reshape(-1)
        select = (rows[:, None] == jnp.arange(length_three)[None, :]).astype(jnp.bfloat16)
        return message_rows(spectra, edge, select, count)
    select = (rows[:, None] == jnp.arange(length_three)[None, :]).astype(jnp.bfloat16)
    chosen = jnp.einsum(
        "rk,jabk->rjba",
        select,
        spectra[:, : half_one + 1],
        preferred_element_type=jnp.float32,
    )
    chosen_edge = jnp.einsum(
        "rk,jak->rja",
        select.astype(jnp.float32),
        edge,
        precision=lax.Precision.HIGHEST,
        preferred_element_type=jnp.float32,
    )
    body = chosen[..., :half_one].reshape(half_px, count, slots * local_two, half_one)
    edge_two = chosen_edge[..., None, :half_one]
    corner = jnp.broadcast_to(chosen_edge[..., None, half_one:], edge_two.shape)
    last = chosen[..., half_one].reshape(half_px, count, slots, local_two)
    edge_one = jnp.stack(
        [
            jnp.pad(
                last[delta],
                (
                    (0, 0),
                    (0, 0),
                    (delta * local_two, (half_px - 1 - delta) * local_two),
                ),
            )
            for delta in range(half_px)
        ]
    )
    edge_one = edge_one.reshape(half_px * count, slots, 1, half_px * local_two)
    edges = jnp.concatenate([edge_two, edge_one, corner], axis=2)
    edges = edges.reshape(half_px, count, 3 * slots, half_one)
    spare = -(slots * (local_two + 3)) % 8
    message = jnp.concatenate([body, edges], axis=2)
    message = jnp.pad(message, ((0, 0), (0, 0), (0, spare), (0, 0)))
    return [message[delta] for delta in range(half_px)]


def on_device(adjoint, saved, spectra, freq_index, picked):
    width_px = lax.axis_size("px")
    width_py = lax.axis_size("py")
    px_index = lax.axis_index("px")
    py_index = lax.axis_index("py")
    devices = width_px * width_py
    half_px = width_px // 2
    half_devices = devices // 2
    half_index = px_index // half_px
    px_low = px_index % half_px
    rows_one, rows_two, length_three = adjoint.shape
    length_one = rows_one * width_px
    length_two = rows_two * width_py
    slots = picked.shape[0]

    order = paired_order(length_three)
    shared_depth = 8
    shared_chunks = SHARED if length_three % (8 * devices * SHARED) == 0 else 0
    shared_count = half_devices * shared_depth
    shared = [
        order[chunk * shared_count : (chunk + 1) * shared_count].reshape(half_devices, -1)
        for chunk in range(shared_chunks)
    ]
    single = order[shared_chunks * shared_count :].reshape(devices, -1)
    depth = single.shape[1]
    owned = [np.concatenate([chunk, chunk]) for chunk in shared] + [single]
    folded = np.concatenate(owned, axis=1)
    folded = np.minimum(folded, length_three - folded)
    distinct = [list(dict.fromkeys(row.tolist())) for row in folded]
    count = max(len(row) for row in distinct)
    wanted = np.array([row + [row[-1]] * (count - len(row)) for row in distinct])
    places = np.array([[row.index(k) for k in ks] for row, ks in zip(distinct, folded)])

    half_one = length_one // 2
    edge = lax.ppermute(
        spectra[:, : half_one + 1, 0].astype(jnp.float32),
        "px",
        [(0, half_px), (half_px, 0)],
    )
    last = hartley(length_three)
    sent_shared = []
    for chunk in shared:
        sent_shared.append(
            forward_last(adjoint, left_table(last[chunk.reshape(-1)]), 2).reshape(
                devices, shared_depth, rows_one, rows_two
            )
        )
    sent_single = forward_last(adjoint, left_table(last[single.reshape(-1)]), 1).reshape(
        devices, depth, rows_one, rows_two
    )

    def exchange(value):
        return lax.all_to_all(value, ("px", "py"), 0, 0, tiled=True)

    def arranged(value):
        return value.reshape(width_px, width_py, -1, rows_one, rows_two)

    if shared_chunks:
        sent_shared[0], spectra, edge = lax.optimization_barrier(
            (sent_shared[0], spectra, edge)
        )
    messages = kernel_messages(spectra, edge, wanted, width_px, width_py)
    messages = send_messages(messages, width_px)
    if shared_chunks:
        sent_single, messages = lax.optimization_barrier((sent_single, messages))
    places = jnp.asarray(places, dtype=jnp.int32)[px_index * width_py + py_index]
    local_two = length_two // width_px
    special = (px_low * local_two).astype(jnp.int32).reshape(1)

    order_one = np.arange(length_one // 2)
    order_one = np.concatenate([order_one, (length_one - order_one) % length_one])
    order_one[length_one // 2] = length_one // 2
    slabs = half_index * half_px + (px_low ^ jnp.arange(half_px))
    order_two = (slabs[:, None] * local_two + jnp.arange(local_two)[None, :]).reshape(-1)
    order_two = jnp.concatenate([order_two, partners(order_two, length_two)])
    one = hartley(length_one)[order_one]
    one_f = left_table(one)
    one_b = left_table(one.T)
    sites_two = jnp.arange(length_two)
    two_f = traced_table(sites_two, order_two, length_two, 0)
    two_b = traced_table(order_two, sites_two, length_two, 0)
    sites_half = (slabs[:, None] * rows_one + jnp.arange(rows_one)[None, :]).reshape(-1)
    half_one_b = traced_table(sites_half, jnp.asarray(order_one), length_one, 1)
    near_two = (sites_two + py_index * rows_two) % length_two
    near_two_b = traced_table(order_two, near_two, length_two, 0)
    tables = (one_f, two_f, one_b, two_b)
    half_tables = (one_f, two_f, half_one_b, near_two_b)

    feature_ids = jnp.arange(freq_index.shape[0], dtype=jnp.int32)
    chosen = jnp.sum(
        jnp.where(feature_ids[None, :] == picked[:, None], freq_index[None, :], 0), axis=1
    ).astype(jnp.float32)

    shared_source = (
        (px_low ^ jnp.arange(half_px))[None, :] * width_py
        + ((py_index - jnp.arange(width_py)) % width_py)[:, None]
    ).reshape(-1)

    def shared_fields(index, value):
        first = index * shared_depth
        return filter_planes(
            arranged(value),
            messages,
            places[first : first + shared_depth],
            special,
            half_tables,
            slots,
            True,
        )

    def shared_rows(pieces):
        return [pieces[0]] + [
            lax.ppermute(pieces[delta], "px", swap_pairs(width_px, half_px, delta))
            for delta in range(1, half_px)
        ]

    def shared_group(index, pieces):
        parts = [jnp.stack([piece[0] for piece in pieces])]
        for shift in range(1, width_py):
            pairs = [(c, (c + shift) % width_py) for c in range(width_py)]
            far = jnp.stack([piece[shift] for piece in pieces])
            parts.append(lax.ppermute(far, "py", pairs))
        ids = jnp.asarray(shared[index])[shared_source].reshape(-1)
        return parts, traced_table(ids, jnp.arange(length_three), length_three, 0)

    barrier = lax.optimization_barrier
    factors = cosine_factors(saved, chosen, 1.0 / (length_one * length_two * length_three))
    single_table = right_table(last[single.reshape(-1)])
    first = shared_chunks * shared_depth

    def single_fields(value):
        return filter_planes(
            arranged(value),
            messages,
            places[first : first + depth],
            special,
            tables,
            slots,
            False,
        ).reshape(devices, slots, depth, rows_one, rows_two)

    if shared_chunks == 0:
        returned = exchange(single_fields(exchange(sent_single)))
        return backward_last([([returned], single_table)], factors, None)

    arrived = exchange(sent_shared[0])
    arrived_single = exchange(sent_single)
    pieces = shared_fields(0, arrived)
    pieces, sent_shared[1] = barrier((pieces, sent_shared[1]))
    near = shared_rows(pieces)
    arrived = exchange(sent_shared[1])
    fields_single = single_fields(arrived_single)
    fields_single, factors, near = barrier((fields_single, factors, near))
    returned = exchange(fields_single)
    pieces = shared_fields(1, arrived)
    pieces, near = barrier((pieces, near))
    group = shared_group(0, near)
    late = shared_rows(pieces)
    total = backward_last([group], factors, None)
    late, total = barrier((late, total))
    return backward_last(
        [shared_group(1, late), ([returned], single_table)], factors, total
    )


def solution(mesh):
    placed = (
        P(("chain", "px"), "py", None),
        P(("chain", "px"), "py", None),
        P(None, None, "px", None),
        P(),
        P(),
    )
    return jax.shard_map(
        on_device,
        mesh=mesh,
        in_specs=placed,
        out_specs=P(("chain", "px"), "py", None),
        check_vma=False,
    )
```

time: 347 us -> 315 us (0.908)
  waiting for transfers between devices: 209 us -> 163 us
  Pallas kernels: 66.1 us -> 95.5 us
  local copies, waits for them, and re-layouts: 23.3 us -> 10.3 us
  matrix products: 5.18 us -> 0 us
  starting transfers between devices: 28.5 us -> 32.3 us
    all_to_all x5 -> x4, waiting for transfers between devices: 209 us -> 20.6 us  [exchange(): return lax.all_to_all(value, ('px', 'py'), 0, 0, tiled=True)]
    ppermute x1 -> x12, waiting for transfers between devices: 0.01 us -> 142 us  [the longest x6 101 us: shared_rows(): lax.ppermute(pieces[delta], 'px', swap_pairs(width_px, half_px, delta))]
    pallas_call x2 -> x4, Pallas kernels: 28.7 us -> 51.4 us  [the longest x3 42 us: filter_planes(): pl.pallas_call(body, grid_spec=pltpu.PrefetchScalarGridSpec(num_scalar_pr...]
    ppermute x1 -> x12, starting transfers between devices: 1.96 us -> 11.6 us  [the longest x6 5.3 us: shared_rows(): lax.ppermute(pieces[delta], 'px', swap_pairs(width_px, half_px, delta))]
    slice x9 -> x10, local copies, waits for them, and re-layouts: 11.9 us -> 2.35 us  [the longest x1 1.4 us: on_device(): spectra[:, :half_one + 1, 0].astype(jnp.float32)]
    another operation x0 -> x8, other arithmetic: none -> 7.15 us
    select_n x3 -> x4, other arithmetic: 7.03 us -> 0.04 us  [the longest x1 0.01 us: partners(): jnp.where(base, (first + length // 2) % length, (length - first) % length)]
    all_to_all x5 -> x4, starting transfers between devices: 26.5 us -> 20.7 us  [exchange(): return lax.all_to_all(value, ('px', 'py'), 0, 0, tiled=True)]
  transfers between devices with their start and end apart: 6 -> 16, of which waited for: 5 -> 11; matrix products, arithmetic and copies ran while one was open for 11% -> 5% of each run, Pallas kernels for 16% -> 27%
where the time goes in v2:
time: 315 us; the launch traced here: 314 us
  waiting for transfers between devices  163 us (52%)
  Pallas kernels  95.5 us (30%)
  starting transfers between devices  32.3 us (10%)
  other arithmetic  13.1 us (4%)
  local copies, waits for them, and re-layouts  10.3 us (3%)
    ppermute x6, waiting for transfers between devices, shared_rows(): lax.ppermute(pieces[delta], 'px', swap_pairs(width_px, half_px, delta))  101 us
    pallas_call x3, Pallas kernels, filter_planes(): pl.pallas_call(body, grid_spec=pltpu.PrefetchScalarGridSpec(num_scalar_pr...  42 us
    ppermute x3, waiting for transfers between devices, send_messages(): lax.ppermute(message[delta], 'px', swap_pairs(width_px, half_px, delta))  38.5 us
    all_to_all x4, starting transfers between devices, exchange(): return lax.all_to_all(value, ('px', 'py'), 0, 0, tiled=True)  20.7 us
    all_to_all x4, waiting for transfers between devices, exchange(): return lax.all_to_all(value, ('px', 'py'), 0, 0, tiled=True)  20.6 us
    pallas_call x2, Pallas kernels, backward_last(): pl.pallas_call(body, grid=(rows_one // block,), in_specs=in_specs, out_sp...  18.4 us
    pallas_call x3, Pallas kernels, forward_last(): pl.pallas_call(body, grid=(rows_one // block,), in_specs=[pl.BlockSpec((b...  16.5 us
    pallas_call x1, Pallas kernels, message_rows(): pl.pallas_call(body, grid=(1,), in_specs=[pl.BlockSpec(part, lambda i: (0...  9.41 us
  transfers between devices with their start and end apart: 16, of which 11 were waited for; matrix products, arithmetic and copies ran while one was open for 5% of the time, Pallas kernels for 27%

profile of v2, /device:TPU:21, one launch (start us, length us, event | category | flops | bytes accessed | tf_op | source)
XLA Modules:
  0.0 314.5 jit_solution(17701733075149033231)
XLA Ops:
  0.0 1.4 slice.71
  1.4 2.0 collective-permute-start
  3.4 5.5 %forward_last.4 = f32[2,64,32,128]{3,2,1,0:T(8,128)} custom-call(f32[32,128,256]{2,1,0:T(8,128)} %adjoint_ref.5, bf16[64,768]{1,0:T(8,128)(2,1)} %constant.163.clone.table_ref), custom_call_target="tpu_custom_call" | custom-call | flops 402653184 | bytes 6291456 | tf_op jit(solution)/shard_map/forward_last/pallas_call | solution.py:104
  8.9 2.8 collective-permute-done.edge_ref
  11.8 5.4 %all-to-all-start.1 = ((f32[16,8,32,128]{3,2,1,0:T(8,128)}), f32[16,8,32,128]{3,2,1,0:T(8,128)S(1)}, u32[]{:S(2)}, u32[]{:S(2)}) async-start(f32[16,8,32,128]{3,2,1,0:T(8,128)} %bitcast.22), calls=%async_computation.1 | async-start | bytes 4194304 | tf_op jit(solution)/shard_map/all_to_all | solution.py:594
  17.2 0.7 dynamic-slice_reduce_fusion
  18.0 0.7 fusion.37.select_ref
  18.7 9.4 %message_rows.1 = (f32[13,72,128]{2,1,0:T(8,128)}, f32[13,72,128]{2,1,0:T(8,128)}, f32[13,72,128]{2,1,0:T(8,128)}, f32[13,72,128]{2,1,0:T(8,128)}) custom-call(bf16[2,256,32,256]{3,2,1,0:T(8,128)(2,1)} %spectra_ref, f32[2,129,256]{2,1,0:T(8,128)} %copy-done.10, bf16[64,256]{1,0:T(8,128)(2,1)} %fusion.37.select_ref), custom_call_target="tpu_custom_call" | custom-call | flops 268435456 | bytes 6144000 | tf_op jit(solution)/shard_map/message_rows/pallas_call | solution.py:457
  28.1 1.2 collective-permute-start.1
  29.3 1.2 collective-permute-start.2
  30.5 0.3 collective-permute-start.3
  30.8 5.6 %forward_last.3 = f32[1,128,32,128]{3,2,1,0:T(8,128)} custom-call(f32[32,128,256]{2,1,0:T(8,128)} %adjoint_ref.5, bf16[128,768]{1,0:T(8,128)(2,1)} %constant.165.clone.table_ref), custom_call_target="tpu_custom_call" | custom-call | flops 805306368 | bytes 6291456 | tf_op jit(solution)/shard_map/forward_last/pallas_call | solution.py:104
  36.3 9.4 %collective-permute-done.1.refs_1_ = f32[13,72,128]{2,1,0:T(8,128)S(1)} collective-permute-done((f32[13,72,128]{2,1,0:T(8,128)}, f32[13,72,128]{2,1,0:T(8,128)S(1)}, u32[]{:S(2)}, u32[]{:S(2)}) %collective-permute-start.1) | collective-permute-done | bytes 479264 | tf_op jit(solution)/shard_map/ppermute | solution.py:375
  45.7 17.8 %collective-permute-done.2.refs_2_ = f32[13,72,128]{2,1,0:T(8,128)S(1)} collective-permute-done((f32[13,72,128]{2,1,0:T(8,128)}, f32[13,72,128]{2,1,0:T(8,128)S(1)}, u32[]{:S(2)}, u32[]{:S(2)}) %collective-permute-start.2) | collective-permute-done | bytes 479264 | tf_op jit(solution)/shard_map/ppermute | solution.py:375
  63.5 11.3 %collective-permute-done.3.refs_3_ = f32[13,72,128]{2,1,0:T(8,128)S(1)} collective-permute-done((f32[13,72,128]{2,1,0:T(8,128)}, f32[13,72,128]{2,1,0:T(8,128)S(1)}, u32[]{:S(2)}, u32[]{:S(2)}) %collective-permute-start.3) | collective-permute-done | bytes 479264 | tf_op jit(solution)/shard_map/ppermute | solution.py:375
  74.8 0.8 copy-done.19
  75.6 5.0 %all-to-all-start = ((f32[16,8,32,128]{3,2,1,0:T(8,128)}), f32[16,8,32,128]{3,2,1,0:T(8,128)}, u32[]{:S(2)}, u32[]{:S(2)}) async-start(f32[16,8,32,128]{3,2,1,0:T(8,128)} %bitcast.21), calls=%async_computation | async-start | bytes 4194304 | tf_op jit(solution)/shard_map/all_to_all | solution.py:594
  80.8 5.5 %forward_last.5 = f32[2,64,32,128]{3,2,1,0:T(8,128)} custom-call(f32[32,128,256]{2,1,0:T(8,128)} %adjoint_ref.5, bf16[64,768]{1,0:T(8,128)(2,1)} %constant.164.clone.table_ref), custom_call_target="tpu_custom_call" | custom-call | flops 402653184 | bytes 6291456 | tf_op jit(solution)/shard_map/forward_last/pallas_call | solution.py:104
  86.3 0.7 constant_dynamic-slice_fusion
  87.1 0.6 reduce-precision_convert_fusion.3
  87.7 0.7 pad_maximum_fusion.7.refs_6_
  88.4 3.4 %reduce-precision_convert_fusion = (bf16[256,256]{1,0:T(8,128)(2,1)S(1)}, bf16[256,256]{1,0:T(8,128)(2,1)S(1)}, bf16[256,256]{1,0:T(8,128)(2,1)S(1)}, bf16[256,2...) fusion(s32[256]{0:T(256)S(1)} %and_select_fusion.1, s32[256]{0:T(256)S(1)} %pad_add_fusion), kind=kLoop, calls=%fused_computation.21 | loop fusion | flops 3735552 | bytes 788480 | tf_op jit(solution)/shard_map/convert.7
  91.8 0.8 pad_maximum_fusion.6.refs_7_
  92.6 0.8 pad_maximum_fusion.4.refs_5_
  93.4 0.6 slice_bitcast_fusion
  94.0 13.2 %filter_planes.4 = (f32[2,2,8,32,128]{4,3,2,1,0:T(8,128)}, f32[2,2,8,32,128]{4,3,2,1,0:T(8,128)}, f32[2,2,8,32,128]{4,3,2,1,0:T(8,128)}, f32[2,2,8,32,128]{4,3,2,1,0:T(8,128)}) custom-call(s32[8]{0:T(128)} %get-tuple-element.120.places_ref, s32[1]{0:T(128)} %bitcast.1.special_ref, f32[8,2,8,32,128]{4,3,2,1,0:T(8,128)} %bitcast.24, ...), custom_call_target="tpu_custom_call" | custom-call | flops 3221225472 | bytes 5242880 | tf_op jit(solution)/shard_map/filter_planes/pallas_call | solution.py:205
  107.3 20.6 %all-to-all-done = f32[16,8,32,128]{3,2,1,0:T(8,128)} async-done(((f32[16,8,32,128]{3,2,1,0:T(8,128)}), f32[16,8,32,128]{3,2,1,0:T(8,128)}, u32[]{:S(2)}, u32[]{:S(2)}) %all-to-all-start) | async-done | bytes 2097184 | tf_op jit(solution)/shard_map/all_to_all | solution.py:594
  127.9 5.2 %all-to-all-start.2 = ((f32[16,8,32,128]{3,2,1,0:T(8,128)}), f32[16,8,32,128]{3,2,1,0:T(8,128)S(1)}, u32[]{:S(2)}, u32[]{:S(2)}) async-start(f32[16,8,32,128]{3,2,1,0:T(8,128)} %bitcast.9), calls=%async_computation.2 | async-start | bytes 4194304 | tf_op jit(solution)/shard_map/all_to_all | solution.py:594
  133.1 0.2 fusion.38
  133.3 0.5 convert_element_type.41.chosen_ref
  133.8 9.2 %cosine_factors.1.refs_0_ = f32[2,32,128,256]{3,2,1,0:T(8,128)} custom-call(f32[2]{0:T(128)} %convert_element_type.41.chosen_ref, f32[32,128,256]{2,1,0:T(8,128)} %saved_ref.1), custom_call_target="tpu_custom_call" | custom-call | flops 50331648 | bytes 12582912 | tf_op jit(solution)/shard_map/cosine_factors/pallas_call | solution.py:350
  142.9 1.2 collective-permute-start.4
  144.1 1.2 collective-permute-start.5
  145.3 0.3 collective-permute-start.6
  145.6 0.8 pad_maximum_fusion.5.refs_7_
  146.4 15.4 %filter_planes.3 = f32[8,2,2,8,32,128]{5,4,3,2,1,0:T(8,128)} custom-call(s32[8]{0:T(128)} %get-tuple-element.121.places_ref, s32[1]{0:T(128)} %bitcast.1.special_ref, f32[8,2,8,32,128]{4,3,2,1,0:T(8,128)} %bitcast.5.planes_ref, f32[13,72,128]{2,1,0:T(8,128)} %get-tuple-element.56.refs_0_, f32[13,72,128]{2,1,0:T(8,128)} %copy-done.17, ...), custom_call_target="tpu_custom_call" | custom-call | flops 4831838208 | bytes 7340032 | tf_op jit(solution)/shard_map/filter_planes/pallas_call | solution.py:205
  161.8 3.5 %collective-permute-done.4 = f32[2,2,8,32,128]{4,3,2,1,0:T(8,128)S(1)} collective-permute-done((f32[2,2,8,32,128]{4,3,2,1,0:T(8,128)S(1)}, f32[2,2,8,32,128]{4,3,2,1,0:T(8,128)S(1)}, u32[]{:S(2)}, u32[]{:S(2)}) %collective-permute-start.4) | collective-permute-done | bytes 524320 | tf_op jit(solution)/shard_map/ppermute | solution.py:654
  165.2 15.1 %collective-permute-done.5 = f32[2,2,8,32,128]{4,3,2,1,0:T(8,128)S(1)} collective-permute-done((f32[2,2,8,32,128]{4,3,2,1,0:T(8,128)S(1)}, f32[2,2,8,32,128]{4,3,2,1,0:T(8,128)S(1)}, u32[]{:S(2)}, u32[]{:S(2)}) %collective-permute-start.5) | collective-permute-done | bytes 524320 | tf_op jit(solution)/shard_map/ppermute | solution.py:654
  180.3 12.4 %collective-permute-done.6 = f32[2,2,8,32,128]{4,3,2,1,0:T(8,128)S(1)} collective-permute-done((f32[2,2,8,32,128]{4,3,2,1,0:T(8,128)S(1)}, f32[2,2,8,32,128]{4,3,2,1,0:T(8,128)S(1)}, u32[]{:S(2)}, u32[]{:S(2)}) %collective-permute-start.6) | collective-permute-done | bytes 524320 | tf_op jit(solution)/shard_map/ppermute | solution.py:654
  192.7 0.8 copy-done.8
  193.5 1.3 copy-done.1
  194.8 5.1 %all-to-all-start.3 = ((f32[16,2,8,32,128]{4,3,2,1,0:T(8,128)}), f32[16,2,8,32,128]{4,3,2,1,0:T(8,128)}, u32[]{:S(2)}, u32[]{:S(2)}) async-start(f32[16,2,8,32,128]{4,3,2,1,0:T(8,128)} %bitcast.23), calls=%async_computation.3 | async-start | bytes 8388608 | tf_op jit(solution)/shard_map/all_to_all | solution.py:594
  200.0 13.4 %filter_planes.5 = (f32[2,2,8,32,128]{4,3,2,1,0:T(8,128)}, f32[2,2,8,32,128]{4,3,2,1,0:T(8,128)}, f32[2,2,8,32,128]{4,3,2,1,0:T(8,128)}, f32[2,2,8,32,128]{4,3,2,1,0:T(8,128)}) custom-call(s32[8]{0:T(128)} %get-tuple-element.119.places_ref, s32[1]{0:T(128)} %bitcast.1.special_ref, f32[8,2,8,32,128]{4,3,2,1,0:T(8,128)} %bitcast.25, ...), custom_call_target="tpu_custom_call" | custom-call | flops 3221225472 | bytes 5242880 | tf_op jit(solution)/shard_map/filter_planes/pallas_call | solution.py:205
  213.7 0.4 collective-permute-start.10
  214.3 0.6 gather_fusion.1
  214.9 1.2 collective-permute-start.7
  216.1 1.2 collective-permute-start.8
  217.3 0.2 collective-permute-start.9
  217.6 0.3 reduce-precision_convert_fusion.4
  217.9 0.6 pad_maximum_fusion.9.refs_1_
  218.6 1.1 pad_maximum_fusion.refs_2_
  219.7 1.0 copy-done.2
  220.7 7.8 %backward_last.2.refs_6_ = f32[32,128,256]{2,1,0:T(8,128)} custom-call(f32[2,32,128,256]{3,2,1,0:T(8,128)} %cosine_factors.1.refs_0_, bf16[192,256]{1,0:T(8,128)(2,1)} %pad_maximum_fusion.9.refs_1_, f32[4,2,8,32,128]{4,3,2,1,0:T(8,128)} %pad_maximum_fusion.refs_2_, f32[4,2,8,32,128]{4,3,2,1,0:T(8,128)} %copy-done.2), custom_call_target="tpu_custom_call" | custom-call | flops 805306368 | bytes 18874368 | tf_op jit(solution)/shard_map/backward_last/pallas_call | solution.py:308
  228.5 11.3 %collective-permute-done.7 = f32[2,2,8,32,128]{4,3,2,1,0:T(8,128)S(1)} collective-permute-done((f32[2,2,8,32,128]{4,3,2,1,0:T(8,128)}, f32[2,2,8,32,128]{4,3,2,1,0:T(8,128)S(1)}, u32[]{:S(2)}, u32[]{:S(2)}) %collective-permute-start.7) | collective-permute-done | bytes 524320 | tf_op jit(solution)/shard_map/ppermute | solution.py:654
  239.8 41.3 %collective-permute-done.8 = f32[2,2,8,32,128]{4,3,2,1,0:T(8,128)S(1)} collective-permute-done((f32[2,2,8,32,128]{4,3,2,1,0:T(8,128)}, f32[2,2,8,32,128]{4,3,2,1,0:T(8,128)S(1)}, u32[]{:S(2)}, u32[]{:S(2)}) %collective-permute-start.8) | collective-permute-done | bytes 524320 | tf_op jit(solution)/shard_map/ppermute | solution.py:654
  281.0 17.5 %collective-permute-done.9 = f32[2,2,8,32,128]{4,3,2,1,0:T(8,128)S(1)} collective-permute-done((f32[2,2,8,32,128]{4,3,2,1,0:T(8,128)}, f32[2,2,8,32,128]{4,3,2,1,0:T(8,128)S(1)}, u32[]{:S(2)}, u32[]{:S(2)}) %collective-permute-start.9) | collective-permute-done | bytes 524320 | tf_op jit(solution)/shard_map/ppermute | solution.py:654
  298.8 0.1 pad_maximum_fusion.3
  298.9 1.2 collective-permute-start.11
  300.1 0.6 gather_fusion
  300.7 0.4 reduce-precision_convert_fusion.5
  301.1 0.7 pad_maximum_fusion.8.refs_1_
  301.8 1.1 pad_maximum_fusion.2.refs_3_
  302.9 1.0 copy-done.3
  303.8 10.6 %backward_last.3 = f32[32,128,256]{2,1,0:T(8,128)} custom-call(f32[2,32,128,256]{3,2,1,0:T(8,128)} %cosine_factors.1.refs_0_, bf16[192,256]{1,0:T(8,128)(2,1)} %pad_maximum_fusion.8.refs_1_, bf16[384,256]{1,0:T(8,128)(2,1)} %constant.171.clone.refs_2_, f32[4,2,8,32,128]{4,3,2,1,0:T(8,128)} %pad_maximum_fusion.2.refs_3_, f32[4,2,8,32,128]{4,3,2,1,0:T(8,128)} %copy-done.3, ...), custom_call_target="tpu_custom_call" | custom-call | flops 2415919104 | bytes 23068672 | tf_op jit(solution)/shard_map/backward_last/pallas_call | solution.py:308
  (70 shorter events, 1.2 us)
Async XLA Ops:
  1.4 10.3 %collective-permute-start = (f32[2,129,256]{2,1,0:T(8,128)S(1)}, f32[2,129,256]{2,1,0:T(8,128)S(1)}, u32[]{:S(2)}, u32[]{:S(2)}) collective-permute-start(f32[2,129,256]{2,1,0:T(8,128)S(1)} %fusion.18), channel_id=1, source_target_pairs={{0,8},{8,0},{1,9},{9,1},{16,24},{24,16},{17,25},{25,17}} | collective-permute-start | bytes 792584 | tf_op jit(solution)/shard_map/ppermute | solution.py:576
  11.8 7.0 %copy-start.10 = (f32[2,129,256]{2,1,0:T(8,128)}, f32[2,129,256]{2,1,0:T(8,128)S(1)}, u32[]{:S(2)}) copy-start(f32[2,129,256]{2,1,0:T(8,128)S(1)} %collective-permute-done.edge_ref) | copy-start | bytes 792580
  11.8 63.8 %all-to-all-start.1 = ((f32[16,8,32,128]{3,2,1,0:T(8,128)}), f32[16,8,32,128]{3,2,1,0:T(8,128)S(1)}, u32[]{:S(2)}, u32[]{:S(2)}) async-start(f32[16,8,32,128]{3,2,1,0:T(8,128)} %bitcast.22), calls=%async_computation.1 | async-start | bytes 4194304 | tf_op jit(solution)/shard_map/all_to_all | solution.py:594
  28.1 17.6 %collective-permute-start.1 = (f32[13,72,128]{2,1,0:T(8,128)}, f32[13,72,128]{2,1,0:T(8,128)S(1)}, u32[]{:S(2)}, u32[]{:S(2)}) collective-permute-start(f32[13,72,128]{2,1,0:T(8,128)} %get-tuple-element.52), channel_id=1, source_target_pairs={{0,2},{2,0},{4,6},{6,4},{8,10},{10,8},{12,14},{14,12},{1,3},{3,1},... | collective-permute-start | bytes 1437704 | tf_op jit(solution)/shard_map/ppermute | solution.py:375
  29.3 34.2 %collective-permute-start.2 = (f32[13,72,128]{2,1,0:T(8,128)}, f32[13,72,128]{2,1,0:T(8,128)S(1)}, u32[]{:S(2)}, u32[]{:S(2)}) collective-permute-start(f32[13,72,128]{2,1,0:T(8,128)} %get-tuple-element.53), channel_id=1, source_target_pairs={{0,4},{2,6},{4,0},{6,2},{8,12},{10,14},{12,8},{14,10},{1,5},{3,7},... | collective-permute-start | bytes 1437704 | tf_op jit(solution)/shard_map/ppermute | solution.py:375
  30.5 44.3 %collective-permute-start.3 = (f32[13,72,128]{2,1,0:T(8,128)}, f32[13,72,128]{2,1,0:T(8,128)S(1)}, u32[]{:S(2)}, u32[]{:S(2)}) collective-permute-start(f32[13,72,128]{2,1,0:T(8,128)} %get-tuple-element.54), channel_id=1, source_target_pairs={{0,6},{2,4},{4,2},{6,0},{8,14},{10,12},{12,10},{14,8},{1,7},{3,5},... | collective-permute-start | bytes 1437704 | tf_op jit(solution)/shard_map/ppermute | solution.py:375
  45.7 40.6 %copy-start.17 = (f32[13,72,128]{2,1,0:T(8,128)}, f32[13,72,128]{2,1,0:T(8,128)S(1)}, u32[]{:S(2)}) copy-start(f32[13,72,128]{2,1,0:T(8,128)S(1)} %collective-permute-done.1.refs_1_) | copy-start | bytes 1437700
  63.5 22.8 %copy-start.18 = (f32[13,72,128]{2,1,0:T(8,128)}, f32[13,72,128]{2,1,0:T(8,128)S(1)}, u32[]{:S(2)}) copy-start(f32[13,72,128]{2,1,0:T(8,128)S(1)} %collective-permute-done.2.refs_2_) | copy-start | bytes 1437700
  74.8 0.8 copy-start.19
  75.6 10.7 %copy-start = (f32[16,8,32,128]{3,2,1,0:T(8,128)}, f32[16,8,32,128]{3,2,1,0:T(8,128)S(1)}, u32[]{:S(2)}) copy-start(f32[16,8,32,128]{3,2,1,0:T(8,128)S(1)} %all-to-all-done.1) | copy-start | bytes 6291460
  75.6 52.3 %all-to-all-start = ((f32[16,8,32,128]{3,2,1,0:T(8,128)}), f32[16,8,32,128]{3,2,1,0:T(8,128)}, u32[]{:S(2)}, u32[]{:S(2)}) async-start(f32[16,8,32,128]{3,2,1,0:T(8,128)} %bitcast.21), calls=%async_computation | async-start | bytes 4194304 | tf_op jit(solution)/shard_map/all_to_all | solution.py:594
  80.6 6.4 %copy-start.13 = (s32[256]{0:T(256)S(1)}, s32[256]{0:T(256)}, u32[]{:S(2)}) copy-start(s32[256]{0:T(256)} %constant.170.clone) | copy-start | bytes 3076
  107.3 25.8 %copy-start.20 = (s32[8]{0:T(128)S(1)}, s32[8]{0:T(128)}, u32[]{:S(2)}) copy-start(s32[8]{0:T(128)} %param.19) | copy-start | bytes 100
  107.3 25.8 %copy-start.21 = (s32[2]{0:T(128)S(1)}, s32[2]{0:T(128)}, u32[]{:S(2)}) copy-start(s32[2]{0:T(128)} %param.20) | copy-start | bytes 28
  127.9 65.7 %all-to-all-start.2 = ((f32[16,8,32,128]{3,2,1,0:T(8,128)}), f32[16,8,32,128]{3,2,1,0:T(8,128)S(1)}, u32[]{:S(2)}, u32[]{:S(2)}) async-start(f32[16,8,32,128]{3,2,1,0:T(8,128)} %bitcast.9), calls=%async_computation.2 | async-start | bytes 4194304 | tf_op jit(solution)/shard_map/all_to_all | solution.py:594
  133.8 9.2 %copy-start.16 = (f32[2,2,8,32,128]{4,3,2,1,0:T(8,128)S(1)}, f32[2,2,8,32,128]{4,3,2,1,0:T(8,128)}, u32[]{:S(2)}) copy-start(f32[2,2,8,32,128]{4,3,2,1,0:T(8,128)} %get-tuple-element.66) | copy-start | bytes 1572868
  133.8 10.4 %copy-start.15 = (f32[2,2,8,32,128]{4,3,2,1,0:T(8,128)S(1)}, f32[2,2,8,32,128]{4,3,2,1,0:T(8,128)}, u32[]{:S(2)}) copy-start(f32[2,2,8,32,128]{4,3,2,1,0:T(8,128)} %get-tuple-element.67) | copy-start | bytes 1572868
  133.8 11.5 %copy-start.14 = (f32[2,2,8,32,128]{4,3,2,1,0:T(8,128)S(1)}, f32[2,2,8,32,128]{4,3,2,1,0:T(8,128)}, u32[]{:S(2)}) copy-start(f32[2,2,8,32,128]{4,3,2,1,0:T(8,128)} %get-tuple-element.68) | copy-start | bytes 1572868
  142.9 22.3 %collective-permute-start.4 = (f32[2,2,8,32,128]{4,3,2,1,0:T(8,128)S(1)}, f32[2,2,8,32,128]{4,3,2,1,0:T(8,128)S(1)}, u32[]{:S(2)}, u32[]{:S(2)}) collective-permute-start(f32[2,2,8,32,128]{4,3,2,1,0:T(8,128)S(1)} %copy-done.16), channel_id=1, source_target_pairs={{0,2},{2,0},{4,6},{6,4},{8,10},{10,8},{12,14},{14,12},{1,3},{3,1},... | collective-permute-start | bytes 1572872 | tf_op jit(solution)/shard_map/ppermute | solution.py:654
  144.1 36.2 %collective-permute-start.5 = (f32[2,2,8,32,128]{4,3,2,1,0:T(8,128)S(1)}, f32[2,2,8,32,128]{4,3,2,1,0:T(8,128)S(1)}, u32[]{:S(2)}, u32[]{:S(2)}) collective-permute-start(f32[2,2,8,32,128]{4,3,2,1,0:T(8,128)S(1)} %copy-done.15), channel_id=1, source_target_pairs={{0,4},{2,6},{4,0},{6,2},{8,12},{10,14},{12,8},{14,10},{1,5},{3,7},... | collective-permute-start | bytes 1572872 | tf_op jit(solution)/shard_map/ppermute | solution.py:654
  145.3 47.4 %collective-permute-start.6 = (f32[2,2,8,32,128]{4,3,2,1,0:T(8,128)S(1)}, f32[2,2,8,32,128]{4,3,2,1,0:T(8,128)S(1)}, u32[]{:S(2)}, u32[]{:S(2)}) collective-permute-start(f32[2,2,8,32,128]{4,3,2,1,0:T(8,128)S(1)} %copy-done.14), channel_id=1, source_target_pairs={{0,6},{2,4},{4,2},{6,0},{8,14},{10,12},{12,10},{14,8},{1,7},{3,5},... | collective-permute-start | bytes 1572872 | tf_op jit(solution)/shard_map/ppermute | solution.py:654
  180.3 13.2 %copy-start.6 = (f32[2,2,8,32,128]{4,3,2,1,0:T(8,128)}, f32[2,2,8,32,128]{4,3,2,1,0:T(8,128)S(1)}, u32[]{:S(2)}) copy-start(f32[2,2,8,32,128]{4,3,2,1,0:T(8,128)S(1)} %collective-permute-done.5) | copy-start | bytes 1572868
  192.7 0.8 copy-start.8
  193.5 1.3 copy-start.1
  194.8 108.0 %all-to-all-start.3 = ((f32[16,2,8,32,128]{4,3,2,1,0:T(8,128)}), f32[16,2,8,32,128]{4,3,2,1,0:T(8,128)}, u32[]{:S(2)}, u32[]{:S(2)}) async-start(f32[16,2,8,32,128]{4,3,2,1,0:T(8,128)} %bitcast.23), calls=%async_computation.3 | async-start | bytes 8388608 | tf_op jit(solution)/shard_map/all_to_all | solution.py:594
  199.9 13.4 %copy-start.5 = (f32[2,2,8,32,128]{4,3,2,1,0:T(8,128)S(1)}, f32[2,2,8,32,128]{4,3,2,1,0:T(8,128)}, u32[]{:S(2)}) copy-start(f32[2,2,8,32,128]{4,3,2,1,0:T(8,128)} %get-tuple-element.83) | copy-start | bytes 1572868
  199.9 13.5 %copy-start.7 = (f32[2,2,8,32,128]{4,3,2,1,0:T(8,128)S(1)}, f32[2,2,8,32,128]{4,3,2,1,0:T(8,128)}, u32[]{:S(2)}) copy-start(f32[2,2,8,32,128]{4,3,2,1,0:T(8,128)} %copy-done.6) | copy-start | bytes 1572868
  200.0 13.5 %copy-start.9 = (f32[2,2,8,32,128]{4,3,2,1,0:T(8,128)S(1)}, f32[2,2,8,32,128]{4,3,2,1,0:T(8,128)}, u32[]{:S(2)}) copy-start(f32[2,2,8,32,128]{4,3,2,1,0:T(8,128)} %copy-done.8) | copy-start | bytes 1572868
  213.3 1.0 copy-start.12
  213.7 6.0 %collective-permute-start.10 = (f32[4,2,8,32,128]{4,3,2,1,0:T(8,128)S(1)}, f32[4,2,8,32,128]{4,3,2,1,0:T(8,128)S(1)}, u32[]{:S(2)}, u32[]{:S(2)}) collective-permute-start(f32[4,2,8,32,128]{4,3,2,1,0:T(8,128)S(1)} %pad_maximum_fusion.1), channel_id=1, source_target_pairs={{0,1},{1,0},{2,3},{3,2},{4,5},{5,4},{6,7},{7,6},{8,9},{9,8},{10,11... | collective-permute-start | bytes 3145736 | tf_op jit(solution)/shard_map/ppermute | solution.py:663
  214.9 24.9 %collective-permute-start.7 = (f32[2,2,8,32,128]{4,3,2,1,0:T(8,128)}, f32[2,2,8,32,128]{4,3,2,1,0:T(8,128)S(1)}, u32[]{:S(2)}, u32[]{:S(2)}) collective-permute-start(f32[2,2,8,32,128]{4,3,2,1,0:T(8,128)} %get-tuple-element.80), channel_id=1, source_target_pairs={{0,2},{2,0},{4,6},{6,4},{8,10},{10,8},{12,14},{14,12},{1,3},{3,1},... | collective-permute-start | bytes 1572872 | tf_op jit(solution)/shard_map/ppermute | solution.py:654
  216.1 64.9 %collective-permute-start.8 = (f32[2,2,8,32,128]{4,3,2,1,0:T(8,128)}, f32[2,2,8,32,128]{4,3,2,1,0:T(8,128)S(1)}, u32[]{:S(2)}, u32[]{:S(2)}) collective-permute-start(f32[2,2,8,32,128]{4,3,2,1,0:T(8,128)} %get-tuple-element.81), channel_id=1, source_target_pairs={{0,4},{2,6},{4,0},{6,2},{8,12},{10,14},{12,8},{14,10},{1,5},{3,7},... | collective-permute-start | bytes 1572872 | tf_op jit(solution)/shard_map/ppermute | solution.py:654
  217.3 81.2 %collective-permute-start.9 = (f32[2,2,8,32,128]{4,3,2,1,0:T(8,128)}, f32[2,2,8,32,128]{4,3,2,1,0:T(8,128)S(1)}, u32[]{:S(2)}, u32[]{:S(2)}) collective-permute-start(f32[2,2,8,32,128]{4,3,2,1,0:T(8,128)} %get-tuple-element.82), channel_id=1, source_target_pairs={{0,6},{2,4},{4,2},{6,0},{8,14},{10,12},{12,10},{14,8},{1,7},{3,5},... | collective-permute-start | bytes 1572872 | tf_op jit(solution)/shard_map/ppermute | solution.py:654
  219.7 78.9 %copy-start.4 = (f32[2,2,8,32,128]{4,3,2,1,0:T(8,128)S(1)}, f32[2,2,8,32,128]{4,3,2,1,0:T(8,128)}, u32[]{:S(2)}) copy-start(f32[2,2,8,32,128]{4,3,2,1,0:T(8,128)} %get-tuple-element.87) | copy-start | bytes 1572868
  219.7 1.0 copy-start.2
  228.5 71.7 %copy-start.11 = (s32[8,8]{1,0:T(8,128)S(1)}, s32[8,8]{1,0:T(8,128)}, u32[]{:S(2)}) copy-start(s32[8,8]{1,0:T(8,128)} %constant.173.clone) | copy-start | bytes 772
  298.9 4.0 %collective-permute-start.11 = (f32[4,2,8,32,128]{4,3,2,1,0:T(8,128)S(1)}, f32[4,2,8,32,128]{4,3,2,1,0:T(8,128)S(1)}, u32[]{:S(2)}, u32[]{:S(2)}) collective-permute-start(f32[4,2,8,32,128]{4,3,2,1,0:T(8,128)S(1)} %pad_maximum_fusion.3), channel_id=1, source_target_pairs={{0,1},{1,0},{2,3},{3,2},{4,5},{5,4},{6,7},{7,6},{8,9},{9,8},{10,11... | collective-permute-start | bytes 3145736 | tf_op jit(solution)/shard_map/ppermute | solution.py:663
  302.9 1.0 copy-start.3

commit v3 on v2

--- a/solution.py
+++ b/solution.py
@@ -78,13 +78,13 @@
     return pltpu.CompilerParams(vmem_limit_bytes=VMEM_BYTES)
 
 
-def forward_last(adjoint, table, copies):
+def forward_last(adjoint, table, depth, copies):
     rows_one, rows_two, length = adjoint.shape
     count = table.shape[0]
     block = min(8, rows_one)
 
     def body(adjoint_ref, table_ref, out_ref):
-        flat = out_ref.reshape(copies * count * block, rows_two)
+        flat = out_ref.reshape(depth * block, rows_two)
         for start in range(0, block, 2):
             value = adjoint_ref[start : start + 2].reshape(2 * rows_two, length)
             high, low = split_value(value)
@@ -96,10 +96,12 @@
                 preferred_element_type=jnp.float32,
             )
             for inner in range(2):
-                piece = result[:, inner * rows_two : (inner + 1) * rows_two]
-                for copy in range(copies):
-                    first = copy * count * block + start + inner
-                    flat[pl.ds(first, count, stride=block), :] = piece
+                columns = slice(inner * rows_two, (inner + 1) * rows_two)
+                for row, rows, planes in copies:
+                    for plane in planes:
+                        flat[
+                            pl.ds(plane * block + start + inner, rows, stride=block), :
+                        ] = result[row : row + rows, columns]
 
     return pl.pallas_call(
         body,
@@ -108,12 +110,12 @@
             pl.BlockSpec((block, rows_two, length), lambda i: (i, 0, 0)),
             pl.BlockSpec(table.shape, lambda i: (0, 0)),
         ],
-        out_specs=pl.BlockSpec((copies, count, block, rows_two), lambda i: (0, 0, i, 0)),
-        out_shape=jax.ShapeDtypeStruct((copies, count, rows_one, rows_two), jnp.float32),
+        out_specs=pl.BlockSpec((depth, block, rows_two), lambda i: (0, i, 0)),
+        out_shape=jax.ShapeDtypeStruct((depth, rows_one, rows_two), jnp.float32),
         compiler_params=params(),
         cost_estimate=pl.CostEstimate(
             flops=6 * count * rows_one * rows_two * length,
-            bytes_accessed=4 * rows_one * rows_two * (length + copies * count),
+            bytes_accessed=4 * rows_one * rows_two * (length + depth),
             transcendentals=0,
         ),
         name="forward_last",
@@ -146,8 +148,9 @@
     )
 
 
-def filter_planes(planes, messages, places, special, tables, slots, split):
-    width_px, width_py, planes_count, rows_one, rows_two = planes.shape
+def filter_planes(planes, first, messages, places, special, tables, slots, split):
+    width_px, width_py, _, rows_one, rows_two = planes.shape
+    planes_count = places.shape[0]
     length_one = width_px * rows_one
     length_two = width_py * rows_two
     out_px = tables[2].shape[0] // rows_one
@@ -210,7 +213,7 @@
             in_specs=[
                 pl.BlockSpec(
                     (width_px, width_py, 1, rows_one, rows_two),
-                    lambda i, *_: (0, 0, i, 0, 0),
+                    lambda i, *_: (0, 0, first + i, 0, 0),
                 )
             ]
             + [
@@ -565,12 +568,15 @@
     single = order[shared_chunks * shared_count :].reshape(devices, -1)
     depth = single.shape[1]
     owned = [np.concatenate([chunk, chunk]) for chunk in shared] + [single]
-    folded = np.concatenate(owned, axis=1)
-    folded = np.minimum(folded, length_three - folded)
-    distinct = [list(dict.fromkeys(row.tolist())) for row in folded]
-    count = max(len(row) for row in distinct)
-    wanted = np.array([row + [row[-1]] * (count - len(row)) for row in distinct])
-    places = np.array([[row.index(k) for k in ks] for row, ks in zip(distinct, folded)])
+
+    def folded_rows(members):
+        folded = np.concatenate(members, axis=1)
+        folded = np.minimum(folded, length_three - folded)
+        distinct = [list(dict.fromkeys(row.tolist())) for row in folded]
+        count = max(len(row) for row in distinct)
+        wanted = np.array([row + [row[-1]] * (count - len(row)) for row in distinct])
+        places = [[row.index(k) for k in ks] for row, ks in zip(distinct, folded)]
+        return wanted, np.array(places)
 
     half_one = length_one // 2
     edge = lax.ppermute(
@@ -579,16 +585,25 @@
         [(0, half_px), (half_px, 0)],
     )
     last = hartley(length_three)
-    sent_shared = []
-    for chunk in shared:
-        sent_shared.append(
-            forward_last(adjoint, left_table(last[chunk.reshape(-1)]), 2).reshape(
-                devices, shared_depth, rows_one, rows_two
-            )
+
+    def send(value, runs):
+        depth = sum(run.shape[1] for run in runs)
+        table = left_table(last[np.concatenate([run.reshape(-1) for run in runs])])
+        copies = []
+        row = 0
+        place = 0
+        for run in runs:
+            for owner in range(run.shape[0]):
+                owners = range(owner, devices, run.shape[0])
+                planes = [target * depth + place for target in owners]
+                copies.append((row, run.shape[1], planes))
+                row += run.shape[1]
+            place += run.shape[1]
+        return forward_last(value, table, devices * depth, copies).reshape(
+            devices, depth, rows_one, rows_two
         )
-    sent_single = forward_last(adjoint, left_table(last[single.reshape(-1)]), 1).reshape(
-        devices, depth, rows_one, rows_two
-    )
+
+    sent = send(adjoint, shared[:1] + [single])
 
     def exchange(value):
         return lax.all_to_all(value, ("px", "py"), 0, 0, tiled=True)
@@ -596,15 +611,13 @@
     def arranged(value):
         return value.reshape(width_px, width_py, -1, rows_one, rows_two)
 
-    if shared_chunks:
-        sent_shared[0], spectra, edge = lax.optimization_barrier(
-            (sent_shared[0], spectra, edge)
-        )
+    barrier = lax.optimization_barrier
+    device = px_index * width_py + py_index
+    sent, spectra, edge, adjoint = barrier((sent, spectra, edge, adjoint))
+    wanted, places = folded_rows(owned)
     messages = kernel_messages(spectra, edge, wanted, width_px, width_py)
     messages = send_messages(messages, width_px)
-    if shared_chunks:
-        sent_single, messages = lax.optimization_barrier((sent_single, messages))
-    places = jnp.asarray(places, dtype=jnp.int32)[px_index * width_py + py_index]
+    places = jnp.asarray(places, dtype=jnp.int32)[device]
     local_two = length_two // width_px
     special = (px_low * local_two).astype(jnp.int32).reshape(1)
 
@@ -641,6 +654,7 @@
         first = index * shared_depth
         return filter_planes(
             arranged(value),
+            0,
             messages,
             places[first : first + shared_depth],
             special,
@@ -661,39 +675,46 @@
             pairs = [(c, (c + shift) % width_py) for c in range(width_py)]
             far = jnp.stack([piece[shift] for piece in pieces])
             parts.append(lax.ppermute(far, "py", pairs))
-        ids = jnp.asarray(shared[index])[shared_source].reshape(-1)
-        return parts, traced_table(ids, jnp.arange(length_three), length_three, 0)
-
-    barrier = lax.optimization_barrier
-    factors = cosine_factors(saved, chosen, 1.0 / (length_one * length_two * length_three))
+        return parts, shared_tables[index]
+
+    shared_tables = []
+    for chunk in shared:
+        ids = jnp.asarray(chunk)[shared_source].reshape(-1)
+        shared_tables.append(
+            traced_table(ids, jnp.arange(length_three), length_three, 0)
+        )
+    scale = 1.0 / (length_one * length_two * length_three)
     single_table = right_table(last[single.reshape(-1)])
     first = shared_chunks * shared_depth
 
     def single_fields(value):
         return filter_planes(
             arranged(value),
+            min(first, shared_depth),
             messages,
-            places[first : first + depth],
+            places[first:],
             special,
             tables,
             slots,
             False,
         ).reshape(devices, slots, depth, rows_one, rows_two)
 
+    factors = cosine_factors(saved, chosen, scale)
     if shared_chunks == 0:
-        returned = exchange(single_fields(exchange(sent_single)))
+        returned = exchange(single_fields(exchange(sent)))
         return backward_last([([returned], single_table)], factors, None)
 
-    arrived = exchange(sent_shared[0])
-    arrived_single = exchange(sent_single)
-    pieces = shared_fields(0, arrived)
-    pieces, sent_shared[1] = barrier((pieces, sent_shared[1]))
-    near = shared_rows(pieces)
-    arrived = exchange(sent_shared[1])
-    fields_single = single_fields(arrived_single)
-    fields_single, factors, near = barrier((fields_single, factors, near))
+    arrived = exchange(sent)
+    sent = send(adjoint, shared[1:])
+    sent, messages, places, tables, half_tables, shared_tables, factors = barrier(
+        (sent, messages, places, tables, half_tables, shared_tables, factors)
+    )
+    arrived_late = exchange(sent)
+    near = shared_rows(shared_fields(0, arrived))
+    fields_single = single_fields(arrived)
+    fields_single, near = barrier((fields_single, near))
     returned = exchange(fields_single)
-    pieces = shared_fields(1, arrived)
+    pieces = shared_fields(1, arrived_late)
     pieces, near = barrier((pieces, near))
     group = shared_group(0, near)
     late = shared_rows(pieces)

time: 315 us -> 302 us (0.959)
  Pallas kernels: 95.5 us -> 90.5 us
  starting transfers between devices: 32.3 us -> 27.6 us
  waiting for transfers between devices: 163 us -> 159 us
    all_to_all x4 -> x3, waiting for transfers between devices: 20.6 us -> 1.37 us  [exchange(): return lax.all_to_all(value, ('px', 'py'), 0, 0, tiled=True)]
    ppermute x3, waiting for transfers between devices: 38.5 us -> 54.9 us  [send_messages(): lax.ppermute(message[delta], 'px', swap_pairs(width_px, half_px, delta))]
    pallas_call x3 -> x2, Pallas kernels: 16.5 us -> 11.6 us  [forward_last(): pl.pallas_call(body, grid=(rows_one // block,), in_specs=[pl.BlockSpec((b...]
    all_to_all x4 -> x3, starting transfers between devices: 20.7 us -> 16 us  [exchange(): return lax.all_to_all(value, ('px', 'py'), 0, 0, tiled=True)]
  transfers between devices with their start and end apart: 16 -> 15, of which waited for: 11 -> 12; matrix products, arithmetic and copies ran while one was open for 5% -> 6% of each run, Pallas kernels for 27% -> 27%
where the time goes in v3:
time: 302 us; the launch traced here: 301 us
  waiting for transfers between devices  159 us (53%)
  Pallas kernels  90.5 us (30%)
  starting transfers between devices  27.6 us (9%)
  other arithmetic  13 us (4%)
  local copies, waits for them, and re-layouts  10.5 us (3%)
    ppermute x6, waiting for transfers between devices, shared_rows(): lax.ppermute(pieces[delta], 'px', swap_pairs(width_px, half_px, delta))  99.3 us
    ppermute x3, waiting for transfers between devices, send_messages(): lax.ppermute(message[delta], 'px', swap_pairs(width_px, half_px, delta))  54.9 us
    pallas_call x3, Pallas kernels, filter_planes(): pl.pallas_call(body, grid_spec=pltpu.PrefetchScalarGridSpec(num_scalar_pr...  42 us
    pallas_call x2, Pallas kernels, backward_last(): pl.pallas_call(body, grid=(rows_one // block,), in_specs=in_specs, out_sp...  18.4 us
    all_to_all x3, starting transfers between devices, exchange(): return lax.all_to_all(value, ('px', 'py'), 0, 0, tiled=True)  16 us
    pallas_call x2, Pallas kernels, forward_last(): pl.pallas_call(body, grid=(rows_one // block,), in_specs=[pl.BlockSpec((b...  11.6 us
    pallas_call x1, Pallas kernels, message_rows(): pl.pallas_call(body, grid=(1,), in_specs=[pl.BlockSpec(part, lambda i: (0...  9.42 us
    pallas_call x1, Pallas kernels, cosine_factors(): pl.pallas_call(body, grid=(rows_one // block,), in_specs=[pl.BlockSpec(me...  9.06 us
  transfers between devices with their start and end apart: 15, of which 12 were waited for; matrix products, arithmetic and copies ran while one was open for 6% of the time, Pallas kernels for 27%

profile of v3, /device:TPU:21, one launch (start us, length us, event | category | flops | bytes accessed | tf_op | source)
XLA Modules:
  0.0 301.0 jit_solution(9865563331870130740)
XLA Ops:
  0.0 1.4 slice.60
  1.4 2.0 collective-permute-start
  3.4 6.1 %forward_last.2 = f32[256,32,128]{2,1,0:T(8,128)} custom-call(f32[32,128,256]{2,1,0:T(8,128)} %adjoint_ref.2, bf16[192,768]{1,0:T(8,128)(2,1)} %constant.161.clone.table_ref), custom_call_target="tpu_custom_call" | custom-call | flops 1207959552 | bytes 8388608 | tf_op jit(solution)/shard_map/forward_last/pallas_call | solution.py:106
  9.5 2.3 collective-permute-done.edge_ref
  11.8 0.7 copy-done.7
  12.4 5.9 %all-to-all-start.1 = ((f32[16,16,32,128]{3,2,1,0:T(8,128)}), f32[16,16,32,128]{3,2,1,0:T(8,128)}, u32[]{:S(2)}, u32[]{:S(2)}) async-start(f32[16,16,32,128]{3,2,1,0:T(8,128)} %bitcast.15), calls=%async_computation.1 | async-start | bytes 8388608 | tf_op jit(solution)/shard_map/all_to_all | solution.py:609
  18.5 0.2 fusion.38
  18.7 0.6 convert_element_type.45.chosen_ref
  19.3 0.7 dynamic-slice_reduce_fusion
  20.1 0.1 eq.55
  20.3 0.6 gather_fusion.1
  21.0 0.6 gather_fusion
  21.6 9.1 %cosine_factors.1.refs_0_ = f32[2,32,128,256]{3,2,1,0:T(8,128)} custom-call(f32[2]{0:T(128)} %convert_element_type.45.chosen_ref, f32[32,128,256]{2,1,0:T(8,128)} %saved_ref.1), custom_call_target="tpu_custom_call" | custom-call | flops 50331648 | bytes 12582912 | tf_op jit(solution)/shard_map/cosine_factors/pallas_call | solution.py:353
  30.7 0.3 reduce-precision_convert_fusion.5
  31.1 0.7 pad_maximum_fusion.8.refs_1_
  31.7 0.3 reduce-precision_convert_fusion.4
  32.1 0.7 pad_maximum_fusion.9.refs_1_
  32.8 0.6 reduce-precision_convert_fusion.3
  33.4 0.7 pad_maximum_fusion.7.refs_6_
  34.1 0.7 fusion.37.select_ref
  34.7 3.4 %reduce-precision_convert_fusion = (bf16[256,256]{1,0:T(8,128)(2,1)S(1)}, bf16[256,256]{1,0:T(8,128)(2,1)S(1)}, bf16[256,256]{1,0:T(8,128)(2,1)S(1)}, bf16[256,2...) fusion(s32[256]{0:T(256)S(1)} %and_select_fusion.1, s32[256]{0:T(256)S(1)} %pad_add_fusion), kind=kLoop, calls=%fused_computation.21 | loop fusion | flops 3735552 | bytes 788480 | tf_op jit(solution)/shard_map/convert.7
  38.2 9.4 %message_rows.1 = (f32[13,72,128]{2,1,0:T(8,128)}, f32[13,72,128]{2,1,0:T(8,128)}, f32[13,72,128]{2,1,0:T(8,128)}, f32[13,72,128]{2,1,0:T(8,128)}) custom-call(bf16[2,256,32,256]{3,2,1,0:T(8,128)(2,1)} %spectra_ref, f32[2,129,256]{2,1,0:T(8,128)} %copy-done.7, bf16[64,256]{1,0:T(8,128)(2,1)} %fusion.37.select_ref), custom_call_target="tpu_custom_call" | custom-call | flops 268435456 | bytes 6144000 | tf_op jit(solution)/shard_map/message_rows/pallas_call | solution.py:460
  47.6 1.2 collective-permute-start.1
  48.8 1.2 collective-permute-start.2
  50.0 0.2 collective-permute-start.3
  50.2 0.7 dynamic-slice_bitcast_fusion
  50.9 0.8 pad_maximum_fusion.6.refs_7_
  51.7 0.8 pad_maximum_fusion.4.refs_5_
  52.5 0.8 pad_maximum_fusion.5.refs_7_
  53.3 5.5 %forward_last.3 = f32[128,32,128]{2,1,0:T(8,128)} custom-call(f32[32,128,256]{2,1,0:T(8,128)} %adjoint_ref.2, bf16[64,768]{1,0:T(8,128)(2,1)} %constant.170.clone.table_ref), custom_call_target="tpu_custom_call" | custom-call | flops 402653184 | bytes 6291456 | tf_op jit(solution)/shard_map/forward_last/pallas_call | solution.py:106
  58.8 5.6 %collective-permute-done.1.refs_1_ = f32[13,72,128]{2,1,0:T(8,128)S(1)} collective-permute-done((f32[13,72,128]{2,1,0:T(8,128)}, f32[13,72,128]{2,1,0:T(8,128)S(1)}, u32[]{:S(2)}, u32[]{:S(2)}) %collective-permute-start.1) | collective-permute-done | bytes 479264 | tf_op jit(solution)/shard_map/ppermute | solution.py:378
  64.4 34.0 %collective-permute-done.2.refs_2_ = f32[13,72,128]{2,1,0:T(8,128)S(1)} collective-permute-done((f32[13,72,128]{2,1,0:T(8,128)}, f32[13,72,128]{2,1,0:T(8,128)S(1)}, u32[]{:S(2)}, u32[]{:S(2)}) %collective-permute-start.2) | collective-permute-done | bytes 479264 | tf_op jit(solution)/shard_map/ppermute | solution.py:378
  98.4 15.3 %collective-permute-done.3.refs_3_ = f32[13,72,128]{2,1,0:T(8,128)S(1)} collective-permute-done((f32[13,72,128]{2,1,0:T(8,128)}, f32[13,72,128]{2,1,0:T(8,128)S(1)}, u32[]{:S(2)}, u32[]{:S(2)}) %collective-permute-start.3) | collective-permute-done | bytes 479264 | tf_op jit(solution)/shard_map/ppermute | solution.py:378
  113.7 1.4 all-to-all-done.1
  115.1 5.0 %all-to-all-start = ((f32[16,8,32,128]{3,2,1,0:T(8,128)}), f32[16,8,32,128]{3,2,1,0:T(8,128)S(1)}, u32[]{:S(2)}, u32[]{:S(2)}) async-start(f32[16,8,32,128]{3,2,1,0:T(8,128)} %bitcast.16), calls=%async_computation | async-start | bytes 4194304 | tf_op jit(solution)/shard_map/all_to_all | solution.py:609
  120.1 0.7 fusion.54
  120.8 13.3 %filter_planes.5 = (f32[2,2,8,32,128]{4,3,2,1,0:T(8,128)}, f32[2,2,8,32,128]{4,3,2,1,0:T(8,128)}, f32[2,2,8,32,128]{4,3,2,1,0:T(8,128)}, f32[2,2,8,32,128]{4,3,2,1,0:T(8,128)}) custom-call(s32[8]{0:T(128)} %get-tuple-element.131.places_ref, s32[1]{0:T(128)} %bitcast.5.special_ref, f32[8,2,16,32,128]{4,3,2,1,0:T(8,128)} %bitcast.7.planes_ref, ...), custom_call_target="tpu_custom_call" | custom-call | flops 3221225472 | bytes 5242880 | tf_op jit(solution)/shard_map/filter_planes/pallas_call | solution.py:208
  134.1 1.2 collective-permute-start.4
  135.3 1.2 collective-permute-start.5
  136.5 0.3 collective-permute-start.6
  136.8 15.4 %filter_planes.4 = f32[8,2,2,8,32,128]{5,4,3,2,1,0:T(8,128)} custom-call(s32[8]{0:T(128)} %get-tuple-element.132.places_ref, s32[1]{0:T(128)} %bitcast.5.special_ref, f32[8,2,16,32,128]{4,3,2,1,0:T(8,128)} %bitcast.7.planes_ref, f32[13,72,128]{2,1,0:T(8,128)} %get-tuple-element.67.refs_0_, f32[13,72,128]{2,1,0:T(8,128)} %copy-done.14, ...), custom_call_target="tpu_custom_call" | custom-call | flops 4831838208 | bytes 7340032 | tf_op jit(solution)/shard_map/filter_planes/pallas_call | solution.py:208
  152.2 1.6 collective-permute-done.4
  153.8 13.6 %collective-permute-done.5 = f32[2,2,8,32,128]{4,3,2,1,0:T(8,128)S(1)} collective-permute-done((f32[2,2,8,32,128]{4,3,2,1,0:T(8,128)}, f32[2,2,8,32,128]{4,3,2,1,0:T(8,128)S(1)}, u32[]{:S(2)}, u32[]{:S(2)}) %collective-permute-start.5) | collective-permute-done | bytes 524320 | tf_op jit(solution)/shard_map/ppermute | solution.py:668
  167.4 12.4 %collective-permute-done.6 = f32[2,2,8,32,128]{4,3,2,1,0:T(8,128)S(1)} collective-permute-done((f32[2,2,8,32,128]{4,3,2,1,0:T(8,128)}, f32[2,2,8,32,128]{4,3,2,1,0:T(8,128)S(1)}, u32[]{:S(2)}, u32[]{:S(2)}) %collective-permute-start.6) | collective-permute-done | bytes 524320 | tf_op jit(solution)/shard_map/ppermute | solution.py:668
  179.8 0.8 copy-done.5
  180.6 1.3 copy-done
  181.9 5.1 %all-to-all-start.2 = ((f32[16,2,8,32,128]{4,3,2,1,0:T(8,128)}), f32[16,2,8,32,128]{4,3,2,1,0:T(8,128)}, u32[]{:S(2)}, u32[]{:S(2)}) async-start(f32[16,2,8,32,128]{4,3,2,1,0:T(8,128)} %bitcast.17), calls=%async_computation.2 | async-start | bytes 8388608 | tf_op jit(solution)/shard_map/all_to_all | solution.py:609
  187.0 13.4 %filter_planes.3 = (f32[2,2,8,32,128]{4,3,2,1,0:T(8,128)}, f32[2,2,8,32,128]{4,3,2,1,0:T(8,128)}, f32[2,2,8,32,128]{4,3,2,1,0:T(8,128)}, f32[2,2,8,32,128]{4,3,2,1,0:T(8,128)}) custom-call(s32[8]{0:T(128)} %get-tuple-element.133.places_ref, s32[1]{0:T(128)} %bitcast.5.special_ref, f32[8,2,8,32,128]{4,3,2,1,0:T(8,128)} %bitcast.18, ...), custom_call_target="tpu_custom_call" | custom-call | flops 3221225472 | bytes 5242880 | tf_op jit(solution)/shard_map/filter_planes/pallas_call | solution.py:208
  200.7 0.4 collective-permute-start.10
  201.1 0.3 copy-done.13
  201.4 1.2 collective-permute-start.7
  202.6 1.2 collective-permute-start.8
  203.8 0.2 collective-permute-start.9
  204.1 1.0 pad_maximum_fusion.refs_2_
  205.1 1.0 copy-done.1
  206.1 7.8 %backward_last.2.refs_6_ = f32[32,128,256]{2,1,0:T(8,128)} custom-call(f32[2,32,128,256]{3,2,1,0:T(8,128)} %cosine_factors.1.refs_0_, bf16[192,256]{1,0:T(8,128)(2,1)} %pad_maximum_fusion.8.refs_1_, f32[4,2,8,32,128]{4,3,2,1,0:T(8,128)} %pad_maximum_fusion.refs_2_, f32[4,2,8,32,128]{4,3,2,1,0:T(8,128)} %copy-done.1), custom_call_target="tpu_custom_call" | custom-call | flops 805306368 | bytes 18874368 | tf_op jit(solution)/shard_map/backward_last/pallas_call | solution.py:311
  213.9 12.7 %collective-permute-done.7 = f32[2,2,8,32,128]{4,3,2,1,0:T(8,128)S(1)} collective-permute-done((f32[2,2,8,32,128]{4,3,2,1,0:T(8,128)S(1)}, f32[2,2,8,32,128]{4,3,2,1,0:T(8,128)S(1)}, u32[]{:S(2)}, u32[]{:S(2)}) %collective-permute-start.7) | collective-permute-done | bytes 524320 | tf_op jit(solution)/shard_map/ppermute | solution.py:668
  226.6 41.5 %collective-permute-done.8 = f32[2,2,8,32,128]{4,3,2,1,0:T(8,128)S(1)} collective-permute-done((f32[2,2,8,32,128]{4,3,2,1,0:T(8,128)S(1)}, f32[2,2,8,32,128]{4,3,2,1,0:T(8,128)S(1)}, u32[]{:S(2)}, u32[]{:S(2)}) %collective-permute-start.8) | collective-permute-done | bytes 524320 | tf_op jit(solution)/shard_map/ppermute | solution.py:668
  268.1 17.5 %collective-permute-done.9 = f32[2,2,8,32,128]{4,3,2,1,0:T(8,128)S(1)} collective-permute-done((f32[2,2,8,32,128]{4,3,2,1,0:T(8,128)S(1)}, f32[2,2,8,32,128]{4,3,2,1,0:T(8,128)S(1)}, u32[]{:S(2)}, u32[]{:S(2)}) %collective-permute-start.9) | collective-permute-done | bytes 524320 | tf_op jit(solution)/shard_map/ppermute | solution.py:668
  285.9 1.2 collective-permute-start.11
  287.1 1.0 pad_maximum_fusion.2.refs_3_
  288.1 1.3 collective-permute-done.11.refs_4_
  289.4 1.0 copy-done.2
  290.4 10.6 %backward_last.3 = f32[32,128,256]{2,1,0:T(8,128)} custom-call(f32[2,32,128,256]{3,2,1,0:T(8,128)} %cosine_factors.1.refs_0_, bf16[192,256]{1,0:T(8,128)(2,1)} %pad_maximum_fusion.9.refs_1_, bf16[384,256]{1,0:T(8,128)(2,1)} %constant.169.clone.refs_2_, f32[4,2,8,32,128]{4,3,2,1,0:T(8,128)} %pad_maximum_fusion.2.refs_3_, f32[4,2,8,32,128]{4,3,2,1,0:T(8,128)} %copy-done.2, ...), custom_call_target="tpu_custom_call" | custom-call | flops 2415919104 | bytes 23068672 | tf_op jit(solution)/shard_map/backward_last/pallas_call | solution.py:311
  (61 shorter events, 1.1 us)
Async XLA Ops:
  1.4 10.3 %collective-permute-start = (f32[2,129,256]{2,1,0:T(8,128)S(1)}, f32[2,129,256]{2,1,0:T(8,128)S(1)}, u32[]{:S(2)}, u32[]{:S(2)}) collective-permute-start(f32[2,129,256]{2,1,0:T(8,128)S(1)} %fusion.18), channel_id=1, source_target_pairs={{0,8},{8,0},{1,9},{9,1},{16,24},{24,16},{17,25},{25,17}} | collective-permute-start | bytes 792584 | tf_op jit(solution)/shard_map/ppermute | solution.py:582
  11.8 0.7 copy-start.7
  11.8 6.7 %copy-start.17 = (s32[8]{0:T(128)S(1)}, s32[8]{0:T(128)}, u32[]{:S(2)}) copy-start(s32[8]{0:T(128)} %param.18) | copy-start | bytes 100
  11.8 6.7 %copy-start.18 = (s32[2]{0:T(128)S(1)}, s32[2]{0:T(128)}, u32[]{:S(2)}) copy-start(s32[2]{0:T(128)} %param.19) | copy-start | bytes 28
  11.8 8.6 %copy-start.9 = (s32[8,8]{1,0:T(8,128)S(1)}, s32[8,8]{1,0:T(8,128)}, u32[]{:S(2)}) copy-start(s32[8,8]{1,0:T(8,128)} %constant.168.clone) | copy-start | bytes 772
  11.8 9.2 %copy-start.8 = (s32[8,8]{1,0:T(8,128)S(1)}, s32[8,8]{1,0:T(8,128)}, u32[]{:S(2)}) copy-start(s32[8,8]{1,0:T(8,128)} %constant.167.clone) | copy-start | bytes 772
  12.4 102.7 %all-to-all-start.1 = ((f32[16,16,32,128]{3,2,1,0:T(8,128)}), f32[16,16,32,128]{3,2,1,0:T(8,128)}, u32[]{:S(2)}, u32[]{:S(2)}) async-start(f32[16,16,32,128]{3,2,1,0:T(8,128)} %bitcast.15), calls=%async_computation.1 | async-start | bytes 8388608 | tf_op jit(solution)/shard_map/all_to_all | solution.py:609
  21.6 11.1 %copy-start.10 = (s32[256]{0:T(256)S(1)}, s32[256]{0:T(256)}, u32[]{:S(2)}) copy-start(s32[256]{0:T(256)} %constant.166.clone) | copy-start | bytes 3076
  47.6 16.8 %collective-permute-start.1 = (f32[13,72,128]{2,1,0:T(8,128)}, f32[13,72,128]{2,1,0:T(8,128)S(1)}, u32[]{:S(2)}, u32[]{:S(2)}) collective-permute-start(f32[13,72,128]{2,1,0:T(8,128)} %get-tuple-element.60), channel_id=1, source_target_pairs={{0,2},{2,0},{4,6},{6,4},{8,10},{10,8},{12,14},{14,12},{1,3},{3,1},... | collective-permute-start | bytes 1437704 | tf_op jit(solution)/shard_map/ppermute | solution.py:378
  48.8 49.7 %collective-permute-start.2 = (f32[13,72,128]{2,1,0:T(8,128)}, f32[13,72,128]{2,1,0:T(8,128)S(1)}, u32[]{:S(2)}, u32[]{:S(2)}) collective-permute-start(f32[13,72,128]{2,1,0:T(8,128)} %get-tuple-element.61), channel_id=1, source_target_pairs={{0,4},{2,6},{4,0},{6,2},{8,12},{10,14},{12,8},{14,10},{1,5},{3,7},... | collective-permute-start | bytes 1437704 | tf_op jit(solution)/shard_map/ppermute | solution.py:378
  50.0 63.7 %collective-permute-start.3 = (f32[13,72,128]{2,1,0:T(8,128)}, f32[13,72,128]{2,1,0:T(8,128)S(1)}, u32[]{:S(2)}, u32[]{:S(2)}) collective-permute-start(f32[13,72,128]{2,1,0:T(8,128)} %get-tuple-element.62), channel_id=1, source_target_pairs={{0,6},{2,4},{4,2},{6,0},{8,14},{10,12},{12,10},{14,8},{1,7},{3,5},... | collective-permute-start | bytes 1437704 | tf_op jit(solution)/shard_map/ppermute | solution.py:378
  64.4 56.4 %copy-start.14 = (f32[13,72,128]{2,1,0:T(8,128)}, f32[13,72,128]{2,1,0:T(8,128)S(1)}, u32[]{:S(2)}) copy-start(f32[13,72,128]{2,1,0:T(8,128)S(1)} %collective-permute-done.1.refs_1_) | copy-start | bytes 1437700
  98.4 22.4 %copy-start.15 = (f32[13,72,128]{2,1,0:T(8,128)}, f32[13,72,128]{2,1,0:T(8,128)S(1)}, u32[]{:S(2)}) copy-start(f32[13,72,128]{2,1,0:T(8,128)S(1)} %collective-permute-done.2.refs_2_) | copy-start | bytes 1437700
  113.7 7.1 %copy-start.16 = (f32[13,72,128]{2,1,0:T(8,128)}, f32[13,72,128]{2,1,0:T(8,128)S(1)}, u32[]{:S(2)}) copy-start(f32[13,72,128]{2,1,0:T(8,128)S(1)} %collective-permute-done.3.refs_3_) | copy-start | bytes 1437700
  115.1 65.5 %all-to-all-start = ((f32[16,8,32,128]{3,2,1,0:T(8,128)}), f32[16,8,32,128]{3,2,1,0:T(8,128)S(1)}, u32[]{:S(2)}, u32[]{:S(2)}) async-start(f32[16,8,32,128]{3,2,1,0:T(8,128)} %bitcast.16), calls=%async_computation | async-start | bytes 4194304 | tf_op jit(solution)/shard_map/all_to_all | solution.py:609
  134.1 19.7 %collective-permute-start.4 = (f32[2,2,8,32,128]{4,3,2,1,0:T(8,128)}, f32[2,2,8,32,128]{4,3,2,1,0:T(8,128)S(1)}, u32[]{:S(2)}, u32[]{:S(2)}) collective-permute-start(f32[2,2,8,32,128]{4,3,2,1,0:T(8,128)} %get-tuple-element.85), channel_id=1, source_target_pairs={{0,2},{2,0},{4,6},{6,4},{8,10},{10,8},{12,14},{14,12},{1,3},{3,1},... | collective-permute-start | bytes 1572872 | tf_op jit(solution)/shard_map/ppermute | solution.py:668
  135.3 32.1 %collective-permute-start.5 = (f32[2,2,8,32,128]{4,3,2,1,0:T(8,128)}, f32[2,2,8,32,128]{4,3,2,1,0:T(8,128)S(1)}, u32[]{:S(2)}, u32[]{:S(2)}) collective-permute-start(f32[2,2,8,32,128]{4,3,2,1,0:T(8,128)} %get-tuple-element.86), channel_id=1, source_target_pairs={{0,4},{2,6},{4,0},{6,2},{8,12},{10,14},{12,8},{14,10},{1,5},{3,7},... | collective-permute-start | bytes 1572872 | tf_op jit(solution)/shard_map/ppermute | solution.py:668
  136.5 43.3 %collective-permute-start.6 = (f32[2,2,8,32,128]{4,3,2,1,0:T(8,128)}, f32[2,2,8,32,128]{4,3,2,1,0:T(8,128)S(1)}, u32[]{:S(2)}, u32[]{:S(2)}) collective-permute-start(f32[2,2,8,32,128]{4,3,2,1,0:T(8,128)} %get-tuple-element.87), channel_id=1, source_target_pairs={{0,6},{2,4},{4,2},{6,0},{8,14},{10,12},{12,10},{14,8},{1,7},{3,5},... | collective-permute-start | bytes 1572872 | tf_op jit(solution)/shard_map/ppermute | solution.py:668
  179.8 0.8 copy-start.5
  180.6 1.3 copy-start
  181.9 107.5 %all-to-all-start.2 = ((f32[16,2,8,32,128]{4,3,2,1,0:T(8,128)}), f32[16,2,8,32,128]{4,3,2,1,0:T(8,128)}, u32[]{:S(2)}, u32[]{:S(2)}) async-start(f32[16,2,8,32,128]{4,3,2,1,0:T(8,128)} %bitcast.17), calls=%async_computation.2 | async-start | bytes 8388608 | tf_op jit(solution)/shard_map/all_to_all | solution.py:609
  187.0 13.4 %copy-start.4 = (f32[2,2,8,32,128]{4,3,2,1,0:T(8,128)S(1)}, f32[2,2,8,32,128]{4,3,2,1,0:T(8,128)}, u32[]{:S(2)}) copy-start(f32[2,2,8,32,128]{4,3,2,1,0:T(8,128)} %get-tuple-element.97) | copy-start | bytes 1572868
  187.0 13.5 %copy-start.6 = (f32[2,2,8,32,128]{4,3,2,1,0:T(8,128)S(1)}, f32[2,2,8,32,128]{4,3,2,1,0:T(8,128)}, u32[]{:S(2)}) copy-start(f32[2,2,8,32,128]{4,3,2,1,0:T(8,128)} %copy-done.5) | copy-start | bytes 1572868
  200.4 1.0 copy-start.13
  200.4 2.2 copy-start.12
  200.4 3.4 %copy-start.11 = (f32[2,2,8,32,128]{4,3,2,1,0:T(8,128)S(1)}, f32[2,2,8,32,128]{4,3,2,1,0:T(8,128)}, u32[]{:S(2)}) copy-start(f32[2,2,8,32,128]{4,3,2,1,0:T(8,128)} %get-tuple-element.95) | copy-start | bytes 1572868
  200.7 4.4 %collective-permute-start.10 = (f32[4,2,8,32,128]{4,3,2,1,0:T(8,128)S(1)}, f32[4,2,8,32,128]{4,3,2,1,0:T(8,128)S(1)}, u32[]{:S(2)}, u32[]{:S(2)}) collective-permute-start(f32[4,2,8,32,128]{4,3,2,1,0:T(8,128)S(1)} %pad_maximum_fusion.1), channel_id=1, source_target_pairs={{0,1},{1,0},{2,3},{3,2},{4,5},{5,4},{6,7},{7,6},{8,9},{9,8},{10,11... | collective-permute-start | bytes 3145736 | tf_op jit(solution)/shard_map/ppermute | solution.py:677
  201.4 25.1 %collective-permute-start.7 = (f32[2,2,8,32,128]{4,3,2,1,0:T(8,128)S(1)}, f32[2,2,8,32,128]{4,3,2,1,0:T(8,128)S(1)}, u32[]{:S(2)}, u32[]{:S(2)}) collective-permute-start(f32[2,2,8,32,128]{4,3,2,1,0:T(8,128)S(1)} %copy-done.13), channel_id=1, source_target_pairs={{0,2},{2,0},{4,6},{6,4},{8,10},{10,8},{12,14},{14,12},{1,3},{3,1},... | collective-permute-start | bytes 1572872 | tf_op jit(solution)/shard_map/ppermute | solution.py:668
  202.6 65.5 %collective-permute-start.8 = (f32[2,2,8,32,128]{4,3,2,1,0:T(8,128)S(1)}, f32[2,2,8,32,128]{4,3,2,1,0:T(8,128)S(1)}, u32[]{:S(2)}, u32[]{:S(2)}) collective-permute-start(f32[2,2,8,32,128]{4,3,2,1,0:T(8,128)S(1)} %copy-done.12), channel_id=1, source_target_pairs={{0,4},{2,6},{4,0},{6,2},{8,12},{10,14},{12,8},{14,10},{1,5},{3,7},... | collective-permute-start | bytes 1572872 | tf_op jit(solution)/shard_map/ppermute | solution.py:668
  203.8 81.8 %collective-permute-start.9 = (f32[2,2,8,32,128]{4,3,2,1,0:T(8,128)S(1)}, f32[2,2,8,32,128]{4,3,2,1,0:T(8,128)S(1)}, u32[]{:S(2)}, u32[]{:S(2)}) collective-permute-start(f32[2,2,8,32,128]{4,3,2,1,0:T(8,128)S(1)} %copy-done.11), channel_id=1, source_target_pairs={{0,6},{2,4},{4,2},{6,0},{8,14},{10,12},{12,10},{14,8},{1,7},{3,5},... | collective-permute-start | bytes 1572872 | tf_op jit(solution)/shard_map/ppermute | solution.py:668
  205.1 80.5 %copy-start.3 = (f32[2,2,8,32,128]{4,3,2,1,0:T(8,128)S(1)}, f32[2,2,8,32,128]{4,3,2,1,0:T(8,128)}, u32[]{:S(2)}) copy-start(f32[2,2,8,32,128]{4,3,2,1,0:T(8,128)} %get-tuple-element.101) | copy-start | bytes 1572868
  205.1 1.0 copy-start.1
  285.9 3.5 %collective-permute-start.11 = (f32[4,2,8,32,128]{4,3,2,1,0:T(8,128)S(1)}, f32[4,2,8,32,128]{4,3,2,1,0:T(8,128)S(1)}, u32[]{:S(2)}, u32[]{:S(2)}) collective-permute-start(f32[4,2,8,32,128]{4,3,2,1,0:T(8,128)S(1)} %pad_maximum_fusion.3), channel_id=1, source_target_pairs={{0,1},{1,0},{2,3},{3,2},{4,5},{5,4},{6,7},{7,6},{8,9},{9,8},{10,11... | collective-permute-start | bytes 3145736 | tf_op jit(solution)/shard_map/ppermute | solution.py:677
  289.4 1.0 copy-start.2

commit v4 on v3

--- a/solution.py
+++ b/solution.py
@@ -9,7 +9,9 @@
 from jax.sharding import PartitionSpec as P
 
 VMEM_BYTES = 56 * 1024 * 1024
+LAST_BYTES = 48 * 1024 * 1024
 SHARED = 2
+GROUP = 4
 
 
 def hartley(length):
@@ -74,8 +76,8 @@
     return jnp.dot(stacked, table, preferred_element_type=jnp.float32)
 
 
-def params():
-    return pltpu.CompilerParams(vmem_limit_bytes=VMEM_BYTES)
+def params(limit=VMEM_BYTES):
+    return pltpu.CompilerParams(vmem_limit_bytes=limit)
 
 
 def forward_last(adjoint, table, depth, copies):
@@ -156,35 +158,41 @@
     out_px = tables[2].shape[0] // rows_one
     message_rows = messages[0].shape[1]
     local_two = length_two // 2 // len(messages)
+    group = next(g for g in (GROUP, 2, 1) if planes_count % g == 0 and first % g == 0)
 
     def body(places_ref, special_ref, planes_ref, *refs):
-        message_refs = refs[: len(messages)]
-        one_f, two_f, one_b, two_b = refs[len(messages) : len(messages) + 4]
-        out_refs = refs[len(messages) + 4 :]
-        value = jnp.concatenate(
-            [
-                planes_ref[:, part, 0].reshape(length_one, rows_two)
-                for part in range(width_py)
-            ],
-            axis=1,
-        )
-        value = right_dot(value, two_f[...])
-        value = left_dot(one_f[...], value)
+        one_f, two_f, one_b, two_b = refs[group * len(messages) :][:4]
+        out_refs = refs[group * len(messages) + 4 :]
+        values = []
+        for member in range(group):
+            value = jnp.concatenate(
+                [
+                    planes_ref[:, part, member].reshape(length_one, rows_two)
+                    for part in range(width_py)
+                ],
+                axis=1,
+            )
+            values.append(right_dot(value, two_f[...]))
+        values = [left_dot(one_f[...], value) for value in values]
         for slot in range(slots):
-            plane = whole_plane(message_refs, slot, slots, special_ref[0], local_two)
-            back = left_dot(one_b[...], value * plane)
-            back = right_dot(back, two_b[...])
-            for part in range(width_py):
-                piece = back[:, part * rows_two : (part + 1) * rows_two]
-                if split:
-                    for index in range(out_px):
-                        out_refs[index][part, slot, 0] = piece[
-                            index * rows_one : (index + 1) * rows_one
-                        ]
-                else:
-                    out_refs[0][:, part, slot, 0] = piece.reshape(
-                        out_px, rows_one, rows_two
-                    )
+            backs = []
+            for member, value in enumerate(values):
+                message_refs = refs[member * len(messages) : (member + 1) * len(messages)]
+                plane = whole_plane(message_refs, slot, slots, special_ref[0], local_two)
+                backs.append(left_dot(one_b[...], value * plane))
+            for member, back in enumerate(backs):
+                back = right_dot(back, two_b[...])
+                for part in range(width_py):
+                    piece = back[:, part * rows_two : (part + 1) * rows_two]
+                    if split:
+                        for index in range(out_px):
+                            out_refs[index][part, slot, member] = piece[
+                                index * rows_one : (index + 1) * rows_one
+                            ]
+                    else:
+                        out_refs[0][:, part, slot, member] = piece.reshape(
+                            out_px, rows_one, rows_two
+                        )
 
     plane_size = length_one * length_two
     if split:
@@ -192,7 +200,8 @@
         out_shape = [jax.ShapeDtypeStruct(extent, jnp.float32)] * out_px
         out_specs = [
             pl.BlockSpec(
-                (width_py, slots, 1, rows_one, rows_two), lambda i, *_: (0, 0, i, 0, 0)
+                (width_py, slots, group, rows_one, rows_two),
+                lambda i, *_: (0, 0, i, 0, 0),
             )
         ] * out_px
     else:
@@ -200,29 +209,30 @@
         out_shape = [jax.ShapeDtypeStruct(extent, jnp.float32)]
         out_specs = [
             pl.BlockSpec(
-                (out_px, width_py, slots, 1, rows_one, rows_two),
+                (out_px, width_py, slots, group, rows_one, rows_two),
                 lambda i, *_: (0, 0, 0, i, 0, 0),
             )
         ]
+
+    def message_spec(member):
+        return pl.BlockSpec(
+            (1, message_rows, length_one // 2),
+            lambda i, places_ref, special_ref: (places_ref[group * i + member], 0, 0),
+        )
+
     out_rows = out_px * rows_one
     outs = pl.pallas_call(
         body,
         grid_spec=pltpu.PrefetchScalarGridSpec(
             num_scalar_prefetch=2,
-            grid=(planes_count,),
+            grid=(planes_count // group,),
             in_specs=[
                 pl.BlockSpec(
-                    (width_px, width_py, 1, rows_one, rows_two),
-                    lambda i, *_: (0, 0, first + i, 0, 0),
+                    (width_px, width_py, group, rows_one, rows_two),
+                    lambda i, *_: (0, 0, first // group + i, 0, 0),
                 )
             ]
-            + [
-                pl.BlockSpec(
-                    (1, message_rows, length_one // 2),
-                    lambda i, places_ref, special_ref: (places_ref[i], 0, 0),
-                )
-            ]
-            * len(messages)
+            + [message_spec(member) for member in range(group) for _ in messages]
             + [pl.BlockSpec(table.shape, lambda i, *_: (0, 0)) for table in tables],
             out_specs=out_specs,
         ),
@@ -241,7 +251,7 @@
             transcendentals=0,
         ),
         name="filter_planes",
-    )(places, special, planes, *messages, *tables)
+    )(places, special, planes, *(messages * group), *tables)
     return outs if split else outs[0]
 
 
@@ -314,7 +324,7 @@
         in_specs=in_specs,
         out_specs=space,
         out_shape=jax.ShapeDtypeStruct((rows_one, rows_two, length), jnp.float32),
-        compiler_params=params(),
+        compiler_params=params(LAST_BYTES),
         cost_estimate=pl.CostEstimate(
             flops=6 * slots * size * planes_count * length,
             bytes_accessed=4 * size * (slots * planes_count + (2 + slots) * length),
@@ -616,6 +626,11 @@
     sent, spectra, edge, adjoint = barrier((sent, spectra, edge, adjoint))
     wanted, places = folded_rows(owned)
     messages = kernel_messages(spectra, edge, wanted, width_px, width_py)
+    messages, saved, adjoint, px_index, py_index = barrier(
+        (messages, saved, adjoint, px_index, py_index)
+    )
+    half_index = px_index // half_px
+    px_low = px_index % half_px
     messages = send_messages(messages, width_px)
     places = jnp.asarray(places, dtype=jnp.int32)[device]
     local_two = length_two // width_px

time: 302 us -> 298 us (0.987)
  waiting for transfers between devices: 159 us -> 180 us
  Pallas kernels: 90.5 us -> 73.7 us
  local copies, waits for them, and re-layouts: 10.5 us -> 6.46 us
  other arithmetic: 13 us -> 9.74 us
    ppermute x6, waiting for transfers between devices: 99.3 us -> 118 us  [shared_rows(): lax.ppermute(pieces[delta], 'px', swap_pairs(width_px, half_px, delta))]
    pallas_call x3, Pallas kernels: 42 us -> 26 us  [filter_planes(): pl.pallas_call(body, grid_spec=pltpu.PrefetchScalarGridSpec(num_scalar_pr...]
    unnamed x38 -> x30, local copies, waits for them, and re-layouts: 5.14 us -> 1.1 us
  transfers between devices with their start and end apart: 15 -> 15, of which waited for: 12 -> 11; matrix products, arithmetic and copies ran while one was open for 6% -> 5% of each run, Pallas kernels for 27% -> 21%
where the time goes in v4:
time: 298 us; the launch traced here: 297 us
  waiting for transfers between devices  180 us (60%)
  Pallas kernels  73.7 us (25%)
  starting transfers between devices  27.6 us (9%)
  other arithmetic  9.74 us (3%)
  local copies, waits for them, and re-layouts  6.46 us (2%)
    ppermute x6, waiting for transfers between devices, shared_rows(): lax.ppermute(pieces[delta], 'px', swap_pairs(width_px, half_px, delta))  118 us
    ppermute x3, waiting for transfers between devices, send_messages(): lax.ppermute(message[delta], 'px', swap_pairs(width_px, half_px, delta))  56.3 us
    pallas_call x3, Pallas kernels, filter_planes(): pl.pallas_call(body, grid_spec=pltpu.PrefetchScalarGridSpec(num_scalar_pr...  26 us
    pallas_call x2, Pallas kernels, backward_last(): pl.pallas_call(body, grid=(rows_one // block,), in_specs=in_specs, out_sp...  17.6 us
    all_to_all x3, starting transfers between devices, exchange(): return lax.all_to_all(value, ('px', 'py'), 0, 0, tiled=True)  16 us
    pallas_call x2, Pallas kernels, forward_last(): pl.pallas_call(body, grid=(rows_one // block,), in_specs=[pl.BlockSpec((b...  11.6 us
    pallas_call x1, Pallas kernels, message_rows(): pl.pallas_call(body, grid=(1,), in_specs=[pl.BlockSpec(part, lambda i: (0...  9.41 us
    pallas_call x1, Pallas kernels, cosine_factors(): pl.pallas_call(body, grid=(rows_one // block,), in_specs=[pl.BlockSpec(me...  9.08 us
  transfers between devices with their start and end apart: 15, of which 11 were waited for; matrix products, arithmetic and copies ran while one was open for 5% of the time, Pallas kernels for 21%

profile of v4, /device:TPU:21, one launch (start us, length us, event | category | flops | bytes accessed | tf_op | source)
XLA Modules:
  0.0 297.4 jit_solution(2758689080829822689)
XLA Ops:
  0.0 1.4 slice.60
  1.4 2.0 collective-permute-start
  3.4 6.1 %forward_last.2 = f32[256,32,128]{2,1,0:T(8,128)} custom-call(f32[32,128,256]{2,1,0:T(8,128)} %adjoint_ref.2, bf16[192,768]{1,0:T(8,128)(2,1)} %constant.161.clone.table_ref), custom_call_target="tpu_custom_call" | custom-call | flops 1207959552 | bytes 8388608 | tf_op jit(solution)/shard_map/forward_last/pallas_call | solution.py:108
  9.5 2.3 collective-permute-done.edge_ref
  11.8 0.7 copy-done.6
  12.5 5.8 %all-to-all-start.1 = ((f32[16,16,32,128]{3,2,1,0:T(8,128)}), f32[16,16,32,128]{3,2,1,0:T(8,128)}, u32[]{:S(2)}, u32[]{:S(2)}) async-start(f32[16,16,32,128]{3,2,1,0:T(8,128)} %bitcast.15), calls=%async_computation.1 | async-start | bytes 8388608 | tf_op jit(solution)/shard_map/all_to_all | solution.py:619
  18.4 0.2 fusion.38
  18.5 0.5 convert_element_type.45.chosen_ref
  19.1 0.7 dynamic-slice_reduce_fusion
  19.8 0.1 reshape_squeeze.3
  19.9 0.1 eq.55
  19.9 0.7 dynamic-slice_bitcast_fusion
  20.6 0.7 fusion.37.select_ref
  21.3 9.4 %message_rows.1 = (f32[13,72,128]{2,1,0:T(8,128)}, f32[13,72,128]{2,1,0:T(8,128)}, f32[13,72,128]{2,1,0:T(8,128)}, f32[13,72,128]{2,1,0:T(8,128)}) custom-call(bf16[2,256,32,256]{3,2,1,0:T(8,128)(2,1)} %spectra_ref, f32[2,129,256]{2,1,0:T(8,128)} %copy-done.6, bf16[64,256]{1,0:T(8,128)(2,1)} %fusion.37.select_ref), custom_call_target="tpu_custom_call" | custom-call | flops 268435456 | bytes 6144000 | tf_op jit(solution)/shard_map/message_rows/pallas_call | solution.py:470
  30.8 0.1 broadcast_add_fusion
  30.8 0.1 add.212
  31.0 0.1 add.192
  31.1 0.6 gather_fusion.1
  31.7 0.1 mul.152
  31.7 0.6 gather_fusion
  32.3 0.1 mul.148
  32.4 1.2 collective-permute-start.1
  33.6 1.2 collective-permute-start.2
  34.8 0.2 collective-permute-start.3
  35.0 9.1 %cosine_factors.1.refs_0_ = f32[2,32,128,256]{3,2,1,0:T(8,128)} custom-call(f32[2]{0:T(128)} %convert_element_type.45.chosen_ref, f32[32,128,256]{2,1,0:T(8,128)} %saved_ref), custom_call_target="tpu_custom_call" | custom-call | flops 50331648 | bytes 12582912 | tf_op jit(solution)/shard_map/cosine_factors/pallas_call | solution.py:363
  44.1 5.5 %forward_last.3 = f32[128,32,128]{2,1,0:T(8,128)} custom-call(f32[32,128,256]{2,1,0:T(8,128)} %adjoint_ref.2, bf16[64,768]{1,0:T(8,128)(2,1)} %constant.170.clone.table_ref), custom_call_target="tpu_custom_call" | custom-call | flops 402653184 | bytes 6291456 | tf_op jit(solution)/shard_map/forward_last/pallas_call | solution.py:108
  49.7 0.3 reduce-precision_convert_fusion.5
  50.0 0.6 reduce-precision_convert_fusion.3
  50.7 0.7 pad_maximum_fusion.7.refs_18_
  51.4 0.3 reduce-precision_convert_fusion.4
  51.7 3.4 %reduce-precision_convert_fusion = (bf16[256,256]{1,0:T(8,128)(2,1)S(1)}, bf16[256,256]{1,0:T(8,128)(2,1)S(1)}, bf16[256,256]{1,0:T(8,128)(2,1)S(1)}, bf16[256,2...) fusion(s32[256]{0:T(256)S(1)} %and_select_fusion.1, s32[256]{0:T(256)S(1)} %pad_add_fusion), kind=kLoop, calls=%fused_computation.21 | loop fusion | flops 3735552 | bytes 788480 | tf_op jit(solution)/shard_map/convert.7
  55.2 0.8 pad_maximum_fusion.6.refs_19_
  55.9 0.8 pad_maximum_fusion.4.refs_17_
  56.7 0.8 pad_maximum_fusion.5.refs_19_
  57.5 40.9 %collective-permute-done.2.refs_2_.refs_6_.refs_10_.refs_14_ = f32[13,72,128]{2,1,0:T(8,128)S(1)} collective-permute-done((f32[13,72,128]{2,1,0:T(8,128)}, f32[13,72,128]{2,1,0:T(8,128)S(1)}, u32[]{:S(2)}, u32[]{:S(2)}) %collective-permute-start.2) | collective-permute-done | bytes 479264 | tf_op jit(solution)/shard_map/ppermute | solution.py:388
  98.5 15.3 %collective-permute-done.3.refs_3_.refs_7_.refs_11_.refs_15_ = f32[13,72,128]{2,1,0:T(8,128)S(1)} collective-permute-done((f32[13,72,128]{2,1,0:T(8,128)}, f32[13,72,128]{2,1,0:T(8,128)S(1)}, u32[]{:S(2)}, u32[]{:S(2)}) %collective-permute-start.3) | collective-permute-done | bytes 479264 | tf_op jit(solution)/shard_map/ppermute | solution.py:388
  113.8 1.3 all-to-all-done.1
  115.1 5.0 %all-to-all-start = ((f32[16,8,32,128]{3,2,1,0:T(8,128)}), f32[16,8,32,128]{3,2,1,0:T(8,128)}, u32[]{:S(2)}, u32[]{:S(2)}) async-start(f32[16,8,32,128]{3,2,1,0:T(8,128)} %bitcast.16), calls=%async_computation | async-start | bytes 4194304 | tf_op jit(solution)/shard_map/all_to_all | solution.py:619
  120.2 0.6 fusion.54
  120.8 8.0 %filter_planes.5 = (f32[2,2,8,32,128]{4,3,2,1,0:T(8,128)}, f32[2,2,8,32,128]{4,3,2,1,0:T(8,128)}, f32[2,2,8,32,128]{4,3,2,1,0:T(8,128)}, f32[2,2,8,32,128]{4,3,2,1,0:T(8,128)}) custom-call(s32[8]{0:T(128)} %get-tuple-element.147.places_ref, s32[1]{0:T(128)} %bitcast.5.special_ref, f32[8,2,16,32,128]{4,3,2,1,0:T(8,128)} %bitcast.7.planes_ref, ...), custom_call_target="tpu_custom_call" | custom-call | flops 3221225472 | bytes 5242880 | tf_op jit(solution)/shard_map/filter_planes/pallas_call | solution.py:224
  128.8 1.2 collective-permute-start.4
  130.1 1.2 collective-permute-start.5
  131.3 0.3 collective-permute-start.6
  131.6 9.8 %filter_planes.4 = f32[8,2,2,8,32,128]{5,4,3,2,1,0:T(8,128)} custom-call(s32[8]{0:T(128)} %get-tuple-element.148.places_ref, s32[1]{0:T(128)} %bitcast.5.special_ref, f32[8,2,16,32,128]{4,3,2,1,0:T(8,128)} %bitcast.7.planes_ref, f32[13,72,128]{2,1,0:T(8,128)} %get-tuple-element.83.refs_0_.refs_4_.refs_8_.refs_12_, f32[13,72,128]{2,1,0:T(8,128)} %copy-done.1, ...), custom_call_target="tpu_custom_call" | custom-call | flops 4831838208 | bytes 7340032 | tf_op jit(solution)/shard_map/filter_planes/pallas_call | solution.py:224
  141.4 7.4 %collective-permute-done.4 = f32[2,2,8,32,128]{4,3,2,1,0:T(8,128)S(1)} collective-permute-done((f32[2,2,8,32,128]{4,3,2,1,0:T(8,128)}, f32[2,2,8,32,128]{4,3,2,1,0:T(8,128)S(1)}, u32[]{:S(2)}, u32[]{:S(2)}) %collective-permute-start.4) | collective-permute-done | bytes 524320 | tf_op jit(solution)/shard_map/ppermute | solution.py:683
  148.8 18.7 %collective-permute-done.5 = f32[2,2,8,32,128]{4,3,2,1,0:T(8,128)S(1)} collective-permute-done((f32[2,2,8,32,128]{4,3,2,1,0:T(8,128)}, f32[2,2,8,32,128]{4,3,2,1,0:T(8,128)S(1)}, u32[]{:S(2)}, u32[]{:S(2)}) %collective-permute-start.5) | collective-permute-done | bytes 524320 | tf_op jit(solution)/shard_map/ppermute | solution.py:683
  167.5 12.2 %collective-permute-done.6 = f32[2,2,8,32,128]{4,3,2,1,0:T(8,128)S(1)} collective-permute-done((f32[2,2,8,32,128]{4,3,2,1,0:T(8,128)}, f32[2,2,8,32,128]{4,3,2,1,0:T(8,128)S(1)}, u32[]{:S(2)}, u32[]{:S(2)}) %collective-permute-start.6) | collective-permute-done | bytes 524320 | tf_op jit(solution)/shard_map/ppermute | solution.py:683
  179.8 5.1 %all-to-all-start.2 = ((f32[16,2,8,32,128]{4,3,2,1,0:T(8,128)}), f32[16,2,8,32,128]{4,3,2,1,0:T(8,128)}, u32[]{:S(2)}, u32[]{:S(2)}) async-start(f32[16,2,8,32,128]{4,3,2,1,0:T(8,128)} %bitcast.17), calls=%async_computation.2 | async-start | bytes 8388608 | tf_op jit(solution)/shard_map/all_to_all | solution.py:619
  184.9 8.1 %filter_planes.3 = (f32[2,2,8,32,128]{4,3,2,1,0:T(8,128)}, f32[2,2,8,32,128]{4,3,2,1,0:T(8,128)}, f32[2,2,8,32,128]{4,3,2,1,0:T(8,128)}, f32[2,2,8,32,128]{4,3,2,1,0:T(8,128)}) custom-call(s32[8]{0:T(128)} %get-tuple-element.149.places_ref, s32[1]{0:T(128)} %bitcast.5.special_ref, f32[8,2,8,32,128]{4,3,2,1,0:T(8,128)} %bitcast.6.planes_ref, ...), custom_call_target="tpu_custom_call" | custom-call | flops 3221225472 | bytes 5242880 | tf_op jit(solution)/shard_map/filter_planes/pallas_call | solution.py:224
  193.3 0.1 pad_maximum_fusion.1
  193.4 0.4 collective-permute-start.10
  193.8 0.3 copy-done.12
  194.1 1.2 collective-permute-start.7
  195.3 1.2 collective-permute-start.8
  196.5 0.2 collective-permute-start.9
  196.9 7.5 %backward_last.2.refs_6_ = f32[32,128,256]{2,1,0:T(8,128)} custom-call(f32[2,32,128,256]{3,2,1,0:T(8,128)} %cosine_factors.1.refs_0_, bf16[192,256]{1,0:T(8,128)(2,1)S(1)} %pad_maximum_fusion.8.refs_1_, f32[4,2,8,32,128]{4,3,2,1,0:T(8,128)S(1)} %pad_maximum_fusion.refs_2_, f32[4,2,8,32,128]{4,3,2,1,0:T(8,128)S(1)} %collective-permute-done.10.refs_3_), custom_call_target="tpu_custom_call" | custom-call | flops 805306368 | bytes 18874368 | tf_op jit(solution)/shard_map/backward_last/pallas_call | solution.py:321
  204.4 20.1 %collective-permute-done.7 = f32[2,2,8,32,128]{4,3,2,1,0:T(8,128)S(1)} collective-permute-done((f32[2,2,8,32,128]{4,3,2,1,0:T(8,128)S(1)}, f32[2,2,8,32,128]{4,3,2,1,0:T(8,128)S(1)}, u32[]{:S(2)}, u32[]{:S(2)}) %collective-permute-start.7) | collective-permute-done | bytes 524320 | tf_op jit(solution)/shard_map/ppermute | solution.py:683
  224.5 41.5 %collective-permute-done.8 = f32[2,2,8,32,128]{4,3,2,1,0:T(8,128)S(1)} collective-permute-done((f32[2,2,8,32,128]{4,3,2,1,0:T(8,128)S(1)}, f32[2,2,8,32,128]{4,3,2,1,0:T(8,128)S(1)}, u32[]{:S(2)}, u32[]{:S(2)}) %collective-permute-start.8) | collective-permute-done | bytes 524320 | tf_op jit(solution)/shard_map/ppermute | solution.py:683
  266.0 17.5 %collective-permute-done.9 = f32[2,2,8,32,128]{4,3,2,1,0:T(8,128)S(1)} collective-permute-done((f32[2,2,8,32,128]{4,3,2,1,0:T(8,128)S(1)}, f32[2,2,8,32,128]{4,3,2,1,0:T(8,128)S(1)}, u32[]{:S(2)}, u32[]{:S(2)}) %collective-permute-start.9) | collective-permute-done | bytes 524320 | tf_op jit(solution)/shard_map/ppermute | solution.py:683
  283.7 0.1 pad_maximum_fusion.3
  283.8 1.2 collective-permute-start.11
  285.0 0.1 pad_maximum_fusion.2.refs_3_
  285.1 2.2 collective-permute-done.11.refs_4_
  287.3 10.1 %backward_last.3 = f32[32,128,256]{2,1,0:T(8,128)} custom-call(f32[2,32,128,256]{3,2,1,0:T(8,128)} %cosine_factors.1.refs_0_, bf16[192,256]{1,0:T(8,128)(2,1)S(1)} %pad_maximum_fusion.9.refs_1_, bf16[384,256]{1,0:T(8,128)(2,1)S(1)} %copy-done, f32[4,2,8,32,128]{4,3,2,1,0:T(8,128)S(1)} %pad_maximum_fusion.2.refs_3_, ...), custom_call_target="tpu_custom_call" | custom-call | flops 2415919104 | bytes 23068672 | tf_op jit(solution)/shard_map/backward_last/pallas_call | solution.py:321
  (53 shorter events, 0.6 us)
Async XLA Ops:
  1.4 10.3 %collective-permute-start = (f32[2,129,256]{2,1,0:T(8,128)S(1)}, f32[2,129,256]{2,1,0:T(8,128)S(1)}, u32[]{:S(2)}, u32[]{:S(2)}) collective-permute-start(f32[2,129,256]{2,1,0:T(8,128)S(1)} %fusion.18), channel_id=1, source_target_pairs={{0,8},{8,0},{1,9},{9,1},{16,24},{24,16},{17,25},{25,17}} | collective-permute-start | bytes 792584 | tf_op jit(solution)/shard_map/ppermute | solution.py:592
  11.8 0.7 copy-start.6
  11.8 6.6 %copy-start.13 = (s32[8]{0:T(128)S(1)}, s32[8]{0:T(128)}, u32[]{:S(2)}) copy-start(s32[8]{0:T(128)} %param.18) | copy-start | bytes 100
  11.8 6.6 %copy-start.14 = (s32[2]{0:T(128)S(1)}, s32[2]{0:T(128)}, u32[]{:S(2)}) copy-start(s32[2]{0:T(128)} %param.19) | copy-start | bytes 28
  12.5 102.6 %all-to-all-start.1 = ((f32[16,16,32,128]{3,2,1,0:T(8,128)}), f32[16,16,32,128]{3,2,1,0:T(8,128)}, u32[]{:S(2)}, u32[]{:S(2)}) async-start(f32[16,16,32,128]{3,2,1,0:T(8,128)} %bitcast.15), calls=%async_computation.1 | async-start | bytes 8388608 | tf_op jit(solution)/shard_map/all_to_all | solution.py:619
  21.3 9.8 %copy-start.8 = (s32[8,8]{1,0:T(8,128)S(1)}, s32[8,8]{1,0:T(8,128)}, u32[]{:S(2)}) copy-start(s32[8,8]{1,0:T(8,128)} %constant.168.clone) | copy-start | bytes 772
  21.3 10.4 %copy-start.7 = (s32[8,8]{1,0:T(8,128)S(1)}, s32[8,8]{1,0:T(8,128)}, u32[]{:S(2)}) copy-start(s32[8,8]{1,0:T(8,128)} %constant.167.clone) | copy-start | bytes 772
  32.4 25.2 %collective-permute-start.1 = (f32[13,72,128]{2,1,0:T(8,128)}, f32[13,72,128]{2,1,0:T(8,128)S(1)}, u32[]{:S(2)}, u32[]{:S(2)}) collective-permute-start(f32[13,72,128]{2,1,0:T(8,128)} %get-tuple-element.73), channel_id=1, source_target_pairs={{0,2},{2,0},{4,6},{6,4},{8,10},{10,8},{12,14},{14,12},{1,3},{3,1},... | collective-permute-start | bytes 1437704 | tf_op jit(solution)/shard_map/ppermute | solution.py:388
  33.6 64.9 %collective-permute-start.2 = (f32[13,72,128]{2,1,0:T(8,128)}, f32[13,72,128]{2,1,0:T(8,128)S(1)}, u32[]{:S(2)}, u32[]{:S(2)}) collective-permute-start(f32[13,72,128]{2,1,0:T(8,128)} %get-tuple-element.74), channel_id=1, source_target_pairs={{0,4},{2,6},{4,0},{6,2},{8,12},{10,14},{12,8},{14,10},{1,5},{3,7},... | collective-permute-start | bytes 1437704 | tf_op jit(solution)/shard_map/ppermute | solution.py:388
  34.8 79.0 %collective-permute-start.3 = (f32[13,72,128]{2,1,0:T(8,128)}, f32[13,72,128]{2,1,0:T(8,128)S(1)}, u32[]{:S(2)}, u32[]{:S(2)}) collective-permute-start(f32[13,72,128]{2,1,0:T(8,128)} %get-tuple-element.75), channel_id=1, source_target_pairs={{0,6},{2,4},{4,2},{6,0},{8,14},{10,12},{12,10},{14,8},{1,7},{3,5},... | collective-permute-start | bytes 1437704 | tf_op jit(solution)/shard_map/ppermute | solution.py:388
  44.1 5.9 %copy-start.9 = (s32[256]{0:T(256)S(1)}, s32[256]{0:T(256)}, u32[]{:S(2)}) copy-start(s32[256]{0:T(256)} %constant.166.clone) | copy-start | bytes 3076
  57.5 63.3 %copy-start.1 = (f32[13,72,128]{2,1,0:T(8,128)}, f32[13,72,128]{2,1,0:T(8,128)S(1)}, u32[]{:S(2)}) copy-start(f32[13,72,128]{2,1,0:T(8,128)S(1)} %collective-permute-done.1.refs_1_.refs_5_.refs_9_.refs_13_) | copy-start | bytes 1437700
  98.5 22.3 %copy-start.2 = (f32[13,72,128]{2,1,0:T(8,128)}, f32[13,72,128]{2,1,0:T(8,128)S(1)}, u32[]{:S(2)}) copy-start(f32[13,72,128]{2,1,0:T(8,128)S(1)} %collective-permute-done.2.refs_2_.refs_6_.refs_10_.refs_14_) | copy-start | bytes 1437700
  113.8 7.0 %copy-start.3 = (f32[13,72,128]{2,1,0:T(8,128)}, f32[13,72,128]{2,1,0:T(8,128)S(1)}, u32[]{:S(2)}) copy-start(f32[13,72,128]{2,1,0:T(8,128)S(1)} %collective-permute-done.3.refs_3_.refs_7_.refs_11_.refs_15_) | copy-start | bytes 1437700
  115.1 64.7 %all-to-all-start = ((f32[16,8,32,128]{3,2,1,0:T(8,128)}), f32[16,8,32,128]{3,2,1,0:T(8,128)}, u32[]{:S(2)}, u32[]{:S(2)}) async-start(f32[16,8,32,128]{3,2,1,0:T(8,128)} %bitcast.16), calls=%async_computation | async-start | bytes 4194304 | tf_op jit(solution)/shard_map/all_to_all | solution.py:619
  128.8 20.0 %collective-permute-start.4 = (f32[2,2,8,32,128]{4,3,2,1,0:T(8,128)}, f32[2,2,8,32,128]{4,3,2,1,0:T(8,128)S(1)}, u32[]{:S(2)}, u32[]{:S(2)}) collective-permute-start(f32[2,2,8,32,128]{4,3,2,1,0:T(8,128)} %get-tuple-element.101), channel_id=1, source_target_pairs={{0,2},{2,0},{4,6},{6,4},{8,10},{10,8},{12,14},{14,12},{1,3},{3,1},... | collective-permute-start | bytes 1572872 | tf_op jit(solution)/shard_map/ppermute | solution.py:683
  130.1 37.5 %collective-permute-start.5 = (f32[2,2,8,32,128]{4,3,2,1,0:T(8,128)}, f32[2,2,8,32,128]{4,3,2,1,0:T(8,128)S(1)}, u32[]{:S(2)}, u32[]{:S(2)}) collective-permute-start(f32[2,2,8,32,128]{4,3,2,1,0:T(8,128)} %get-tuple-element.102), channel_id=1, source_target_pairs={{0,4},{2,6},{4,0},{6,2},{8,12},{10,14},{12,8},{14,10},{1,5},{3,7},... | collective-permute-start | bytes 1572872 | tf_op jit(solution)/shard_map/ppermute | solution.py:683
  131.3 48.5 %collective-permute-start.6 = (f32[2,2,8,32,128]{4,3,2,1,0:T(8,128)}, f32[2,2,8,32,128]{4,3,2,1,0:T(8,128)S(1)}, u32[]{:S(2)}, u32[]{:S(2)}) collective-permute-start(f32[2,2,8,32,128]{4,3,2,1,0:T(8,128)} %get-tuple-element.103), channel_id=1, source_target_pairs={{0,6},{2,4},{4,2},{6,0},{8,14},{10,12},{12,10},{14,8},{1,7},{3,5},... | collective-permute-start | bytes 1572872 | tf_op jit(solution)/shard_map/ppermute | solution.py:683
  179.8 107.5 %all-to-all-start.2 = ((f32[16,2,8,32,128]{4,3,2,1,0:T(8,128)}), f32[16,2,8,32,128]{4,3,2,1,0:T(8,128)}, u32[]{:S(2)}, u32[]{:S(2)}) async-start(f32[16,2,8,32,128]{4,3,2,1,0:T(8,128)} %bitcast.17), calls=%async_computation.2 | async-start | bytes 8388608 | tf_op jit(solution)/shard_map/all_to_all | solution.py:619
  184.9 8.2 %copy-start.5 = (f32[2,2,8,32,128]{4,3,2,1,0:T(8,128)S(1)}, f32[2,2,8,32,128]{4,3,2,1,0:T(8,128)}, u32[]{:S(2)}) copy-start(f32[2,2,8,32,128]{4,3,2,1,0:T(8,128)} %get-tuple-element.113) | copy-start | bytes 1572868
  193.1 1.0 copy-start.12
  193.1 2.2 copy-start.11
  193.1 3.4 %copy-start.10 = (f32[2,2,8,32,128]{4,3,2,1,0:T(8,128)S(1)}, f32[2,2,8,32,128]{4,3,2,1,0:T(8,128)}, u32[]{:S(2)}) copy-start(f32[2,2,8,32,128]{4,3,2,1,0:T(8,128)} %get-tuple-element.111) | copy-start | bytes 1572868
  193.4 3.5 %collective-permute-start.10 = (f32[4,2,8,32,128]{4,3,2,1,0:T(8,128)S(1)}, f32[4,2,8,32,128]{4,3,2,1,0:T(8,128)S(1)}, u32[]{:S(2)}, u32[]{:S(2)}) collective-permute-start(f32[4,2,8,32,128]{4,3,2,1,0:T(8,128)S(1)} %pad_maximum_fusion.1), channel_id=1, source_target_pairs={{0,1},{1,0},{2,3},{3,2},{4,5},{5,4},{6,7},{7,6},{8,9},{9,8},{10,11... | collective-permute-start | bytes 3145736 | tf_op jit(solution)/shard_map/ppermute | solution.py:692
  194.1 30.4 %collective-permute-start.7 = (f32[2,2,8,32,128]{4,3,2,1,0:T(8,128)S(1)}, f32[2,2,8,32,128]{4,3,2,1,0:T(8,128)S(1)}, u32[]{:S(2)}, u32[]{:S(2)}) collective-permute-start(f32[2,2,8,32,128]{4,3,2,1,0:T(8,128)S(1)} %copy-done.12), channel_id=1, source_target_pairs={{0,2},{2,0},{4,6},{6,4},{8,10},{10,8},{12,14},{14,12},{1,3},{3,1},... | collective-permute-start | bytes 1572872 | tf_op jit(solution)/shard_map/ppermute | solution.py:683
  195.3 70.7 %collective-permute-start.8 = (f32[2,2,8,32,128]{4,3,2,1,0:T(8,128)S(1)}, f32[2,2,8,32,128]{4,3,2,1,0:T(8,128)S(1)}, u32[]{:S(2)}, u32[]{:S(2)}) collective-permute-start(f32[2,2,8,32,128]{4,3,2,1,0:T(8,128)S(1)} %copy-done.11), channel_id=1, source_target_pairs={{0,4},{2,6},{4,0},{6,2},{8,12},{10,14},{12,8},{14,10},{1,5},{3,7},... | collective-permute-start | bytes 1572872 | tf_op jit(solution)/shard_map/ppermute | solution.py:683
  196.5 87.0 %collective-permute-start.9 = (f32[2,2,8,32,128]{4,3,2,1,0:T(8,128)S(1)}, f32[2,2,8,32,128]{4,3,2,1,0:T(8,128)S(1)}, u32[]{:S(2)}, u32[]{:S(2)}) collective-permute-start(f32[2,2,8,32,128]{4,3,2,1,0:T(8,128)S(1)} %copy-done.10), channel_id=1, source_target_pairs={{0,6},{2,4},{4,2},{6,0},{8,14},{10,12},{12,10},{14,8},{1,7},{3,5},... | collective-permute-start | bytes 1572872 | tf_op jit(solution)/shard_map/ppermute | solution.py:683
  196.9 86.7 %copy-start.4 = (f32[2,2,8,32,128]{4,3,2,1,0:T(8,128)S(1)}, f32[2,2,8,32,128]{4,3,2,1,0:T(8,128)}, u32[]{:S(2)}) copy-start(f32[2,2,8,32,128]{4,3,2,1,0:T(8,128)} %get-tuple-element.117) | copy-start | bytes 1572868
  204.4 82.9 %copy-start = (bf16[384,256]{1,0:T(8,128)(2,1)S(1)}, bf16[384,256]{1,0:T(8,128)(2,1)}, u32[]{:S(2)}) copy-start(bf16[384,256]{1,0:T(8,128)(2,1)} %constant.169.clone.refs_2_) | copy-start | bytes 589828
  283.8 3.5 %collective-permute-start.11 = (f32[4,2,8,32,128]{4,3,2,1,0:T(8,128)S(1)}, f32[4,2,8,32,128]{4,3,2,1,0:T(8,128)S(1)}, u32[]{:S(2)}, u32[]{:S(2)}) collective-permute-start(f32[4,2,8,32,128]{4,3,2,1,0:T(8,128)S(1)} %pad_maximum_fusion.3), channel_id=1, source_target_pairs={{0,1},{1,0},{2,3},{3,2},{4,5},{5,4},{6,7},{7,6},{8,9},{9,8},{10,11... | collective-permute-start | bytes 3145736 | tf_op jit(solution)/shard_map/ppermute | solution.py:692

commit v5 on v4

--- a/solution.py
+++ b/solution.py
@@ -280,7 +280,11 @@
                 for source in range(sources):
                     row = (source * slots + slot) * depth * block + site
                     found.append(flats[index][pl.ds(row, depth, stride=block), :])
-            return jnp.concatenate(found, axis=0).T
+            value = jnp.concatenate(found, axis=0)
+            if value.shape[0] * 2 != rows_two:
+                return value.T
+            high = value.astype(jnp.bfloat16).astype(jnp.float32)
+            return jnp.concatenate([high, value - high], axis=0).T
 
         for start in range(0, block, 2):
             result = None
@@ -293,7 +297,18 @@
                         [columns(slot, start + inner, first, last) for inner in range(2)],
                         axis=0,
                     )
-                    value = right_dot(value, table_ref[...])
+                    if value.shape[1] * 3 == table_ref.shape[0]:
+                        value = right_dot(value, table_ref[...])
+                    else:
+                        value = value.astype(jnp.bfloat16)
+                        value = jnp.dot(
+                            jnp.concatenate([value, value], axis=1),
+                            jnp.concatenate(
+                                [table_ref[...], jnp.zeros_like(table_ref[: value.shape[1] // 2])],
+                                axis=0,
+                            ),
+                            preferred_element_type=jnp.float32,
+                        )
                     field = value if field is None else field + value
                     first = last
                 field = field.reshape(2, rows_two, length)

time: 298 us -> 298 us (level)
  no operation moved by 1% of the time
where the time goes in v5:
time: 298 us; the launch traced here: 297 us
  waiting for transfers between devices  180 us (60%)
  Pallas kernels  72.5 us (24%)
  starting transfers between devices  27.6 us (9%)
  other arithmetic  9.74 us (3%)
  local copies, waits for them, and re-layouts  6.46 us (2%)
    ppermute x6, waiting for transfers between devices, shared_rows(): lax.ppermute(pieces[delta], 'px', swap_pairs(width_px, half_px, delta))  118 us
    ppermute x3, waiting for transfers between devices, send_messages(): lax.ppermute(message[delta], 'px', swap_pairs(width_px, half_px, delta))  56.3 us
    pallas_call x3, Pallas kernels, filter_planes(): pl.pallas_call(body, grid_spec=pltpu.PrefetchScalarGridSpec(num_scalar_pr...  26 us
    pallas_call x2, Pallas kernels, backward_last(): pl.pallas_call(body, grid=(rows_one // block,), in_specs=in_specs, out_sp...  16.4 us
    all_to_all x3, starting transfers between devices, exchange(): return lax.all_to_all(value, ('px', 'py'), 0, 0, tiled=True)  16 us
    pallas_call x2, Pallas kernels, forward_last(): pl.pallas_call(body, grid=(rows_one // block,), in_specs=[pl.BlockSpec((b...  11.6 us
    pallas_call x1, Pallas kernels, message_rows(): pl.pallas_call(body, grid=(1,), in_specs=[pl.BlockSpec(part, lambda i: (0...  9.41 us
    pallas_call x1, Pallas kernels, cosine_factors(): pl.pallas_call(body, grid=(rows_one // block,), in_specs=[pl.BlockSpec(me...  9.08 us
  transfers between devices with their start and end apart: 15, of which 11 were waited for; matrix products, arithmetic and copies ran while one was open for 5% of the time, Pallas kernels for 21%

profile of v5, /device:TPU:21, one launch (start us, length us, event | category | flops | bytes accessed | tf_op | source)
XLA Modules:
  0.0 297.0 jit_solution(10588148569294527579)
XLA Ops:
  0.0 1.4 slice.60
  1.4 2.0 collective-permute-start
  3.4 6.1 %forward_last.2 = f32[256,32,128]{2,1,0:T(8,128)} custom-call(f32[32,128,256]{2,1,0:T(8,128)} %adjoint_ref.2, bf16[192,768]{1,0:T(8,128)(2,1)} %constant.161.clone.table_ref), custom_call_target="tpu_custom_call" | custom-call | flops 1207959552 | bytes 8388608 | tf_op jit(solution)/shard_map/forward_last/pallas_call | solution.py:108
  9.5 2.3 collective-permute-done.edge_ref
  11.8 0.7 copy-done.6
  12.5 5.8 %all-to-all-start.1 = ((f32[16,16,32,128]{3,2,1,0:T(8,128)}), f32[16,16,32,128]{3,2,1,0:T(8,128)}, u32[]{:S(2)}, u32[]{:S(2)}) async-start(f32[16,16,32,128]{3,2,1,0:T(8,128)} %bitcast.15), calls=%async_computation.1 | async-start | bytes 8388608 | tf_op jit(solution)/shard_map/all_to_all | solution.py:634
  18.4 0.2 fusion.38
  18.5 0.5 convert_element_type.45.chosen_ref
  19.1 0.7 dynamic-slice_reduce_fusion
  19.8 0.1 reshape_squeeze.3
  19.9 0.1 eq.55
  19.9 0.7 dynamic-slice_bitcast_fusion
  20.6 0.7 fusion.37.select_ref
  21.3 9.4 %message_rows.1 = (f32[13,72,128]{2,1,0:T(8,128)}, f32[13,72,128]{2,1,0:T(8,128)}, f32[13,72,128]{2,1,0:T(8,128)}, f32[13,72,128]{2,1,0:T(8,128)}) custom-call(bf16[2,256,32,256]{3,2,1,0:T(8,128)(2,1)} %spectra_ref, f32[2,129,256]{2,1,0:T(8,128)} %copy-done.6, bf16[64,256]{1,0:T(8,128)(2,1)} %fusion.37.select_ref), custom_call_target="tpu_custom_call" | custom-call | flops 268435456 | bytes 6144000 | tf_op jit(solution)/shard_map/message_rows/pallas_call | solution.py:485
  30.8 0.1 broadcast_add_fusion
  30.8 0.1 add.212
  31.0 0.1 add.192
  31.1 0.6 gather_fusion.1
  31.7 0.1 mul.152
  31.7 0.6 gather_fusion
  32.3 0.1 mul.148
  32.4 1.2 collective-permute-start.1
  33.6 1.2 collective-permute-start.2
  34.8 0.2 collective-permute-start.3
  35.0 9.1 %cosine_factors.1.refs_0_ = f32[2,32,128,256]{3,2,1,0:T(8,128)} custom-call(f32[2]{0:T(128)} %convert_element_type.45.chosen_ref, f32[32,128,256]{2,1,0:T(8,128)} %saved_ref), custom_call_target="tpu_custom_call" | custom-call | flops 50331648 | bytes 12582912 | tf_op jit(solution)/shard_map/cosine_factors/pallas_call | solution.py:378
  44.1 5.5 %forward_last.3 = f32[128,32,128]{2,1,0:T(8,128)} custom-call(f32[32,128,256]{2,1,0:T(8,128)} %adjoint_ref.2, bf16[64,768]{1,0:T(8,128)(2,1)} %constant.170.clone.table_ref), custom_call_target="tpu_custom_call" | custom-call | flops 402653184 | bytes 6291456 | tf_op jit(solution)/shard_map/forward_last/pallas_call | solution.py:108
  49.7 0.3 reduce-precision_convert_fusion.5
  50.0 0.6 reduce-precision_convert_fusion.3
  50.7 0.7 pad_maximum_fusion.7.refs_18_
  51.4 0.3 reduce-precision_convert_fusion.4
  51.7 3.4 %reduce-precision_convert_fusion = (bf16[256,256]{1,0:T(8,128)(2,1)S(1)}, bf16[256,256]{1,0:T(8,128)(2,1)S(1)}, bf16[256,256]{1,0:T(8,128)(2,1)S(1)}, bf16[256,2...) fusion(s32[256]{0:T(256)S(1)} %and_select_fusion.1, s32[256]{0:T(256)S(1)} %pad_add_fusion), kind=kLoop, calls=%fused_computation.21 | loop fusion | flops 3735552 | bytes 788480 | tf_op jit(solution)/shard_map/convert.7
  55.2 0.8 pad_maximum_fusion.6.refs_19_
  55.9 0.8 pad_maximum_fusion.4.refs_17_
  56.7 0.8 pad_maximum_fusion.5.refs_19_
  57.5 40.9 %collective-permute-done.2.refs_2_.refs_6_.refs_10_.refs_14_ = f32[13,72,128]{2,1,0:T(8,128)S(1)} collective-permute-done((f32[13,72,128]{2,1,0:T(8,128)}, f32[13,72,128]{2,1,0:T(8,128)S(1)}, u32[]{:S(2)}, u32[]{:S(2)}) %collective-permute-start.2) | collective-permute-done | bytes 479264 | tf_op jit(solution)/shard_map/ppermute | solution.py:403
  98.5 15.3 %collective-permute-done.3.refs_3_.refs_7_.refs_11_.refs_15_ = f32[13,72,128]{2,1,0:T(8,128)S(1)} collective-permute-done((f32[13,72,128]{2,1,0:T(8,128)}, f32[13,72,128]{2,1,0:T(8,128)S(1)}, u32[]{:S(2)}, u32[]{:S(2)}) %collective-permute-start.3) | collective-permute-done | bytes 479264 | tf_op jit(solution)/shard_map/ppermute | solution.py:403
  113.8 1.3 all-to-all-done.1
  115.1 5.0 %all-to-all-start = ((f32[16,8,32,128]{3,2,1,0:T(8,128)}), f32[16,8,32,128]{3,2,1,0:T(8,128)}, u32[]{:S(2)}, u32[]{:S(2)}) async-start(f32[16,8,32,128]{3,2,1,0:T(8,128)} %bitcast.16), calls=%async_computation | async-start | bytes 4194304 | tf_op jit(solution)/shard_map/all_to_all | solution.py:634
  120.2 0.6 fusion.54
  120.8 8.0 %filter_planes.5 = (f32[2,2,8,32,128]{4,3,2,1,0:T(8,128)}, f32[2,2,8,32,128]{4,3,2,1,0:T(8,128)}, f32[2,2,8,32,128]{4,3,2,1,0:T(8,128)}, f32[2,2,8,32,128]{4,3,2,1,0:T(8,128)}) custom-call(s32[8]{0:T(128)} %get-tuple-element.147.places_ref, s32[1]{0:T(128)} %bitcast.5.special_ref, f32[8,2,16,32,128]{4,3,2,1,0:T(8,128)} %bitcast.7.planes_ref, ...), custom_call_target="tpu_custom_call" | custom-call | flops 3221225472 | bytes 5242880 | tf_op jit(solution)/shard_map/filter_planes/pallas_call | solution.py:224
  128.8 1.2 collective-permute-start.4
  130.1 1.2 collective-permute-start.5
  131.3 0.3 collective-permute-start.6
  131.6 9.8 %filter_planes.4 = f32[8,2,2,8,32,128]{5,4,3,2,1,0:T(8,128)} custom-call(s32[8]{0:T(128)} %get-tuple-element.148.places_ref, s32[1]{0:T(128)} %bitcast.5.special_ref, f32[8,2,16,32,128]{4,3,2,1,0:T(8,128)} %bitcast.7.planes_ref, f32[13,72,128]{2,1,0:T(8,128)} %get-tuple-element.83.refs_0_.refs_4_.refs_8_.refs_12_, f32[13,72,128]{2,1,0:T(8,128)} %copy-done.1, ...), custom_call_target="tpu_custom_call" | custom-call | flops 4831838208 | bytes 7340032 | tf_op jit(solution)/shard_map/filter_planes/pallas_call | solution.py:224
  141.4 7.4 %collective-permute-done.4 = f32[2,2,8,32,128]{4,3,2,1,0:T(8,128)S(1)} collective-permute-done((f32[2,2,8,32,128]{4,3,2,1,0:T(8,128)}, f32[2,2,8,32,128]{4,3,2,1,0:T(8,128)S(1)}, u32[]{:S(2)}, u32[]{:S(2)}) %collective-permute-start.4) | collective-permute-done | bytes 524320 | tf_op jit(solution)/shard_map/ppermute | solution.py:698
  148.8 18.7 %collective-permute-done.5 = f32[2,2,8,32,128]{4,3,2,1,0:T(8,128)S(1)} collective-permute-done((f32[2,2,8,32,128]{4,3,2,1,0:T(8,128)}, f32[2,2,8,32,128]{4,3,2,1,0:T(8,128)S(1)}, u32[]{:S(2)}, u32[]{:S(2)}) %collective-permute-start.5) | collective-permute-done | bytes 524320 | tf_op jit(solution)/shard_map/ppermute | solution.py:698
  167.5 12.2 %collective-permute-done.6 = f32[2,2,8,32,128]{4,3,2,1,0:T(8,128)S(1)} collective-permute-done((f32[2,2,8,32,128]{4,3,2,1,0:T(8,128)}, f32[2,2,8,32,128]{4,3,2,1,0:T(8,128)S(1)}, u32[]{:S(2)}, u32[]{:S(2)}) %collective-permute-start.6) | collective-permute-done | bytes 524320 | tf_op jit(solution)/shard_map/ppermute | solution.py:698
  179.8 5.1 %all-to-all-start.2 = ((f32[16,2,8,32,128]{4,3,2,1,0:T(8,128)}), f32[16,2,8,32,128]{4,3,2,1,0:T(8,128)}, u32[]{:S(2)}, u32[]{:S(2)}) async-start(f32[16,2,8,32,128]{4,3,2,1,0:T(8,128)} %bitcast.17), calls=%async_computation.2 | async-start | bytes 8388608 | tf_op jit(solution)/shard_map/all_to_all | solution.py:634
  184.9 8.1 %filter_planes.3 = (f32[2,2,8,32,128]{4,3,2,1,0:T(8,128)}, f32[2,2,8,32,128]{4,3,2,1,0:T(8,128)}, f32[2,2,8,32,128]{4,3,2,1,0:T(8,128)}, f32[2,2,8,32,128]{4,3,2,1,0:T(8,128)}) custom-call(s32[8]{0:T(128)} %get-tuple-element.149.places_ref, s32[1]{0:T(128)} %bitcast.5.special_ref, f32[8,2,8,32,128]{4,3,2,1,0:T(8,128)} %bitcast.6.planes_ref, ...), custom_call_target="tpu_custom_call" | custom-call | flops 3221225472 | bytes 5242880 | tf_op jit(solution)/shard_map/filter_planes/pallas_call | solution.py:224
  193.3 0.1 pad_maximum_fusion.1
  193.4 0.4 collective-permute-start.10
  193.8 0.3 copy-done.12
  194.1 1.2 collective-permute-start.7
  195.3 1.2 collective-permute-start.8
  196.5 0.2 collective-permute-start.9
  196.9 6.7 %backward_last.2.refs_6_ = f32[32,128,256]{2,1,0:T(8,128)} custom-call(f32[2,32,128,256]{3,2,1,0:T(8,128)} %cosine_factors.1.refs_0_, bf16[192,256]{1,0:T(8,128)(2,1)S(1)} %pad_maximum_fusion.8.refs_1_, f32[4,2,8,32,128]{4,3,2,1,0:T(8,128)S(1)} %pad_maximum_fusion.refs_2_, f32[4,2,8,32,128]{4,3,2,1,0:T(8,128)S(1)} %collective-permute-done.10.refs_3_), custom_call_target="tpu_custom_call" | custom-call | flops 805306368 | bytes 18874368 | tf_op jit(solution)/shard_map/backward_last/pallas_call | solution.py:336
  203.5 21.0 %collective-permute-done.7 = f32[2,2,8,32,128]{4,3,2,1,0:T(8,128)S(1)} collective-permute-done((f32[2,2,8,32,128]{4,3,2,1,0:T(8,128)S(1)}, f32[2,2,8,32,128]{4,3,2,1,0:T(8,128)S(1)}, u32[]{:S(2)}, u32[]{:S(2)}) %collective-permute-start.7) | collective-permute-done | bytes 524320 | tf_op jit(solution)/shard_map/ppermute | solution.py:698
  224.5 41.5 %collective-permute-done.8 = f32[2,2,8,32,128]{4,3,2,1,0:T(8,128)S(1)} collective-permute-done((f32[2,2,8,32,128]{4,3,2,1,0:T(8,128)S(1)}, f32[2,2,8,32,128]{4,3,2,1,0:T(8,128)S(1)}, u32[]{:S(2)}, u32[]{:S(2)}) %collective-permute-start.8) | collective-permute-done | bytes 524320 | tf_op jit(solution)/shard_map/ppermute | solution.py:698
  266.0 17.5 %collective-permute-done.9 = f32[2,2,8,32,128]{4,3,2,1,0:T(8,128)S(1)} collective-permute-done((f32[2,2,8,32,128]{4,3,2,1,0:T(8,128)S(1)}, f32[2,2,8,32,128]{4,3,2,1,0:T(8,128)S(1)}, u32[]{:S(2)}, u32[]{:S(2)}) %collective-permute-start.9) | collective-permute-done | bytes 524320 | tf_op jit(solution)/shard_map/ppermute | solution.py:698
  283.7 0.1 pad_maximum_fusion.3
  283.8 1.2 collective-permute-start.11
  285.0 0.1 pad_maximum_fusion.2.refs_3_
  285.1 2.2 collective-permute-done.11.refs_4_
  287.3 9.7 %backward_last.3 = f32[32,128,256]{2,1,0:T(8,128)} custom-call(f32[2,32,128,256]{3,2,1,0:T(8,128)} %cosine_factors.1.refs_0_, bf16[192,256]{1,0:T(8,128)(2,1)S(1)} %pad_maximum_fusion.9.refs_1_, bf16[384,256]{1,0:T(8,128)(2,1)S(1)} %copy-done, f32[4,2,8,32,128]{4,3,2,1,0:T(8,128)S(1)} %pad_maximum_fusion.2.refs_3_, ...), custom_call_target="tpu_custom_call" | custom-call | flops 2415919104 | bytes 23068672 | tf_op jit(solution)/shard_map/backward_last/pallas_call | solution.py:336
  (53 shorter events, 0.6 us)
Async XLA Ops:
  1.4 10.3 %collective-permute-start = (f32[2,129,256]{2,1,0:T(8,128)S(1)}, f32[2,129,256]{2,1,0:T(8,128)S(1)}, u32[]{:S(2)}, u32[]{:S(2)}) collective-permute-start(f32[2,129,256]{2,1,0:T(8,128)S(1)} %fusion.18), channel_id=1, source_target_pairs={{0,8},{8,0},{1,9},{9,1},{16,24},{24,16},{17,25},{25,17}} | collective-permute-start | bytes 792584 | tf_op jit(solution)/shard_map/ppermute | solution.py:607
  11.8 0.7 copy-start.6
  11.8 6.6 %copy-start.13 = (s32[8]{0:T(128)S(1)}, s32[8]{0:T(128)}, u32[]{:S(2)}) copy-start(s32[8]{0:T(128)} %param.18) | copy-start | bytes 100
  11.8 6.6 %copy-start.14 = (s32[2]{0:T(128)S(1)}, s32[2]{0:T(128)}, u32[]{:S(2)}) copy-start(s32[2]{0:T(128)} %param.19) | copy-start | bytes 28
  12.5 102.6 %all-to-all-start.1 = ((f32[16,16,32,128]{3,2,1,0:T(8,128)}), f32[16,16,32,128]{3,2,1,0:T(8,128)}, u32[]{:S(2)}, u32[]{:S(2)}) async-start(f32[16,16,32,128]{3,2,1,0:T(8,128)} %bitcast.15), calls=%async_computation.1 | async-start | bytes 8388608 | tf_op jit(solution)/shard_map/all_to_all | solution.py:634
  21.3 9.8 %copy-start.8 = (s32[8,8]{1,0:T(8,128)S(1)}, s32[8,8]{1,0:T(8,128)}, u32[]{:S(2)}) copy-start(s32[8,8]{1,0:T(8,128)} %constant.168.clone) | copy-start | bytes 772
  21.3 10.4 %copy-start.7 = (s32[8,8]{1,0:T(8,128)S(1)}, s32[8,8]{1,0:T(8,128)}, u32[]{:S(2)}) copy-start(s32[8,8]{1,0:T(8,128)} %constant.167.clone) | copy-start | bytes 772
  32.4 25.2 %collective-permute-start.1 = (f32[13,72,128]{2,1,0:T(8,128)}, f32[13,72,128]{2,1,0:T(8,128)S(1)}, u32[]{:S(2)}, u32[]{:S(2)}) collective-permute-start(f32[13,72,128]{2,1,0:T(8,128)} %get-tuple-element.73), channel_id=1, source_target_pairs={{0,2},{2,0},{4,6},{6,4},{8,10},{10,8},{12,14},{14,12},{1,3},{3,1},... | collective-permute-start | bytes 1437704 | tf_op jit(solution)/shard_map/ppermute | solution.py:403
  33.6 64.9 %collective-permute-start.2 = (f32[13,72,128]{2,1,0:T(8,128)}, f32[13,72,128]{2,1,0:T(8,128)S(1)}, u32[]{:S(2)}, u32[]{:S(2)}) collective-permute-start(f32[13,72,128]{2,1,0:T(8,128)} %get-tuple-element.74), channel_id=1, source_target_pairs={{0,4},{2,6},{4,0},{6,2},{8,12},{10,14},{12,8},{14,10},{1,5},{3,7},... | collective-permute-start | bytes 1437704 | tf_op jit(solution)/shard_map/ppermute | solution.py:403
  34.8 79.0 %collective-permute-start.3 = (f32[13,72,128]{2,1,0:T(8,128)}, f32[13,72,128]{2,1,0:T(8,128)S(1)}, u32[]{:S(2)}, u32[]{:S(2)}) collective-permute-start(f32[13,72,128]{2,1,0:T(8,128)} %get-tuple-element.75), channel_id=1, source_target_pairs={{0,6},{2,4},{4,2},{6,0},{8,14},{10,12},{12,10},{14,8},{1,7},{3,5},... | collective-permute-start | bytes 1437704 | tf_op jit(solution)/shard_map/ppermute | solution.py:403
  44.1 5.9 %copy-start.9 = (s32[256]{0:T(256)S(1)}, s32[256]{0:T(256)}, u32[]{:S(2)}) copy-start(s32[256]{0:T(256)} %constant.166.clone) | copy-start | bytes 3076
  57.5 63.3 %copy-start.1 = (f32[13,72,128]{2,1,0:T(8,128)}, f32[13,72,128]{2,1,0:T(8,128)S(1)}, u32[]{:S(2)}) copy-start(f32[13,72,128]{2,1,0:T(8,128)S(1)} %collective-permute-done.1.refs_1_.refs_5_.refs_9_.refs_13_) | copy-start | bytes 1437700
  98.5 22.3 %copy-start.2 = (f32[13,72,128]{2,1,0:T(8,128)}, f32[13,72,128]{2,1,0:T(8,128)S(1)}, u32[]{:S(2)}) copy-start(f32[13,72,128]{2,1,0:T(8,128)S(1)} %collective-permute-done.2.refs_2_.refs_6_.refs_10_.refs_14_) | copy-start | bytes 1437700
  113.8 7.0 %copy-start.3 = (f32[13,72,128]{2,1,0:T(8,128)}, f32[13,72,128]{2,1,0:T(8,128)S(1)}, u32[]{:S(2)}) copy-start(f32[13,72,128]{2,1,0:T(8,128)S(1)} %collective-permute-done.3.refs_3_.refs_7_.refs_11_.refs_15_) | copy-start | bytes 1437700
  115.1 64.7 %all-to-all-start = ((f32[16,8,32,128]{3,2,1,0:T(8,128)}), f32[16,8,32,128]{3,2,1,0:T(8,128)}, u32[]{:S(2)}, u32[]{:S(2)}) async-start(f32[16,8,32,128]{3,2,1,0:T(8,128)} %bitcast.16), calls=%async_computation | async-start | bytes 4194304 | tf_op jit(solution)/shard_map/all_to_all | solution.py:634
  128.8 20.0 %collective-permute-start.4 = (f32[2,2,8,32,128]{4,3,2,1,0:T(8,128)}, f32[2,2,8,32,128]{4,3,2,1,0:T(8,128)S(1)}, u32[]{:S(2)}, u32[]{:S(2)}) collective-permute-start(f32[2,2,8,32,128]{4,3,2,1,0:T(8,128)} %get-tuple-element.101), channel_id=1, source_target_pairs={{0,2},{2,0},{4,6},{6,4},{8,10},{10,8},{12,14},{14,12},{1,3},{3,1},... | collective-permute-start | bytes 1572872 | tf_op jit(solution)/shard_map/ppermute | solution.py:698
  130.1 37.5 %collective-permute-start.5 = (f32[2,2,8,32,128]{4,3,2,1,0:T(8,128)}, f32[2,2,8,32,128]{4,3,2,1,0:T(8,128)S(1)}, u32[]{:S(2)}, u32[]{:S(2)}) collective-permute-start(f32[2,2,8,32,128]{4,3,2,1,0:T(8,128)} %get-tuple-element.102), channel_id=1, source_target_pairs={{0,4},{2,6},{4,0},{6,2},{8,12},{10,14},{12,8},{14,10},{1,5},{3,7},... | collective-permute-start | bytes 1572872 | tf_op jit(solution)/shard_map/ppermute | solution.py:698
  131.3 48.5 %collective-permute-start.6 = (f32[2,2,8,32,128]{4,3,2,1,0:T(8,128)}, f32[2,2,8,32,128]{4,3,2,1,0:T(8,128)S(1)}, u32[]{:S(2)}, u32[]{:S(2)}) collective-permute-start(f32[2,2,8,32,128]{4,3,2,1,0:T(8,128)} %get-tuple-element.103), channel_id=1, source_target_pairs={{0,6},{2,4},{4,2},{6,0},{8,14},{10,12},{12,10},{14,8},{1,7},{3,5},... | collective-permute-start | bytes 1572872 | tf_op jit(solution)/shard_map/ppermute | solution.py:698
  179.8 107.5 %all-to-all-start.2 = ((f32[16,2,8,32,128]{4,3,2,1,0:T(8,128)}), f32[16,2,8,32,128]{4,3,2,1,0:T(8,128)}, u32[]{:S(2)}, u32[]{:S(2)}) async-start(f32[16,2,8,32,128]{4,3,2,1,0:T(8,128)} %bitcast.17), calls=%async_computation.2 | async-start | bytes 8388608 | tf_op jit(solution)/shard_map/all_to_all | solution.py:634
  184.9 8.2 %copy-start.5 = (f32[2,2,8,32,128]{4,3,2,1,0:T(8,128)S(1)}, f32[2,2,8,32,128]{4,3,2,1,0:T(8,128)}, u32[]{:S(2)}) copy-start(f32[2,2,8,32,128]{4,3,2,1,0:T(8,128)} %get-tuple-element.113) | copy-start | bytes 1572868
  193.1 1.0 copy-start.12
  193.1 2.2 copy-start.11
  193.1 3.4 %copy-start.10 = (f32[2,2,8,32,128]{4,3,2,1,0:T(8,128)S(1)}, f32[2,2,8,32,128]{4,3,2,1,0:T(8,128)}, u32[]{:S(2)}) copy-start(f32[2,2,8,32,128]{4,3,2,1,0:T(8,128)} %get-tuple-element.111) | copy-start | bytes 1572868
  193.4 3.5 %collective-permute-start.10 = (f32[4,2,8,32,128]{4,3,2,1,0:T(8,128)S(1)}, f32[4,2,8,32,128]{4,3,2,1,0:T(8,128)S(1)}, u32[]{:S(2)}, u32[]{:S(2)}) collective-permute-start(f32[4,2,8,32,128]{4,3,2,1,0:T(8,128)S(1)} %pad_maximum_fusion.1), channel_id=1, source_target_pairs={{0,1},{1,0},{2,3},{3,2},{4,5},{5,4},{6,7},{7,6},{8,9},{9,8},{10,11... | collective-permute-start | bytes 3145736 | tf_op jit(solution)/shard_map/ppermute | solution.py:707
  194.1 30.4 %collective-permute-start.7 = (f32[2,2,8,32,128]{4,3,2,1,0:T(8,128)S(1)}, f32[2,2,8,32,128]{4,3,2,1,0:T(8,128)S(1)}, u32[]{:S(2)}, u32[]{:S(2)}) collective-permute-start(f32[2,2,8,32,128]{4,3,2,1,0:T(8,128)S(1)} %copy-done.12), channel_id=1, source_target_pairs={{0,2},{2,0},{4,6},{6,4},{8,10},{10,8},{12,14},{14,12},{1,3},{3,1},... | collective-permute-start | bytes 1572872 | tf_op jit(solution)/shard_map/ppermute | solution.py:698
  195.3 70.7 %collective-permute-start.8 = (f32[2,2,8,32,128]{4,3,2,1,0:T(8,128)S(1)}, f32[2,2,8,32,128]{4,3,2,1,0:T(8,128)S(1)}, u32[]{:S(2)}, u32[]{:S(2)}) collective-permute-start(f32[2,2,8,32,128]{4,3,2,1,0:T(8,128)S(1)} %copy-done.11), channel_id=1, source_target_pairs={{0,4},{2,6},{4,0},{6,2},{8,12},{10,14},{12,8},{14,10},{1,5},{3,7},... | collective-permute-start | bytes 1572872 | tf_op jit(solution)/shard_map/ppermute | solution.py:698
  196.5 87.0 %collective-permute-start.9 = (f32[2,2,8,32,128]{4,3,2,1,0:T(8,128)S(1)}, f32[2,2,8,32,128]{4,3,2,1,0:T(8,128)S(1)}, u32[]{:S(2)}, u32[]{:S(2)}) collective-permute-start(f32[2,2,8,32,128]{4,3,2,1,0:T(8,128)S(1)} %copy-done.10), channel_id=1, source_target_pairs={{0,6},{2,4},{4,2},{6,0},{8,14},{10,12},{12,10},{14,8},{1,7},{3,5},... | collective-permute-start | bytes 1572872 | tf_op jit(solution)/shard_map/ppermute | solution.py:698
  196.9 86.7 %copy-start.4 = (f32[2,2,8,32,128]{4,3,2,1,0:T(8,128)S(1)}, f32[2,2,8,32,128]{4,3,2,1,0:T(8,128)}, u32[]{:S(2)}) copy-start(f32[2,2,8,32,128]{4,3,2,1,0:T(8,128)} %get-tuple-element.117) | copy-start | bytes 1572868
  203.5 83.8 %copy-start = (bf16[384,256]{1,0:T(8,128)(2,1)S(1)}, bf16[384,256]{1,0:T(8,128)(2,1)}, u32[]{:S(2)}) copy-start(bf16[384,256]{1,0:T(8,128)(2,1)} %constant.169.clone.refs_2_) | copy-start | bytes 589828
  283.8 3.5 %collective-permute-start.11 = (f32[4,2,8,32,128]{4,3,2,1,0:T(8,128)S(1)}, f32[4,2,8,32,128]{4,3,2,1,0:T(8,128)S(1)}, u32[]{:S(2)}, u32[]{:S(2)}) collective-permute-start(f32[4,2,8,32,128]{4,3,2,1,0:T(8,128)S(1)} %pad_maximum_fusion.3), channel_id=1, source_target_pairs={{0,1},{1,0},{2,3},{3,2},{4,5},{5,4},{6,7},{7,6},{8,9},{9,8},{10,11... | collective-permute-start | bytes 3145736 | tf_op jit(solution)/shard_map/ppermute | solution.py:707

commit v6 on v5

--- a/solution.py
+++ b/solution.py
@@ -83,7 +83,7 @@
 def forward_last(adjoint, table, depth, copies):
     rows_one, rows_two, length = adjoint.shape
     count = table.shape[0]
-    block = min(8, rows_one)
+    block = min(16, rows_one)
 
     def body(adjoint_ref, table_ref, out_ref):
         flat = out_ref.reshape(depth * block, rows_two)
@@ -638,7 +638,7 @@
 
     barrier = lax.optimization_barrier
     device = px_index * width_py + py_index
-    sent, spectra, edge, adjoint = barrier((sent, spectra, edge, adjoint))
+    sent, spectra, _, adjoint = barrier((sent, spectra, edge[0, 0, :1], adjoint))
     wanted, places = folded_rows(owned)
     messages = kernel_messages(spectra, edge, wanted, width_px, width_py)
     messages, saved, adjoint, px_index, py_index = barrier(

time: 298 us -> 332 us (1.11)
  waiting for transfers between devices: 180 us -> 210 us
  starting transfers between devices: 27.6 us -> 32.4 us
    ppermute x1, waiting for transfers between devices: 2.25 us -> 89.8 us  [on_device(): lax.ppermute(spectra[:, :half_one + 1, 0].astype(jnp.float32), 'px', [(0,...]
    ppermute x3, waiting for transfers between devices: 56.3 us -> 0.01 us  [send_messages(): lax.ppermute(message[delta], 'px', swap_pairs(width_px, half_px, delta))]
    all_to_all x3, starting transfers between devices: 16 us -> 20.7 us  [exchange(): return lax.all_to_all(value, ('px', 'py'), 0, 0, tiled=True)]
  transfers between devices with their start and end apart: 15 -> 15, of which waited for: 11 -> 8; matrix products, arithmetic and copies ran while one was open for 5% -> 5% of each run, Pallas kernels for 21% -> 17%
where the time goes in v6:
time: 332 us; the launch traced here: 331 us
  waiting for transfers between devices  210 us (63%)
  Pallas kernels  72 us (22%)
  starting transfers between devices  32.4 us (10%)
  other arithmetic  9.74 us (3%)
  local copies, waits for them, and re-layouts  6.38 us (2%)
    ppermute x6, waiting for transfers between devices, shared_rows(): lax.ppermute(pieces[delta], 'px', swap_pairs(width_px, half_px, delta))  118 us
    ppermute x1, waiting for transfers between devices, on_device(): lax.ppermute(spectra[:, :half_one + 1, 0].astype(jnp.float32), 'px', [(0,...  89.8 us
    pallas_call x3, Pallas kernels, filter_planes(): pl.pallas_call(body, grid_spec=pltpu.PrefetchScalarGridSpec(num_scalar_pr...  26 us
    all_to_all x3, starting transfers between devices, exchange(): return lax.all_to_all(value, ('px', 'py'), 0, 0, tiled=True)  20.7 us
    pallas_call x2, Pallas kernels, backward_last(): pl.pallas_call(body, grid=(rows_one // block,), in_specs=in_specs, out_sp...  16.4 us
    pallas_call x2, Pallas kernels, forward_last(): pl.pallas_call(body, grid=(rows_one // block,), in_specs=[pl.BlockSpec((b...  11.1 us
    pallas_call x1, Pallas kernels, message_rows(): pl.pallas_call(body, grid=(1,), in_specs=[pl.BlockSpec(part, lambda i: (0...  9.39 us
    pallas_call x1, Pallas kernels, cosine_factors(): pl.pallas_call(body, grid=(rows_one // block,), in_specs=[pl.BlockSpec(me...  9.08 us
  transfers between devices with their start and end apart: 15, of which 8 were waited for; matrix products, arithmetic and copies ran while one was open for 5% of the time, Pallas kernels for 17%

profile of v6, /device:TPU:21, one launch (start us, length us, event | category | flops | bytes accessed | tf_op | source)
XLA Modules:
  0.0 331.3 jit_solution(9816007023958622209)
XLA Ops:
  0.0 5.9 %forward_last.2 = f32[256,32,128]{2,1,0:T(8,128)} custom-call(f32[32,128,256]{2,1,0:T(8,128)} %adjoint_ref.2, bf16[192,768]{1,0:T(8,128)(2,1)} %constant.161.clone.table_ref), custom_call_target="tpu_custom_call" | custom-call | flops 1207959552 | bytes 8388608 | tf_op jit(solution)/shard_map/forward_last/pallas_call | solution.py:108
  5.9 6.6 %all-to-all-start.1 = ((f32[16,16,32,128]{3,2,1,0:T(8,128)}), f32[16,16,32,128]{3,2,1,0:T(8,128)}, u32[]{:S(2)}, u32[]{:S(2)}) async-start(f32[16,16,32,128]{3,2,1,0:T(8,128)} %bitcast.15), calls=%async_computation.1 | async-start | bytes 8388608 | tf_op jit(solution)/shard_map/all_to_all | solution.py:634
  12.5 1.4 slice.61
  14.0 2.0 collective-permute-start
  16.0 0.2 fusion.38
  16.2 0.7 dynamic-slice_bitcast_fusion
  16.9 0.7 dynamic-slice_reduce_fusion
  17.6 0.5 convert_element_type.45.chosen_ref
  18.1 0.1 reshape_squeeze.3
  18.2 0.1 eq.55
  18.3 0.7 fusion.37.select_ref
  18.9 89.8 %collective-permute-done.edge_ref = f32[2,129,256]{2,1,0:T(8,128)S(1)} collective-permute-done((f32[2,129,256]{2,1,0:T(8,128)S(1)}, f32[2,129,256]{2,1,0:T(8,128)S(1)}, u32[]{:S(2)}, u32[]{:S(2)}) %collective-permute-start) | collective-permute-done | bytes 264224 | tf_op jit(solution)/shard_map/ppermute | solution.py:607
  108.8 0.7 copy-done.6
  109.5 9.4 %message_rows.1 = (f32[13,72,128]{2,1,0:T(8,128)}, f32[13,72,128]{2,1,0:T(8,128)}, f32[13,72,128]{2,1,0:T(8,128)}, f32[13,72,128]{2,1,0:T(8,128)}) custom-call(bf16[2,256,32,256]{3,2,1,0:T(8,128)(2,1)} %spectra_ref, f32[2,129,256]{2,1,0:T(8,128)} %copy-done.6, bf16[64,256]{1,0:T(8,128)(2,1)} %fusion.37.select_ref), custom_call_target="tpu_custom_call" | custom-call | flops 268435456 | bytes 6144000 | tf_op jit(solution)/shard_map/message_rows/pallas_call | solution.py:485
  118.9 0.1 broadcast_add_fusion
  119.0 0.1 add.212
  119.1 0.1 iota_add_fusion
  119.1 0.1 add.192
  119.2 0.6 gather_fusion.1
  119.8 0.1 mul.152
  119.9 0.6 gather_fusion
  120.5 0.1 mul.148
  120.5 0.0 collective-permute-start.1
  120.5 0.1 collective-permute-start.2
  120.6 2.6 collective-permute-start.3
  123.2 9.1 %cosine_factors.1.refs_0_ = f32[2,32,128,256]{3,2,1,0:T(8,128)} custom-call(f32[2]{0:T(128)} %convert_element_type.45.chosen_ref, f32[32,128,256]{2,1,0:T(8,128)} %saved_ref), custom_call_target="tpu_custom_call" | custom-call | flops 50331648 | bytes 12582912 | tf_op jit(solution)/shard_map/cosine_factors/pallas_call | solution.py:378
  132.3 5.2 %forward_last.3 = f32[128,32,128]{2,1,0:T(8,128)} custom-call(f32[32,128,256]{2,1,0:T(8,128)} %adjoint_ref.2, bf16[64,768]{1,0:T(8,128)(2,1)} %constant.170.clone.table_ref), custom_call_target="tpu_custom_call" | custom-call | flops 402653184 | bytes 6291456 | tf_op jit(solution)/shard_map/forward_last/pallas_call | solution.py:108
  137.5 0.3 reduce-precision_convert_fusion.5
  137.9 0.6 reduce-precision_convert_fusion.3
  138.5 0.7 pad_maximum_fusion.7.refs_18_
  139.2 0.3 reduce-precision_convert_fusion.4
  139.6 3.4 %reduce-precision_convert_fusion = (bf16[256,256]{1,0:T(8,128)(2,1)S(1)}, bf16[256,256]{1,0:T(8,128)(2,1)S(1)}, bf16[256,256]{1,0:T(8,128)(2,1)S(1)}, bf16[256,2...) fusion(s32[256]{0:T(256)S(1)} %and_select_fusion.1, s32[256]{0:T(256)S(1)} %pad_add_fusion), kind=kLoop, calls=%fused_computation.21 | loop fusion | flops 3735552 | bytes 788480 | tf_op jit(solution)/shard_map/convert.7
  143.0 0.8 pad_maximum_fusion.6.refs_19_
  143.8 0.8 pad_maximum_fusion.4.refs_17_
  144.6 0.8 pad_maximum_fusion.5.refs_19_
  145.4 0.0 collective-permute-done.2.refs_2_.refs_6_.refs_10_.refs_14_
  145.4 9.0 %all-to-all-start = ((f32[16,8,32,128]{3,2,1,0:T(8,128)}), f32[16,8,32,128]{3,2,1,0:T(8,128)}, u32[]{:S(2)}, u32[]{:S(2)}) async-start(f32[16,8,32,128]{3,2,1,0:T(8,128)} %bitcast.16), calls=%async_computation | async-start | bytes 4194304 | tf_op jit(solution)/shard_map/all_to_all | solution.py:634
  154.4 0.6 fusion.54
  155.1 8.0 %filter_planes.5 = (f32[2,2,8,32,128]{4,3,2,1,0:T(8,128)}, f32[2,2,8,32,128]{4,3,2,1,0:T(8,128)}, f32[2,2,8,32,128]{4,3,2,1,0:T(8,128)}, f32[2,2,8,32,128]{4,3,2,1,0:T(8,128)}) custom-call(s32[8]{0:T(128)} %get-tuple-element.145.places_ref, s32[1]{0:T(128)} %bitcast.5.special_ref, f32[8,2,16,32,128]{4,3,2,1,0:T(8,128)} %bitcast.7.planes_ref, ...), custom_call_target="tpu_custom_call" | custom-call | flops 3221225472 | bytes 5242880 | tf_op jit(solution)/shard_map/filter_planes/pallas_call | solution.py:224
  163.1 1.3 collective-permute-start.4
  164.4 1.2 collective-permute-start.5
  165.6 0.2 collective-permute-start.6
  165.8 9.8 %filter_planes.4 = f32[8,2,2,8,32,128]{5,4,3,2,1,0:T(8,128)} custom-call(s32[8]{0:T(128)} %get-tuple-element.146.places_ref, s32[1]{0:T(128)} %bitcast.5.special_ref, f32[8,2,16,32,128]{4,3,2,1,0:T(8,128)} %bitcast.7.planes_ref, f32[13,72,128]{2,1,0:T(8,128)} %get-tuple-element.81.refs_0_.refs_4_.refs_8_.refs_12_, f32[13,72,128]{2,1,0:T(8,128)} %copy-done.1, ...), custom_call_target="tpu_custom_call" | custom-call | flops 4831838208 | bytes 7340032 | tf_op jit(solution)/shard_map/filter_planes/pallas_call | solution.py:224
  175.6 7.6 %collective-permute-done.4 = f32[2,2,8,32,128]{4,3,2,1,0:T(8,128)S(1)} collective-permute-done((f32[2,2,8,32,128]{4,3,2,1,0:T(8,128)}, f32[2,2,8,32,128]{4,3,2,1,0:T(8,128)S(1)}, u32[]{:S(2)}, u32[]{:S(2)}) %collective-permute-start.4) | collective-permute-done | bytes 524320 | tf_op jit(solution)/shard_map/ppermute | solution.py:698
  183.2 18.6 %collective-permute-done.5 = f32[2,2,8,32,128]{4,3,2,1,0:T(8,128)S(1)} collective-permute-done((f32[2,2,8,32,128]{4,3,2,1,0:T(8,128)}, f32[2,2,8,32,128]{4,3,2,1,0:T(8,128)S(1)}, u32[]{:S(2)}, u32[]{:S(2)}) %collective-permute-start.5) | collective-permute-done | bytes 524320 | tf_op jit(solution)/shard_map/ppermute | solution.py:698
  201.8 12.2 %collective-permute-done.6 = f32[2,2,8,32,128]{4,3,2,1,0:T(8,128)S(1)} collective-permute-done((f32[2,2,8,32,128]{4,3,2,1,0:T(8,128)}, f32[2,2,8,32,128]{4,3,2,1,0:T(8,128)S(1)}, u32[]{:S(2)}, u32[]{:S(2)}) %collective-permute-start.6) | collective-permute-done | bytes 524320 | tf_op jit(solution)/shard_map/ppermute | solution.py:698
  214.1 5.1 %all-to-all-start.2 = ((f32[16,2,8,32,128]{4,3,2,1,0:T(8,128)}), f32[16,2,8,32,128]{4,3,2,1,0:T(8,128)}, u32[]{:S(2)}, u32[]{:S(2)}) async-start(f32[16,2,8,32,128]{4,3,2,1,0:T(8,128)} %bitcast.17), calls=%async_computation.2 | async-start | bytes 8388608 | tf_op jit(solution)/shard_map/all_to_all | solution.py:634
  219.2 8.2 %filter_planes.3 = (f32[2,2,8,32,128]{4,3,2,1,0:T(8,128)}, f32[2,2,8,32,128]{4,3,2,1,0:T(8,128)}, f32[2,2,8,32,128]{4,3,2,1,0:T(8,128)}, f32[2,2,8,32,128]{4,3,2,1,0:T(8,128)}) custom-call(s32[8]{0:T(128)} %get-tuple-element.147.places_ref, s32[1]{0:T(128)} %bitcast.5.special_ref, f32[8,2,8,32,128]{4,3,2,1,0:T(8,128)} %bitcast.6.planes_ref, ...), custom_call_target="tpu_custom_call" | custom-call | flops 3221225472 | bytes 5242880 | tf_op jit(solution)/shard_map/filter_planes/pallas_call | solution.py:224
  227.5 0.1 pad_maximum_fusion.1
  227.6 0.5 collective-permute-start.10
  228.1 0.2 copy-done.12
  228.4 1.2 collective-permute-start.7
  229.6 1.2 collective-permute-start.8
  230.8 0.2 collective-permute-start.9
  231.0 0.1 pad_maximum_fusion.refs_2_
  231.1 6.7 %backward_last.2.refs_6_ = f32[32,128,256]{2,1,0:T(8,128)} custom-call(f32[2,32,128,256]{3,2,1,0:T(8,128)} %cosine_factors.1.refs_0_, bf16[192,256]{1,0:T(8,128)(2,1)S(1)} %pad_maximum_fusion.8.refs_1_, f32[4,2,8,32,128]{4,3,2,1,0:T(8,128)S(1)} %pad_maximum_fusion.refs_2_, f32[4,2,8,32,128]{4,3,2,1,0:T(8,128)S(1)} %collective-permute-done.10.refs_3_), custom_call_target="tpu_custom_call" | custom-call | flops 805306368 | bytes 18874368 | tf_op jit(solution)/shard_map/backward_last/pallas_call | solution.py:336
  237.8 20.9 %collective-permute-done.7 = f32[2,2,8,32,128]{4,3,2,1,0:T(8,128)S(1)} collective-permute-done((f32[2,2,8,32,128]{4,3,2,1,0:T(8,128)S(1)}, f32[2,2,8,32,128]{4,3,2,1,0:T(8,128)S(1)}, u32[]{:S(2)}, u32[]{:S(2)}) %collective-permute-start.7) | collective-permute-done | bytes 524320 | tf_op jit(solution)/shard_map/ppermute | solution.py:698
  258.7 41.6 %collective-permute-done.8 = f32[2,2,8,32,128]{4,3,2,1,0:T(8,128)S(1)} collective-permute-done((f32[2,2,8,32,128]{4,3,2,1,0:T(8,128)S(1)}, f32[2,2,8,32,128]{4,3,2,1,0:T(8,128)S(1)}, u32[]{:S(2)}, u32[]{:S(2)}) %collective-permute-start.8) | collective-permute-done | bytes 524320 | tf_op jit(solution)/shard_map/ppermute | solution.py:698
  300.3 17.5 %collective-permute-done.9 = f32[2,2,8,32,128]{4,3,2,1,0:T(8,128)S(1)} collective-permute-done((f32[2,2,8,32,128]{4,3,2,1,0:T(8,128)S(1)}, f32[2,2,8,32,128]{4,3,2,1,0:T(8,128)S(1)}, u32[]{:S(2)}, u32[]{:S(2)}) %collective-permute-start.9) | collective-permute-done | bytes 524320 | tf_op jit(solution)/shard_map/ppermute | solution.py:698
  318.0 0.1 pad_maximum_fusion.3
  318.0 1.2 collective-permute-start.11
  319.3 0.1 pad_maximum_fusion.2.refs_3_
  319.4 2.2 collective-permute-done.11.refs_4_
  321.6 9.7 %backward_last.3 = f32[32,128,256]{2,1,0:T(8,128)} custom-call(f32[2,32,128,256]{3,2,1,0:T(8,128)} %cosine_factors.1.refs_0_, bf16[192,256]{1,0:T(8,128)(2,1)S(1)} %pad_maximum_fusion.9.refs_1_, bf16[384,256]{1,0:T(8,128)(2,1)S(1)} %copy-done, f32[4,2,8,32,128]{4,3,2,1,0:T(8,128)S(1)} %pad_maximum_fusion.2.refs_3_, ...), custom_call_target="tpu_custom_call" | custom-call | flops 2415919104 | bytes 23068672 | tf_op jit(solution)/shard_map/backward_last/pallas_call | solution.py:336
  (53 shorter events, 0.5 us)
Async XLA Ops:
  5.9 10.0 %copy-start.13 = (s32[8]{0:T(128)S(1)}, s32[8]{0:T(128)}, u32[]{:S(2)}) copy-start(s32[8]{0:T(128)} %param.18) | copy-start | bytes 100
  5.9 10.0 %copy-start.14 = (s32[2]{0:T(128)S(1)}, s32[2]{0:T(128)}, u32[]{:S(2)}) copy-start(s32[2]{0:T(128)} %param.19) | copy-start | bytes 28
  5.9 139.5 %all-to-all-start.1 = ((f32[16,16,32,128]{3,2,1,0:T(8,128)}), f32[16,16,32,128]{3,2,1,0:T(8,128)}, u32[]{:S(2)}, u32[]{:S(2)}) async-start(f32[16,16,32,128]{3,2,1,0:T(8,128)} %bitcast.15), calls=%async_computation.1 | async-start | bytes 8388608 | tf_op jit(solution)/shard_map/all_to_all | solution.py:634
  14.0 94.8 %collective-permute-start = (f32[2,129,256]{2,1,0:T(8,128)S(1)}, f32[2,129,256]{2,1,0:T(8,128)S(1)}, u32[]{:S(2)}, u32[]{:S(2)}) collective-permute-start(f32[2,129,256]{2,1,0:T(8,128)S(1)} %fusion.18), channel_id=1, source_target_pairs={{0,8},{8,0},{1,9},{9,1},{16,24},{24,16},{17,25},{25,17}} | collective-permute-start | bytes 792584 | tf_op jit(solution)/shard_map/ppermute | solution.py:607
  18.9 100.3 %copy-start.8 = (s32[8,8]{1,0:T(8,128)S(1)}, s32[8,8]{1,0:T(8,128)}, u32[]{:S(2)}) copy-start(s32[8,8]{1,0:T(8,128)} %constant.168.clone) | copy-start | bytes 772
  18.9 100.9 %copy-start.7 = (s32[8,8]{1,0:T(8,128)S(1)}, s32[8,8]{1,0:T(8,128)}, u32[]{:S(2)}) copy-start(s32[8,8]{1,0:T(8,128)} %constant.167.clone) | copy-start | bytes 772
  108.8 0.7 copy-start.6
  120.5 24.9 %collective-permute-start.1 = (f32[13,72,128]{2,1,0:T(8,128)}, f32[13,72,128]{2,1,0:T(8,128)S(1)}, u32[]{:S(2)}, u32[]{:S(2)}) collective-permute-start(f32[13,72,128]{2,1,0:T(8,128)} %get-tuple-element.71), channel_id=1, source_target_pairs={{0,2},{2,0},{4,6},{6,4},{8,10},{10,8},{12,14},{14,12},{1,3},{3,1},... | collective-permute-start | bytes 1437704 | tf_op jit(solution)/shard_map/ppermute | solution.py:403
  120.5 24.9 %collective-permute-start.2 = (f32[13,72,128]{2,1,0:T(8,128)}, f32[13,72,128]{2,1,0:T(8,128)S(1)}, u32[]{:S(2)}, u32[]{:S(2)}) collective-permute-start(f32[13,72,128]{2,1,0:T(8,128)} %get-tuple-element.72), channel_id=1, source_target_pairs={{0,4},{2,6},{4,0},{6,2},{8,12},{10,14},{12,8},{14,10},{1,5},{3,7},... | collective-permute-start | bytes 1437704 | tf_op jit(solution)/shard_map/ppermute | solution.py:403
  120.6 24.8 %collective-permute-start.3 = (f32[13,72,128]{2,1,0:T(8,128)}, f32[13,72,128]{2,1,0:T(8,128)S(1)}, u32[]{:S(2)}, u32[]{:S(2)}) collective-permute-start(f32[13,72,128]{2,1,0:T(8,128)} %get-tuple-element.73), channel_id=1, source_target_pairs={{0,6},{2,4},{4,2},{6,0},{8,14},{10,12},{12,10},{14,8},{1,7},{3,5},... | collective-permute-start | bytes 1437704 | tf_op jit(solution)/shard_map/ppermute | solution.py:403
  132.3 5.6 %copy-start.9 = (s32[256]{0:T(256)S(1)}, s32[256]{0:T(256)}, u32[]{:S(2)}) copy-start(s32[256]{0:T(256)} %constant.166.clone) | copy-start | bytes 3076
  145.4 9.7 %copy-start.1 = (f32[13,72,128]{2,1,0:T(8,128)}, f32[13,72,128]{2,1,0:T(8,128)S(1)}, u32[]{:S(2)}) copy-start(f32[13,72,128]{2,1,0:T(8,128)S(1)} %collective-permute-done.1.refs_1_.refs_5_.refs_9_.refs_13_) | copy-start | bytes 1437700
  145.4 9.7 %copy-start.2 = (f32[13,72,128]{2,1,0:T(8,128)}, f32[13,72,128]{2,1,0:T(8,128)S(1)}, u32[]{:S(2)}) copy-start(f32[13,72,128]{2,1,0:T(8,128)S(1)} %collective-permute-done.2.refs_2_.refs_6_.refs_10_.refs_14_) | copy-start | bytes 1437700
  145.4 9.6 %copy-start.3 = (f32[13,72,128]{2,1,0:T(8,128)}, f32[13,72,128]{2,1,0:T(8,128)S(1)}, u32[]{:S(2)}) copy-start(f32[13,72,128]{2,1,0:T(8,128)S(1)} %collective-permute-done.3.refs_3_.refs_7_.refs_11_.refs_15_) | copy-start | bytes 1437700
  145.4 68.6 %all-to-all-start = ((f32[16,8,32,128]{3,2,1,0:T(8,128)}), f32[16,8,32,128]{3,2,1,0:T(8,128)}, u32[]{:S(2)}, u32[]{:S(2)}) async-start(f32[16,8,32,128]{3,2,1,0:T(8,128)} %bitcast.16), calls=%async_computation | async-start | bytes 4194304 | tf_op jit(solution)/shard_map/all_to_all | solution.py:634
  163.1 20.1 %collective-permute-start.4 = (f32[2,2,8,32,128]{4,3,2,1,0:T(8,128)}, f32[2,2,8,32,128]{4,3,2,1,0:T(8,128)S(1)}, u32[]{:S(2)}, u32[]{:S(2)}) collective-permute-start(f32[2,2,8,32,128]{4,3,2,1,0:T(8,128)} %get-tuple-element.99), channel_id=1, source_target_pairs={{0,2},{2,0},{4,6},{6,4},{8,10},{10,8},{12,14},{14,12},{1,3},{3,1},... | collective-permute-start | bytes 1572872 | tf_op jit(solution)/shard_map/ppermute | solution.py:698
  164.4 37.4 %collective-permute-start.5 = (f32[2,2,8,32,128]{4,3,2,1,0:T(8,128)}, f32[2,2,8,32,128]{4,3,2,1,0:T(8,128)S(1)}, u32[]{:S(2)}, u32[]{:S(2)}) collective-permute-start(f32[2,2,8,32,128]{4,3,2,1,0:T(8,128)} %get-tuple-element.100), channel_id=1, source_target_pairs={{0,4},{2,6},{4,0},{6,2},{8,12},{10,14},{12,8},{14,10},{1,5},{3,7},... | collective-permute-start | bytes 1572872 | tf_op jit(solution)/shard_map/ppermute | solution.py:698
  165.6 48.5 %collective-permute-start.6 = (f32[2,2,8,32,128]{4,3,2,1,0:T(8,128)}, f32[2,2,8,32,128]{4,3,2,1,0:T(8,128)S(1)}, u32[]{:S(2)}, u32[]{:S(2)}) collective-permute-start(f32[2,2,8,32,128]{4,3,2,1,0:T(8,128)} %get-tuple-element.101), channel_id=1, source_target_pairs={{0,6},{2,4},{4,2},{6,0},{8,14},{10,12},{12,10},{14,8},{1,7},{3,5},... | collective-permute-start | bytes 1572872 | tf_op jit(solution)/shard_map/ppermute | solution.py:698
  214.1 107.5 %all-to-all-start.2 = ((f32[16,2,8,32,128]{4,3,2,1,0:T(8,128)}), f32[16,2,8,32,128]{4,3,2,1,0:T(8,128)}, u32[]{:S(2)}, u32[]{:S(2)}) async-start(f32[16,2,8,32,128]{4,3,2,1,0:T(8,128)} %bitcast.17), calls=%async_computation.2 | async-start | bytes 8388608 | tf_op jit(solution)/shard_map/all_to_all | solution.py:634
  219.2 8.2 %copy-start.5 = (f32[2,2,8,32,128]{4,3,2,1,0:T(8,128)S(1)}, f32[2,2,8,32,128]{4,3,2,1,0:T(8,128)}, u32[]{:S(2)}) copy-start(f32[2,2,8,32,128]{4,3,2,1,0:T(8,128)} %get-tuple-element.111) | copy-start | bytes 1572868
  227.3 1.0 copy-start.12
  227.3 2.2 copy-start.11
  227.3 3.4 %copy-start.10 = (f32[2,2,8,32,128]{4,3,2,1,0:T(8,128)S(1)}, f32[2,2,8,32,128]{4,3,2,1,0:T(8,128)}, u32[]{:S(2)}) copy-start(f32[2,2,8,32,128]{4,3,2,1,0:T(8,128)} %get-tuple-element.109) | copy-start | bytes 1572868
  227.6 3.5 %collective-permute-start.10 = (f32[4,2,8,32,128]{4,3,2,1,0:T(8,128)S(1)}, f32[4,2,8,32,128]{4,3,2,1,0:T(8,128)S(1)}, u32[]{:S(2)}, u32[]{:S(2)}) collective-permute-start(f32[4,2,8,32,128]{4,3,2,1,0:T(8,128)S(1)} %pad_maximum_fusion.1), channel_id=1, source_target_pairs={{0,1},{1,0},{2,3},{3,2},{4,5},{5,4},{6,7},{7,6},{8,9},{9,8},{10,11... | collective-permute-start | bytes 3145736 | tf_op jit(solution)/shard_map/ppermute | solution.py:707
  228.4 30.4 %collective-permute-start.7 = (f32[2,2,8,32,128]{4,3,2,1,0:T(8,128)S(1)}, f32[2,2,8,32,128]{4,3,2,1,0:T(8,128)S(1)}, u32[]{:S(2)}, u32[]{:S(2)}) collective-permute-start(f32[2,2,8,32,128]{4,3,2,1,0:T(8,128)S(1)} %copy-done.12), channel_id=1, source_target_pairs={{0,2},{2,0},{4,6},{6,4},{8,10},{10,8},{12,14},{14,12},{1,3},{3,1},... | collective-permute-start | bytes 1572872 | tf_op jit(solution)/shard_map/ppermute | solution.py:698
  229.6 70.7 %collective-permute-start.8 = (f32[2,2,8,32,128]{4,3,2,1,0:T(8,128)S(1)}, f32[2,2,8,32,128]{4,3,2,1,0:T(8,128)S(1)}, u32[]{:S(2)}, u32[]{:S(2)}) collective-permute-start(f32[2,2,8,32,128]{4,3,2,1,0:T(8,128)S(1)} %copy-done.11), channel_id=1, source_target_pairs={{0,4},{2,6},{4,0},{6,2},{8,12},{10,14},{12,8},{14,10},{1,5},{3,7},... | collective-permute-start | bytes 1572872 | tf_op jit(solution)/shard_map/ppermute | solution.py:698
  230.8 87.0 %collective-permute-start.9 = (f32[2,2,8,32,128]{4,3,2,1,0:T(8,128)S(1)}, f32[2,2,8,32,128]{4,3,2,1,0:T(8,128)S(1)}, u32[]{:S(2)}, u32[]{:S(2)}) collective-permute-start(f32[2,2,8,32,128]{4,3,2,1,0:T(8,128)S(1)} %copy-done.10), channel_id=1, source_target_pairs={{0,6},{2,4},{4,2},{6,0},{8,14},{10,12},{12,10},{14,8},{1,7},{3,5},... | collective-permute-start | bytes 1572872 | tf_op jit(solution)/shard_map/ppermute | solution.py:698
  231.1 86.7 %copy-start.4 = (f32[2,2,8,32,128]{4,3,2,1,0:T(8,128)S(1)}, f32[2,2,8,32,128]{4,3,2,1,0:T(8,128)}, u32[]{:S(2)}) copy-start(f32[2,2,8,32,128]{4,3,2,1,0:T(8,128)} %get-tuple-element.115) | copy-start | bytes 1572868
  237.8 83.8 %copy-start = (bf16[384,256]{1,0:T(8,128)(2,1)S(1)}, bf16[384,256]{1,0:T(8,128)(2,1)}, u32[]{:S(2)}) copy-start(bf16[384,256]{1,0:T(8,128)(2,1)} %constant.169.clone.refs_2_) | copy-start | bytes 589828
  318.0 3.5 %collective-permute-start.11 = (f32[4,2,8,32,128]{4,3,2,1,0:T(8,128)S(1)}, f32[4,2,8,32,128]{4,3,2,1,0:T(8,128)S(1)}, u32[]{:S(2)}, u32[]{:S(2)}) collective-permute-start(f32[4,2,8,32,128]{4,3,2,1,0:T(8,128)S(1)} %pad_maximum_fusion.3), channel_id=1, source_target_pairs={{0,1},{1,0},{2,3},{3,2},{4,5},{5,4},{6,7},{7,6},{8,9},{9,8},{10,11... | collective-permute-start | bytes 3145736 | tf_op jit(solution)/shard_map/ppermute | solution.py:707

commit v7 on v6

--- a/solution.py
+++ b/solution.py
@@ -494,7 +494,7 @@
         out_shape=[jax.ShapeDtypeStruct((count, extent, half_one), jnp.float32)] * half_px,
         scratch_shapes=[pltpu.VMEM((half_one * local_two, lanes), jnp.float32)]
         * (length_three // lanes),
-        compiler_params=params(),
+        compiler_params=params(LAST_BYTES),
         cost_estimate=pl.CostEstimate(
             flops=2 * slots * select.shape[0] * half_one * local_two * length_three,
             bytes_accessed=2 * math.prod(part) + 4 * half_px * count * extent * half_one,
@@ -638,7 +638,7 @@
 
     barrier = lax.optimization_barrier
     device = px_index * width_py + py_index
-    sent, spectra, _, adjoint = barrier((sent, spectra, edge[0, 0, :1], adjoint))
+    sent, spectra, edge, adjoint = barrier((sent, spectra, edge, adjoint))
     wanted, places = folded_rows(owned)
     messages = kernel_messages(spectra, edge, wanted, width_px, width_py)
     messages, saved, adjoint, px_index, py_index = barrier(

time: 332 us -> 297 us (0.89)
  waiting for transfers between devices: 210 us -> 182 us
  starting transfers between devices: 32.4 us -> 27.8 us
    ppermute x1, waiting for transfers between devices: 89.8 us -> 2.4 us  [on_device(): lax.ppermute(spectra[:, :half_one + 1, 0].astype(jnp.float32), 'px', [(0,...]
    ppermute x3, waiting for transfers between devices: 0.01 us -> 57.4 us  [send_messages(): lax.ppermute(message[delta], 'px', swap_pairs(width_px, half_px, delta))]
    all_to_all x3, starting transfers between devices: 20.7 us -> 16.1 us  [exchange(): return lax.all_to_all(value, ('px', 'py'), 0, 0, tiled=True)]
  transfers between devices with their start and end apart: 15 -> 15, of which waited for: 8 -> 12; matrix products, arithmetic and copies ran while one was open for 5% -> 4% of each run, Pallas kernels for 17% -> 21%
where the time goes in v7:
time: 297 us; the launch traced here: 296 us
  waiting for transfers between devices  182 us (61%)
  Pallas kernels  70.7 us (24%)
  starting transfers between devices  27.8 us (9%)
  other arithmetic  9.32 us (3%)
  local copies, waits for them, and re-layouts  6.51 us (2%)
    ppermute x6, waiting for transfers between devices, shared_rows(): lax.ppermute(pieces[delta], 'px', swap_pairs(width_px, half_px, delta))  118 us
    ppermute x3, waiting for transfers between devices, send_messages(): lax.ppermute(message[delta], 'px', swap_pairs(width_px, half_px, delta))  57.4 us
    pallas_call x3, Pallas kernels, filter_planes(): pl.pallas_call(body, grid_spec=pltpu.PrefetchScalarGridSpec(num_scalar_pr...  26 us
    pallas_call x2, Pallas kernels, backward_last(): pl.pallas_call(body, grid=(rows_one // block,), in_specs=in_specs, out_sp...  16.4 us
    all_to_all x3, starting transfers between devices, exchange(): return lax.all_to_all(value, ('px', 'py'), 0, 0, tiled=True)  16.1 us
    pallas_call x2, Pallas kernels, forward_last(): pl.pallas_call(body, grid=(rows_one // block,), in_specs=[pl.BlockSpec((b...  11.2 us
    pallas_call x1, Pallas kernels, cosine_factors(): pl.pallas_call(body, grid=(rows_one // block,), in_specs=[pl.BlockSpec(me...  9.08 us
    pallas_call x1, Pallas kernels, message_rows(): pl.pallas_call(body, grid=(1,), in_specs=[pl.BlockSpec(part, lambda i: (0...  8.13 us
  transfers between devices with their start and end apart: 15, of which 12 were waited for; matrix products, arithmetic and copies ran while one was open for 4% of the time, Pallas kernels for 21%

profile of v7, /device:TPU:21, one launch (start us, length us, event | category | flops | bytes accessed | tf_op | source)
XLA Modules:
  0.0 296.4 jit_solution(640341483709663681)
XLA Ops:
  0.0 1.4 slice.60
  1.4 2.0 collective-permute-start
  3.4 5.9 %forward_last.2 = f32[256,32,128]{2,1,0:T(8,128)} custom-call(f32[32,128,256]{2,1,0:T(8,128)} %adjoint_ref.2, bf16[192,768]{1,0:T(8,128)(2,1)} %constant.161.clone.table_ref), custom_call_target="tpu_custom_call" | custom-call | flops 1207959552 | bytes 8388608 | tf_op jit(solution)/shard_map/forward_last/pallas_call | solution.py:108
  9.3 2.4 collective-permute-done.edge_ref
  11.8 6.0 %all-to-all-start.1 = ((f32[16,16,32,128]{3,2,1,0:T(8,128)}), f32[16,16,32,128]{3,2,1,0:T(8,128)}, u32[]{:S(2)}, u32[]{:S(2)}) async-start(f32[16,16,32,128]{3,2,1,0:T(8,128)} %bitcast.15), calls=%async_computation.1 | async-start | bytes 8388608 | tf_op jit(solution)/shard_map/all_to_all | solution.py:634
  17.8 0.2 fusion.38
  17.9 0.5 convert_element_type.45.chosen_ref
  18.5 0.7 dynamic-slice_reduce_fusion
  19.2 0.1 reshape_squeeze.3
  19.3 0.1 eq.55
  19.3 0.7 dynamic-slice_bitcast_fusion
  20.0 0.1 fusion.37.select_ref
  20.1 8.1 %message_rows.1 = (f32[13,72,128]{2,1,0:T(8,128)S(1)}, f32[13,72,128]{2,1,0:T(8,128)S(1)}, f32[13,72,128]{2,1,0:T(8,128)S(1)}, f32[13,72,128]{2,1,0:T(8,128)S(1)}) custom-call(bf16[2,256,32,256]{3,2,1,0:T(8,128)(2,1)} %spectra_ref, f32[2,129,256]{2,1,0:T(8,128)S(1)} %collective-permute-done.edge_ref, bf16[64,256]{1,0:T(8,128)(2,1)S(1)} %fusion.37.select_ref), custom_call_target="tpu_custom_call" | custom-call | flops 268435456 | bytes 6144000 | tf_op jit(solution)/shard_map/message_rows/pallas_call | solution.py:485
  28.3 0.8 copy-done
  29.1 0.1 broadcast_add_fusion
  29.2 0.1 add.212
  29.3 0.1 add.192
  29.4 0.6 gather_fusion.1
  30.0 0.1 mul.152
  30.1 0.6 gather_fusion
  30.6 0.1 mul.148
  30.7 1.2 collective-permute-start.1
  31.9 1.2 collective-permute-start.2
  33.1 0.2 collective-permute-start.3
  33.4 9.1 %cosine_factors.1.refs_0_ = f32[2,32,128,256]{3,2,1,0:T(8,128)} custom-call(f32[2]{0:T(128)} %convert_element_type.45.chosen_ref, f32[32,128,256]{2,1,0:T(8,128)} %saved_ref), custom_call_target="tpu_custom_call" | custom-call | flops 50331648 | bytes 12582912 | tf_op jit(solution)/shard_map/cosine_factors/pallas_call | solution.py:378
  42.4 5.2 %forward_last.3 = f32[128,32,128]{2,1,0:T(8,128)} custom-call(f32[32,128,256]{2,1,0:T(8,128)} %adjoint_ref.2, bf16[64,768]{1,0:T(8,128)(2,1)} %constant.170.clone.table_ref), custom_call_target="tpu_custom_call" | custom-call | flops 402653184 | bytes 6291456 | tf_op jit(solution)/shard_map/forward_last/pallas_call | solution.py:108
  47.7 0.3 reduce-precision_convert_fusion.5
  48.1 0.6 reduce-precision_convert_fusion.3
  48.7 0.7 pad_maximum_fusion.7.refs_18_
  49.4 0.3 reduce-precision_convert_fusion.4
  49.7 3.6 %reduce-precision_convert_fusion = (bf16[256,256]{1,0:T(8,128)(2,1)S(1)}, bf16[256,256]{1,0:T(8,128)(2,1)S(1)}, bf16[256,256]{1,0:T(8,128)(2,1)S(1)}, bf16[256,2...) fusion(s32[256]{0:T(256)S(1)} %and_select_fusion.1, s32[256]{0:T(256)S(1)} %pad_add_fusion), kind=kLoop, calls=%fused_computation.21 | loop fusion | flops 3735552 | bytes 788480 | tf_op jit(solution)/shard_map/convert.7
  53.4 0.8 pad_maximum_fusion.6.refs_19_
  54.1 0.8 pad_maximum_fusion.4.refs_17_
  54.9 0.8 pad_maximum_fusion.5.refs_19_
  55.8 0.6 collective-permute-done.1.refs_1_.refs_5_.refs_9_.refs_13_
  56.3 41.5 %collective-permute-done.2.refs_2_.refs_6_.refs_10_.refs_14_ = f32[13,72,128]{2,1,0:T(8,128)S(1)} collective-permute-done((f32[13,72,128]{2,1,0:T(8,128)S(1)}, f32[13,72,128]{2,1,0:T(8,128)S(1)}, u32[]{:S(2)}, u32[]{:S(2)}) %collective-permute-start.2) | collective-permute-done | bytes 479264 | tf_op jit(solution)/shard_map/ppermute | solution.py:403
  97.9 15.3 %collective-permute-done.3.refs_3_.refs_7_.refs_11_.refs_15_ = f32[13,72,128]{2,1,0:T(8,128)S(1)} collective-permute-done((f32[13,72,128]{2,1,0:T(8,128)S(1)}, f32[13,72,128]{2,1,0:T(8,128)S(1)}, u32[]{:S(2)}, u32[]{:S(2)}) %collective-permute-start.3) | collective-permute-done | bytes 479264 | tf_op jit(solution)/shard_map/ppermute | solution.py:403
  113.2 1.3 all-to-all-done.1
  114.5 5.0 %all-to-all-start = ((f32[16,8,32,128]{3,2,1,0:T(8,128)}), f32[16,8,32,128]{3,2,1,0:T(8,128)}, u32[]{:S(2)}, u32[]{:S(2)}) async-start(f32[16,8,32,128]{3,2,1,0:T(8,128)} %bitcast.16), calls=%async_computation | async-start | bytes 4194304 | tf_op jit(solution)/shard_map/all_to_all | solution.py:634
  119.6 0.6 fusion.54
  120.2 8.0 %filter_planes.5 = (f32[2,2,8,32,128]{4,3,2,1,0:T(8,128)}, f32[2,2,8,32,128]{4,3,2,1,0:T(8,128)}, f32[2,2,8,32,128]{4,3,2,1,0:T(8,128)}, f32[2,2,8,32,128]{4,3,2,1,0:T(8,128)}) custom-call(s32[8]{0:T(128)} %get-tuple-element.147.places_ref, s32[1]{0:T(128)} %bitcast.5.special_ref, f32[8,2,16,32,128]{4,3,2,1,0:T(8,128)} %bitcast.7.planes_ref, ...), custom_call_target="tpu_custom_call" | custom-call | flops 3221225472 | bytes 5242880 | tf_op jit(solution)/shard_map/filter_planes/pallas_call | solution.py:224
  128.3 1.2 collective-permute-start.4
  129.5 1.2 collective-permute-start.5
  130.7 0.3 collective-permute-start.6
  131.0 9.8 %filter_planes.4 = f32[8,2,2,8,32,128]{5,4,3,2,1,0:T(8,128)} custom-call(s32[8]{0:T(128)} %get-tuple-element.148.places_ref, s32[1]{0:T(128)} %bitcast.5.special_ref, f32[8,2,16,32,128]{4,3,2,1,0:T(8,128)} %bitcast.7.planes_ref, f32[13,72,128]{2,1,0:T(8,128)} %copy-done, f32[13,72,128]{2,1,0:T(8,128)} %copy-done.2, f32[13,72,128]{2,1,0:T(8,128)} %copy-done.3, ...), custom_call_target="tpu_custom_call" | custom-call | flops 4831838208 | bytes 7340032 | tf_op jit(solution)/shard_map/filter_planes/pallas_call | solution.py:224
  140.8 7.6 %collective-permute-done.4 = f32[2,2,8,32,128]{4,3,2,1,0:T(8,128)S(1)} collective-permute-done((f32[2,2,8,32,128]{4,3,2,1,0:T(8,128)}, f32[2,2,8,32,128]{4,3,2,1,0:T(8,128)S(1)}, u32[]{:S(2)}, u32[]{:S(2)}) %collective-permute-start.4) | collective-permute-done | bytes 524320 | tf_op jit(solution)/shard_map/ppermute | solution.py:698
  148.4 18.6 %collective-permute-done.5 = f32[2,2,8,32,128]{4,3,2,1,0:T(8,128)S(1)} collective-permute-done((f32[2,2,8,32,128]{4,3,2,1,0:T(8,128)}, f32[2,2,8,32,128]{4,3,2,1,0:T(8,128)S(1)}, u32[]{:S(2)}, u32[]{:S(2)}) %collective-permute-start.5) | collective-permute-done | bytes 524320 | tf_op jit(solution)/shard_map/ppermute | solution.py:698
  166.9 12.2 %collective-permute-done.6 = f32[2,2,8,32,128]{4,3,2,1,0:T(8,128)S(1)} collective-permute-done((f32[2,2,8,32,128]{4,3,2,1,0:T(8,128)}, f32[2,2,8,32,128]{4,3,2,1,0:T(8,128)S(1)}, u32[]{:S(2)}, u32[]{:S(2)}) %collective-permute-start.6) | collective-permute-done | bytes 524320 | tf_op jit(solution)/shard_map/ppermute | solution.py:698
  179.2 5.1 %all-to-all-start.2 = ((f32[16,2,8,32,128]{4,3,2,1,0:T(8,128)}), f32[16,2,8,32,128]{4,3,2,1,0:T(8,128)}, u32[]{:S(2)}, u32[]{:S(2)}) async-start(f32[16,2,8,32,128]{4,3,2,1,0:T(8,128)} %bitcast.17), calls=%async_computation.2 | async-start | bytes 8388608 | tf_op jit(solution)/shard_map/all_to_all | solution.py:634
  184.3 8.2 %filter_planes.3 = (f32[2,2,8,32,128]{4,3,2,1,0:T(8,128)}, f32[2,2,8,32,128]{4,3,2,1,0:T(8,128)}, f32[2,2,8,32,128]{4,3,2,1,0:T(8,128)}, f32[2,2,8,32,128]{4,3,2,1,0:T(8,128)}) custom-call(s32[8]{0:T(128)} %get-tuple-element.149.places_ref, s32[1]{0:T(128)} %bitcast.5.special_ref, f32[8,2,8,32,128]{4,3,2,1,0:T(8,128)} %bitcast.6.planes_ref, ...), custom_call_target="tpu_custom_call" | custom-call | flops 3221225472 | bytes 5242880 | tf_op jit(solution)/shard_map/filter_planes/pallas_call | solution.py:224
  192.8 0.4 collective-permute-start.10
  193.2 0.3 copy-done.12
  193.5 1.2 collective-permute-start.7
  194.7 1.2 collective-permute-start.8
  195.9 0.2 collective-permute-start.9
  196.3 6.7 %backward_last.2.refs_6_ = f32[32,128,256]{2,1,0:T(8,128)} custom-call(f32[2,32,128,256]{3,2,1,0:T(8,128)} %cosine_factors.1.refs_0_, bf16[192,256]{1,0:T(8,128)(2,1)S(1)} %pad_maximum_fusion.8.refs_1_, f32[4,2,8,32,128]{4,3,2,1,0:T(8,128)S(1)} %pad_maximum_fusion.refs_2_, f32[4,2,8,32,128]{4,3,2,1,0:T(8,128)S(1)} %collective-permute-done.10.refs_3_), custom_call_target="tpu_custom_call" | custom-call | flops 805306368 | bytes 18874368 | tf_op jit(solution)/shard_map/backward_last/pallas_call | solution.py:336
  202.9 21.0 %collective-permute-done.7 = f32[2,2,8,32,128]{4,3,2,1,0:T(8,128)S(1)} collective-permute-done((f32[2,2,8,32,128]{4,3,2,1,0:T(8,128)S(1)}, f32[2,2,8,32,128]{4,3,2,1,0:T(8,128)S(1)}, u32[]{:S(2)}, u32[]{:S(2)}) %collective-permute-start.7) | collective-permute-done | bytes 524320 | tf_op jit(solution)/shard_map/ppermute | solution.py:698
  223.9 41.5 %collective-permute-done.8 = f32[2,2,8,32,128]{4,3,2,1,0:T(8,128)S(1)} collective-permute-done((f32[2,2,8,32,128]{4,3,2,1,0:T(8,128)S(1)}, f32[2,2,8,32,128]{4,3,2,1,0:T(8,128)S(1)}, u32[]{:S(2)}, u32[]{:S(2)}) %collective-permute-start.8) | collective-permute-done | bytes 524320 | tf_op jit(solution)/shard_map/ppermute | solution.py:698
  265.4 17.5 %collective-permute-done.9 = f32[2,2,8,32,128]{4,3,2,1,0:T(8,128)S(1)} collective-permute-done((f32[2,2,8,32,128]{4,3,2,1,0:T(8,128)S(1)}, f32[2,2,8,32,128]{4,3,2,1,0:T(8,128)S(1)}, u32[]{:S(2)}, u32[]{:S(2)}) %collective-permute-start.9) | collective-permute-done | bytes 524320 | tf_op jit(solution)/shard_map/ppermute | solution.py:698
  283.1 0.1 pad_maximum_fusion.3
  283.2 1.2 collective-permute-start.11
  284.4 0.1 pad_maximum_fusion.2.refs_3_
  284.5 2.2 collective-permute-done.11.refs_4_
  286.7 9.7 %backward_last.3 = f32[32,128,256]{2,1,0:T(8,128)} custom-call(f32[2,32,128,256]{3,2,1,0:T(8,128)} %cosine_factors.1.refs_0_, bf16[192,256]{1,0:T(8,128)(2,1)S(1)} %pad_maximum_fusion.9.refs_1_, bf16[384,256]{1,0:T(8,128)(2,1)S(1)} %copy-done.1, f32[4,2,8,32,128]{4,3,2,1,0:T(8,128)S(1)} %pad_maximum_fusion.2.refs_3_, ...), custom_call_target="tpu_custom_call" | custom-call | flops 2415919104 | bytes 23068672 | tf_op jit(solution)/shard_map/backward_last/pallas_call | solution.py:336
  (53 shorter events, 0.7 us)
Async XLA Ops:
  1.4 10.3 %collective-permute-start = (f32[2,129,256]{2,1,0:T(8,128)S(1)}, f32[2,129,256]{2,1,0:T(8,128)S(1)}, u32[]{:S(2)}, u32[]{:S(2)}) collective-permute-start(f32[2,129,256]{2,1,0:T(8,128)S(1)} %fusion.18), channel_id=1, source_target_pairs={{0,8},{8,0},{1,9},{9,1},{16,24},{24,16},{17,25},{25,17}} | collective-permute-start | bytes 792584 | tf_op jit(solution)/shard_map/ppermute | solution.py:607
  11.8 6.0 %copy-start.13 = (s32[8]{0:T(128)S(1)}, s32[8]{0:T(128)}, u32[]{:S(2)}) copy-start(s32[8]{0:T(128)} %param.18) | copy-start | bytes 100
  11.8 6.0 %copy-start.14 = (s32[2]{0:T(128)S(1)}, s32[2]{0:T(128)}, u32[]{:S(2)}) copy-start(s32[2]{0:T(128)} %param.19) | copy-start | bytes 28
  11.8 102.8 %all-to-all-start.1 = ((f32[16,16,32,128]{3,2,1,0:T(8,128)}), f32[16,16,32,128]{3,2,1,0:T(8,128)}, u32[]{:S(2)}, u32[]{:S(2)}) async-start(f32[16,16,32,128]{3,2,1,0:T(8,128)} %bitcast.15), calls=%async_computation.1 | async-start | bytes 8388608 | tf_op jit(solution)/shard_map/all_to_all | solution.py:634
  20.1 9.3 %copy-start.8 = (s32[8,8]{1,0:T(8,128)S(1)}, s32[8,8]{1,0:T(8,128)}, u32[]{:S(2)}) copy-start(s32[8,8]{1,0:T(8,128)} %constant.168.clone) | copy-start | bytes 772
  20.1 9.9 %copy-start.7 = (s32[8,8]{1,0:T(8,128)S(1)}, s32[8,8]{1,0:T(8,128)}, u32[]{:S(2)}) copy-start(s32[8,8]{1,0:T(8,128)} %constant.167.clone) | copy-start | bytes 772
  28.3 0.8 copy-start
  30.7 25.6 %collective-permute-start.1 = (f32[13,72,128]{2,1,0:T(8,128)S(1)}, f32[13,72,128]{2,1,0:T(8,128)S(1)}, u32[]{:S(2)}, u32[]{:S(2)}) collective-permute-start(f32[13,72,128]{2,1,0:T(8,128)S(1)} %get-tuple-element.73), channel_id=1, source_target_pairs={{0,2},{2,0},{4,6},{6,4},{8,10},{10,8},{12,14},{14,12},{1,3},{3,1},... | collective-permute-start | bytes 1437704 | tf_op jit(solution)/shard_map/ppermute | solution.py:403
  31.9 66.0 %collective-permute-start.2 = (f32[13,72,128]{2,1,0:T(8,128)S(1)}, f32[13,72,128]{2,1,0:T(8,128)S(1)}, u32[]{:S(2)}, u32[]{:S(2)}) collective-permute-start(f32[13,72,128]{2,1,0:T(8,128)S(1)} %get-tuple-element.74), channel_id=1, source_target_pairs={{0,4},{2,6},{4,0},{6,2},{8,12},{10,14},{12,8},{14,10},{1,5},{3,7},... | collective-permute-start | bytes 1437704 | tf_op jit(solution)/shard_map/ppermute | solution.py:403
  33.1 80.1 %collective-permute-start.3 = (f32[13,72,128]{2,1,0:T(8,128)S(1)}, f32[13,72,128]{2,1,0:T(8,128)S(1)}, u32[]{:S(2)}, u32[]{:S(2)}) collective-permute-start(f32[13,72,128]{2,1,0:T(8,128)S(1)} %get-tuple-element.75), channel_id=1, source_target_pairs={{0,6},{2,4},{4,2},{6,0},{8,14},{10,12},{12,10},{14,8},{1,7},{3,5},... | collective-permute-start | bytes 1437704 | tf_op jit(solution)/shard_map/ppermute | solution.py:403
  42.4 5.6 %copy-start.9 = (s32[256]{0:T(256)S(1)}, s32[256]{0:T(256)}, u32[]{:S(2)}) copy-start(s32[256]{0:T(256)} %constant.166.clone) | copy-start | bytes 3076
  56.3 63.9 %copy-start.2 = (f32[13,72,128]{2,1,0:T(8,128)}, f32[13,72,128]{2,1,0:T(8,128)S(1)}, u32[]{:S(2)}) copy-start(f32[13,72,128]{2,1,0:T(8,128)S(1)} %collective-permute-done.1.refs_1_.refs_5_.refs_9_.refs_13_) | copy-start | bytes 1437700
  97.9 22.3 %copy-start.3 = (f32[13,72,128]{2,1,0:T(8,128)}, f32[13,72,128]{2,1,0:T(8,128)S(1)}, u32[]{:S(2)}) copy-start(f32[13,72,128]{2,1,0:T(8,128)S(1)} %collective-permute-done.2.refs_2_.refs_6_.refs_10_.refs_14_) | copy-start | bytes 1437700
  113.2 7.0 %copy-start.4 = (f32[13,72,128]{2,1,0:T(8,128)}, f32[13,72,128]{2,1,0:T(8,128)S(1)}, u32[]{:S(2)}) copy-start(f32[13,72,128]{2,1,0:T(8,128)S(1)} %collective-permute-done.3.refs_3_.refs_7_.refs_11_.refs_15_) | copy-start | bytes 1437700
  114.5 64.7 %all-to-all-start = ((f32[16,8,32,128]{3,2,1,0:T(8,128)}), f32[16,8,32,128]{3,2,1,0:T(8,128)}, u32[]{:S(2)}, u32[]{:S(2)}) async-start(f32[16,8,32,128]{3,2,1,0:T(8,128)} %bitcast.16), calls=%async_computation | async-start | bytes 4194304 | tf_op jit(solution)/shard_map/all_to_all | solution.py:634
  128.3 20.1 %collective-permute-start.4 = (f32[2,2,8,32,128]{4,3,2,1,0:T(8,128)}, f32[2,2,8,32,128]{4,3,2,1,0:T(8,128)S(1)}, u32[]{:S(2)}, u32[]{:S(2)}) collective-permute-start(f32[2,2,8,32,128]{4,3,2,1,0:T(8,128)} %get-tuple-element.101), channel_id=1, source_target_pairs={{0,2},{2,0},{4,6},{6,4},{8,10},{10,8},{12,14},{14,12},{1,3},{3,1},... | collective-permute-start | bytes 1572872 | tf_op jit(solution)/shard_map/ppermute | solution.py:698
  129.5 37.4 %collective-permute-start.5 = (f32[2,2,8,32,128]{4,3,2,1,0:T(8,128)}, f32[2,2,8,32,128]{4,3,2,1,0:T(8,128)S(1)}, u32[]{:S(2)}, u32[]{:S(2)}) collective-permute-start(f32[2,2,8,32,128]{4,3,2,1,0:T(8,128)} %get-tuple-element.102), channel_id=1, source_target_pairs={{0,4},{2,6},{4,0},{6,2},{8,12},{10,14},{12,8},{14,10},{1,5},{3,7},... | collective-permute-start | bytes 1572872 | tf_op jit(solution)/shard_map/ppermute | solution.py:698
  130.7 48.5 %collective-permute-start.6 = (f32[2,2,8,32,128]{4,3,2,1,0:T(8,128)}, f32[2,2,8,32,128]{4,3,2,1,0:T(8,128)S(1)}, u32[]{:S(2)}, u32[]{:S(2)}) collective-permute-start(f32[2,2,8,32,128]{4,3,2,1,0:T(8,128)} %get-tuple-element.103), channel_id=1, source_target_pairs={{0,6},{2,4},{4,2},{6,0},{8,14},{10,12},{12,10},{14,8},{1,7},{3,5},... | collective-permute-start | bytes 1572872 | tf_op jit(solution)/shard_map/ppermute | solution.py:698
  179.2 107.5 %all-to-all-start.2 = ((f32[16,2,8,32,128]{4,3,2,1,0:T(8,128)}), f32[16,2,8,32,128]{4,3,2,1,0:T(8,128)}, u32[]{:S(2)}, u32[]{:S(2)}) async-start(f32[16,2,8,32,128]{4,3,2,1,0:T(8,128)} %bitcast.17), calls=%async_computation.2 | async-start | bytes 8388608 | tf_op jit(solution)/shard_map/all_to_all | solution.py:634
  184.3 8.2 %copy-start.6 = (f32[2,2,8,32,128]{4,3,2,1,0:T(8,128)S(1)}, f32[2,2,8,32,128]{4,3,2,1,0:T(8,128)}, u32[]{:S(2)}) copy-start(f32[2,2,8,32,128]{4,3,2,1,0:T(8,128)} %get-tuple-element.113) | copy-start | bytes 1572868
  192.5 1.0 copy-start.12
  192.5 2.2 copy-start.11
  192.5 3.4 %copy-start.10 = (f32[2,2,8,32,128]{4,3,2,1,0:T(8,128)S(1)}, f32[2,2,8,32,128]{4,3,2,1,0:T(8,128)}, u32[]{:S(2)}) copy-start(f32[2,2,8,32,128]{4,3,2,1,0:T(8,128)} %get-tuple-element.111) | copy-start | bytes 1572868
  192.8 3.5 %collective-permute-start.10 = (f32[4,2,8,32,128]{4,3,2,1,0:T(8,128)S(1)}, f32[4,2,8,32,128]{4,3,2,1,0:T(8,128)S(1)}, u32[]{:S(2)}, u32[]{:S(2)}) collective-permute-start(f32[4,2,8,32,128]{4,3,2,1,0:T(8,128)S(1)} %pad_maximum_fusion.1), channel_id=1, source_target_pairs={{0,1},{1,0},{2,3},{3,2},{4,5},{5,4},{6,7},{7,6},{8,9},{9,8},{10,11... | collective-permute-start | bytes 3145736 | tf_op jit(solution)/shard_map/ppermute | solution.py:707
  193.5 30.4 %collective-permute-start.7 = (f32[2,2,8,32,128]{4,3,2,1,0:T(8,128)S(1)}, f32[2,2,8,32,128]{4,3,2,1,0:T(8,128)S(1)}, u32[]{:S(2)}, u32[]{:S(2)}) collective-permute-start(f32[2,2,8,32,128]{4,3,2,1,0:T(8,128)S(1)} %copy-done.12), channel_id=1, source_target_pairs={{0,2},{2,0},{4,6},{6,4},{8,10},{10,8},{12,14},{14,12},{1,3},{3,1},... | collective-permute-start | bytes 1572872 | tf_op jit(solution)/shard_map/ppermute | solution.py:698
  194.7 70.7 %collective-permute-start.8 = (f32[2,2,8,32,128]{4,3,2,1,0:T(8,128)S(1)}, f32[2,2,8,32,128]{4,3,2,1,0:T(8,128)S(1)}, u32[]{:S(2)}, u32[]{:S(2)}) collective-permute-start(f32[2,2,8,32,128]{4,3,2,1,0:T(8,128)S(1)} %copy-done.11), channel_id=1, source_target_pairs={{0,4},{2,6},{4,0},{6,2},{8,12},{10,14},{12,8},{14,10},{1,5},{3,7},... | collective-permute-start | bytes 1572872 | tf_op jit(solution)/shard_map/ppermute | solution.py:698
  195.9 87.0 %collective-permute-start.9 = (f32[2,2,8,32,128]{4,3,2,1,0:T(8,128)S(1)}, f32[2,2,8,32,128]{4,3,2,1,0:T(8,128)S(1)}, u32[]{:S(2)}, u32[]{:S(2)}) collective-permute-start(f32[2,2,8,32,128]{4,3,2,1,0:T(8,128)S(1)} %copy-done.10), channel_id=1, source_target_pairs={{0,6},{2,4},{4,2},{6,0},{8,14},{10,12},{12,10},{14,8},{1,7},{3,5},... | collective-permute-start | bytes 1572872 | tf_op jit(solution)/shard_map/ppermute | solution.py:698
  196.3 86.7 %copy-start.5 = (f32[2,2,8,32,128]{4,3,2,1,0:T(8,128)S(1)}, f32[2,2,8,32,128]{4,3,2,1,0:T(8,128)}, u32[]{:S(2)}) copy-start(f32[2,2,8,32,128]{4,3,2,1,0:T(8,128)} %get-tuple-element.117) | copy-start | bytes 1572868
  202.9 83.8 %copy-start.1 = (bf16[384,256]{1,0:T(8,128)(2,1)S(1)}, bf16[384,256]{1,0:T(8,128)(2,1)}, u32[]{:S(2)}) copy-start(bf16[384,256]{1,0:T(8,128)(2,1)} %constant.169.clone.refs_2_) | copy-start | bytes 589828
  283.2 3.5 %collective-permute-start.11 = (f32[4,2,8,32,128]{4,3,2,1,0:T(8,128)S(1)}, f32[4,2,8,32,128]{4,3,2,1,0:T(8,128)S(1)}, u32[]{:S(2)}, u32[]{:S(2)}) collective-permute-start(f32[4,2,8,32,128]{4,3,2,1,0:T(8,128)S(1)} %pad_maximum_fusion.3), channel_id=1, source_target_pairs={{0,1},{1,0},{2,3},{3,2},{4,5},{5,4},{6,7},{7,6},{8,9},{9,8},{10,11... | collective-permute-start | bytes 3145736 | tf_op jit(solution)/shard_map/ppermute | solution.py:707
